TPU v7x, 32 devices: a whole 2x2x4 slice. The times are simulated.
32 devices in a mesh: tm: 8 (over y, x, core), pen: 4 (over z).
Axes of the slice: x: 2, y: 2, z: 4, core: 2. Of those that a mesh axis runs over, the one named last changes fastest.
Arguments:
- clips: bfloat16 [4, 16384, 256], P('pen', 'tm'), may hold values from -6 to 6
- targets: bfloat16 [4, 16384, 1024], P('pen', 'tm'), may hold values from -6 to 6
- conv_weight: bfloat16 [3, 3, 256, 256], replicated, may hold values from -0.21875 to 0.21875
- head_weight: bfloat16 [256, 1024], replicated, may hold values from -0.375 to 0.375
Outputs:
- conv_grad: float32 [3, 3, 256, 256], P(None, None, 'pen')
- head_grad: float32 [256, 1024], P('pen')
All inputs are finite; a program needn't handle non-finite values.
Results may differ from a plain program's by a relative error of at most 0.00031.
Values may be sent and summed in bfloat16 or wider, within the bound.
No kernel may reach another device: no remote copies, remote signals or barrier semaphores. Data moves between devices by JAX's collectives and lax.ppermute only.
A program may use at most 128 MiB of HBM per device.

v0:
```python
import jax
import jax.numpy as jnp
from jax import lax
from jax.sharding import PartitionSpec as P

FEAT = 1024
D1 = 16
D2 = 64
D3 = 256


def padded_2(block, sides, width):
    for axis, dim in sides:
        count = lax.axis_size(axis)
        forward = [(i, i + 1) for i in range(count - 1)]
        backward = [(target, source) for source, target in forward]
        low = lax.ppermute(
            lax.slice_in_dim(block, block.shape[dim] - width, None, axis=dim), axis, forward
        )
        high = lax.ppermute(lax.slice_in_dim(block, 0, width, axis=dim), axis, backward)
        block = jnp.concatenate([low, block, high], axis=dim)
    return block


def trans_dot(left, right):
    return lax.dot_general(
        left.astype(jnp.float32),
        right,
        (((0,), (0,)), ((), ())),
        precision=lax.Precision.HIGHEST,
        preferred_element_type=jnp.float32,
    )


def full_dot(left, right):
    return jnp.dot(
        left,
        right.astype(jnp.float32),
        precision=lax.Precision.HIGHEST,
        preferred_element_type=jnp.float32,
    )


def three_taps(source, weights, width, length):
    total = jnp.dot(source[0:length], weights[0], preferred_element_type=jnp.float32)
    total = total + jnp.dot(
        source[width : width + length], weights[1], preferred_element_type=jnp.float32
    )
    return total + jnp.dot(
        source[2 * width : 2 * width + length], weights[2], preferred_element_type=jnp.float32
    )


def on_device(clips, targets, conv_weight, head_weight):
    clip = clips[0]
    target = targets[0]
    count = clip.shape[0]
    dilations = (D1, D2, D3)
    saved = []
    hidden = clip
    for layer in range(3):
        width = dilations[layer]
        padded = padded_2(hidden, (("tm", 0),), width)
        pre = three_taps(padded, conv_weight[layer], width, count)
        saved.append((padded, pre))
        hidden = (hidden.astype(jnp.float32) + jax.nn.silu(pre)).astype(jnp.bfloat16)
    pred = jnp.dot(hidden, head_weight, preferred_element_type=jnp.float32)
    grad_pred = (pred - target.astype(jnp.float32)) * (2.0 / FEAT)
    head_local = trans_dot(hidden, grad_pred)
    error = full_dot(grad_pred, head_weight.T)
    layer_grads = [None, None, None]
    for layer in (2, 1, 0):
        width = dilations[layer]
        padded, pre = saved[layer]
        sig = jax.nn.sigmoid(pre)
        back = error * sig * (1.0 + pre * (1.0 - sig))
        taps = [trans_dot(padded[k * width : k * width + count], back) for k in range(3)]
        layer_grads[layer] = jnp.stack(taps)
        if layer > 0:
            back_pad = padded_2(back, (("tm", 0),), width)
            for k in range(3):
                start = (2 - k) * width
                error = error + full_dot(back_pad[start : start + count], conv_weight[layer, k].T)
    conv_local = jnp.stack(layer_grads)
    summed = lax.psum((conv_local, head_local), "tm")
    conv_part, head_part = (
        lax.psum_scatter(summed[0], "pen", scatter_dimension=2, tiled=True),
        lax.psum_scatter(summed[1], "pen", scatter_dimension=0, tiled=True),
    )
    return (conv_part, head_part)


def solution(mesh):
    in_specs = (P("pen", "tm", None), P("pen", "tm", None), P(), P())
    out_specs = (P(None, None, "pen", None), P("pen", None))
    return jax.shard_map(
        on_device, mesh=mesh, in_specs=in_specs, out_specs=out_specs, check_vma=False
    )
```

profile of v0, /device:TPU:0, one launch (start us, length us, event | category | flops | bytes accessed | tf_op | source)
XLA Modules:
  0.0 226.3 jit_solution(4922601358827034262)
XLA Ops:
  7.2 0.9 slice_bitcast_fusion.1
  8.1 1.3 collective-permute-start.1
  9.4 3.0 %collective-permute-start = (bf16[16,256]{1,0:T(8,128)(2,1)S(1)}, bf16[16,256]{1,0:T(8,128)(2,1)S(1)}, u32[]{:S(2)}, u32[]{:S(2)}) collective-permute-start(bf16[16,256]{1,0:T(8,128)(2,1)S(1)} %get-tuple-element.12), channel_id=1, source_target_pairs={{0,4},{4,8},{8,12},{12,16},{16,20},{20,24},{24,28},{1,5},{5,9},{9,... | collective-permute-start | bytes 24584 | tf_op jit(solution)/shard_map/ppermute | solution.py:17
  12.4 1.7 fusion.38
  14.1 0.4 fusion.19
  14.6 2.3 %add_convert_fusion.2 = (bf16[2048,256]{1,0:T(8,128)(2,1)S(1)}, f32[2048,256]{1,0:T(8,128)}) fusion(bf16[1,2048,256]{2,1,0:T(8,128)(2,1)S(1)} %copy-done.6, f32[2048,256]{1,0:T(8,128)S(1)} %fusion.19, f32[2048,256]{1,0:T(8,128)S(1)} %fusion.38, bf16[3,3,256,256]{3,2,1,0:T(8,128)(2,1)S(1)} %copy-done.10, bf16[2048,256]{1,0:T(8,128)(2,1)S(1)} %bitcast.111, ...), kind=kOutput, calls=%fused_computation.37 | convolution fusion | flops 275251200 | bytes 9576448 | tf_op jit(solution)/shard_map/dot_general | solution.py:45
  16.9 1.3 collective-permute-start.3
  18.2 0.4 fusion.33
  18.6 5.1 %collective-permute-start.2 = (bf16[64,256]{1,0:T(8,128)(2,1)S(1)}, bf16[64,256]{1,0:T(8,128)(2,1)S(1)}, u32[]{:S(2)}, u32[]{:S(2)}) collective-permute-start(bf16[64,256]{1,0:T(8,128)(2,1)S(1)} %get-tuple-element.10), channel_id=1, source_target_pairs={{0,4},{4,8},{8,12},{12,16},{16,20},{20,24},{24,28},{1,5},{5,9},{9,... | collective-permute-start | bytes 98312 | tf_op jit(solution)/shard_map/ppermute | solution.py:17
  23.7 0.4 fusion.20
  24.1 0.4 collective-permute-done.2
  24.5 2.2 add_convert_fusion.1
  26.8 1.3 collective-permute-start.5
  28.1 0.4 fusion.25
  28.5 4.6 %collective-permute-start.4 = (bf16[256,256]{1,0:T(8,128)(2,1)S(1)}, bf16[256,256]{1,0:T(8,128)(2,1)S(1)}, u32[]{:S(2)}, u32[]{:S(2)}) collective-permute-start(bf16[256,256]{1,0:T(8,128)(2,1)S(1)} %get-tuple-element.8), channel_id=1, source_target_pairs={{0,4},{4,8},{8,12},{12,16},{16,20},{20,24},{24,28},{1,5},{5,9},{9,... | collective-permute-start | bytes 393224 | tf_op jit(solution)/shard_map/ppermute | solution.py:17
  33.2 0.4 fusion.21
  33.6 0.3 collective-permute-done.4
  33.9 0.5 fusion.12
  34.5 4.9 %fusion.76 = f32[2048,1024]{1,0:T(8,128)} fusion(bf16[256,1024]{1,0:T(8,128)(2,1)S(1)} %copy-done, f32[2048,256]{1,0:T(8,128)S(1)} %fusion.12, bf16[2048,256]{1,0:T(8,128)(2,1)S(1)} %get-tuple-element.16), kind=kOutput, calls=%fused_computation.116 | convolution fusion | flops 1077411840 | bytes 12058624 | tf_op jit(solution)/shard_map/dot_general | solution.py:67
  39.4 9.8 %fusion.1 = f32[256,1024]{1,0:T(8,128)} fusion(f32[2048,1024]{1,0:T(8,128)} %fusion.76, bf16[1,2048,1024]{2,1,0:T(8,128)(2,1)S(1)} %copy-done.12, f32[2048,256]{1,0:T(8,128)S(1)} %fusion.12, bf16[2048,256]{1,0:T(8,128)(2,1)S(1)} %get-tuple-element.16), kind=kOutput, calls=%fused_computation.2 | convolution fusion | flops 6452412416 | bytes 16777216 | tf_op jit(solution)/shard_map/dot_general | solution.py:26
  49.2 11.9 %add_multiply_fusion.1 = (f32[2048,256]{1,0:T(8,128)S(1)}, f32[2048,256]{1,0:T(8,128)}) fusion(f32[2048,256]{1,0:T(8,128)} %copy-done.9, bf16[256,1024]{1,0:T(8,128)(2,1)S(1)} %copy-done, f32[2048,1024]{1,0:T(8,128)} %fusion.76, bf16[1,2048,1024]{2,1,0:T(8,128)(2,1)} %param.5), kind=kOutput, calls=%fused_computation.32 | convolution fusion | flops 6452936704 | bytes 19398656 | tf_op jit(solution)/shard_map/dot_general | solution.py:36
  61.1 0.7 fusion.78
  61.9 1.5 convolution_bitcast_fusion.1
  63.4 1.3 collective-permute-start.6
  64.7 5.8 %collective-permute-start.7 = (f32[256,256]{1,0:T(8,128)S(1)}, f32[256,256]{1,0:T(8,128)S(1)}, u32[]{:S(2)}, u32[]{:S(2)}) collective-permute-start(f32[256,256]{1,0:T(8,128)S(1)} %get-tuple-element.6), channel_id=1, source_target_pairs={{0,4},{4,8},{8,12},{12,16},{16,20},{20,24},{24,28},{1,5},{5,9},{9,... | collective-permute-start | bytes 786440 | tf_op jit(solution)/shard_map/ppermute | solution.py:17
  70.5 2.7 %convolution_bitcast_fusion.2 = f32[1,256,256]{2,1,0:T(8,128)S(1)} fusion(f32[2048,256]{1,0:T(8,128)S(1)} %get-tuple-element.18, bf16[2048,256]{1,0:T(8,128)(2,1)} %copy-done.2, bf16[256,256]{1,0:T(8,128)(2,1)S(1)} %collective-permute-done.4), kind=kOutput, calls=%fused_computation.41 | convolution fusion | flops 1612709888 | bytes 3538944 | tf_op jit(solution)/shard_map/dot_general | solution.py:26
  73.2 2.8 %convolution_bitcast_fusion = f32[1,256,256]{2,1,0:T(8,128)S(1)} fusion(f32[2048,256]{1,0:T(8,128)S(1)} %get-tuple-element.18, bf16[256,256]{1,0:T(8,128)(2,1)S(1)} %collective-permute-done.5, bf16[2048,256]{1,0:T(8,128)(2,1)} %copy-done.2), kind=kOutput, calls=%fused_computation.39 | convolution fusion | flops 1612709888 | bytes 3538944 | tf_op jit(solution)/shard_map/dot_general | solution.py:26
  76.2 1.2 convolution_add_fusion.4
  77.3 1.2 convolution_add_fusion.3
  78.5 0.4 copy-done.13
  78.9 1.6 add_multiply_fusion
  80.6 1.1 fusion.31
  81.8 1.5 convolution_bitcast_fusion.4
  83.3 1.3 collective-permute-start.8
  84.6 5.2 %collective-permute-start.9 = (f32[64,256]{1,0:T(8,128)S(1)}, f32[64,256]{1,0:T(8,128)S(1)}, u32[]{:S(2)}, u32[]{:S(2)}) collective-permute-start(f32[64,256]{1,0:T(8,128)S(1)} %get-tuple-element.4), channel_id=1, source_target_pairs={{0,4},{4,8},{8,12},{12,16},{16,20},{20,24},{24,28},{1,5},{5,9},{9,... | collective-permute-start | bytes 196616 | tf_op jit(solution)/shard_map/ppermute | solution.py:17
  89.8 1.5 convolution_bitcast_fusion.5
  91.3 1.5 convolution_bitcast_fusion.3
  92.9 1.2 fusion.10
  94.1 0.4 copy-done.14
  94.5 1.7 fusion.11
  96.2 1.5 convolution_bitcast_fusion.8
  97.7 1.5 convolution_bitcast_fusion.6
  99.2 1.5 convolution_bitcast_fusion.7
  100.7 1.6 pad_maximum_fusion
  102.4 54.3 %reduce-scatter.3.cloned.1.call-done = f32[3,3,64,256]{3,2,1,0:T(8,128)} async-done(((f32[3,3,256,256]{3,2,1,0:T(8,128)}), f32[3,3,64,256]{3,2,1,0:T(8,128)}) %reduce-scatter.3.cloned.1.call-update) | async-done | bytes 589840 | tf_op jit(solution)/shard_map/reduce_scatter | solution.py:87
  156.7 59.0 %all-reduce.3.cloned.1.call-done = (f32[3,3,64,256]{3,2,1,0:T(8,128)}, f32[64,1024]{1,0:T(8,128)}) async-done(((f32[3,3,64,256]{3,2,1,0:T(8,128)}, f32[64,1024]{1,0:T(8,128)}), (f32[3,3,64,256]{3,2,1,0:T(8,128)}, f32[64,1024]{1,0:T(8,128)})) %all-reduce.3.cloned.1.call-update) | async-done | bytes 851984 | tf_op jit(solution)/shard_map/psum | solution.py:85
  215.7 1.9 copy.10
  217.6 1.7 copy.11
  (49 shorter events, 0.5 us)
Async XLA Ops:
  7.2 27.3 %copy-start = (bf16[256,1024]{1,0:T(8,128)(2,1)S(1)}, bf16[256,1024]{1,0:T(8,128)(2,1)}, u32[]{:S(2)}) copy-start(bf16[256,1024]{1,0:T(8,128)(2,1)} %param.7) | copy-start | bytes 1572868
  7.2 6.9 %copy-start.6 = (bf16[1,2048,256]{2,1,0:T(8,128)(2,1)S(1)}, bf16[1,2048,256]{2,1,0:T(8,128)(2,1)}, u32[]{:S(2)}) copy-start(bf16[1,2048,256]{2,1,0:T(8,128)(2,1)} %param.4) | copy-start | bytes 3145732
  7.2 6.9 %copy-start.10 = (bf16[3,3,256,256]{3,2,1,0:T(8,128)(2,1)S(1)}, bf16[3,3,256,256]{3,2,1,0:T(8,128)(2,1)}, u32[]{:S(2)}) copy-start(bf16[3,3,256,256]{3,2,1,0:T(8,128)(2,1)} %param.6) | copy-start | bytes 3538948
  7.2 95.2 %reduce-scatter.5.cloned.1.call-start = ((), (), s32[]{:S(2)}) async-start(), calls=%async_computation.3 | async-start | bytes 1310720 | tf_op jit(solution)/shard_map/reduce_scatter | solution.py:88
  8.1 6.0 %collective-permute-start.1 = (bf16[16,256]{1,0:T(8,128)(2,1)S(1)}, bf16[16,256]{1,0:T(8,128)(2,1)S(1)}, u32[]{:S(2)}, u32[]{:S(2)}) collective-permute-start(bf16[16,256]{1,0:T(8,128)(2,1)S(1)} %get-tuple-element.13), channel_id=1, source_target_pairs={{4,0},{8,4},{12,8},{16,12},{20,16},{24,20},{28,24},{5,1},{9,5},{13... | collective-permute-start | bytes 24584 | tf_op jit(solution)/shard_map/ppermute | solution.py:20
  9.4 5.2 %collective-permute-start = (bf16[16,256]{1,0:T(8,128)(2,1)S(1)}, bf16[16,256]{1,0:T(8,128)(2,1)S(1)}, u32[]{:S(2)}, u32[]{:S(2)}) collective-permute-start(bf16[16,256]{1,0:T(8,128)(2,1)S(1)} %get-tuple-element.12), channel_id=1, source_target_pairs={{0,4},{4,8},{8,12},{12,16},{16,20},{20,24},{24,28},{1,5},{5,9},{9,... | collective-permute-start | bytes 24584 | tf_op jit(solution)/shard_map/ppermute | solution.py:17
  16.9 7.7 %copy-start.4 = (bf16[2048,256]{1,0:T(8,128)(2,1)}, bf16[2048,256]{1,0:T(8,128)(2,1)S(1)}, u32[]{:S(2)}) copy-start(bf16[2048,256]{1,0:T(8,128)(2,1)S(1)} %get-tuple-element.14) | copy-start | bytes 3145732
  16.9 6.8 %collective-permute-start.3 = (bf16[64,256]{1,0:T(8,128)(2,1)S(1)}, bf16[64,256]{1,0:T(8,128)(2,1)S(1)}, u32[]{:S(2)}, u32[]{:S(2)}) collective-permute-start(bf16[64,256]{1,0:T(8,128)(2,1)S(1)} %get-tuple-element.11), channel_id=1, source_target_pairs={{4,0},{8,4},{12,8},{16,12},{20,16},{24,20},{28,24},{5,1},{9,5},{13... | collective-permute-start | bytes 98312 | tf_op jit(solution)/shard_map/ppermute | solution.py:20
  18.6 5.9 %collective-permute-start.2 = (bf16[64,256]{1,0:T(8,128)(2,1)S(1)}, bf16[64,256]{1,0:T(8,128)(2,1)S(1)}, u32[]{:S(2)}, u32[]{:S(2)}) collective-permute-start(bf16[64,256]{1,0:T(8,128)(2,1)S(1)} %get-tuple-element.10), channel_id=1, source_target_pairs={{0,4},{4,8},{8,12},{12,16},{16,20},{20,24},{24,28},{1,5},{5,9},{9,... | collective-permute-start | bytes 98312 | tf_op jit(solution)/shard_map/ppermute | solution.py:17
  26.8 12.6 %copy-start.2 = (bf16[2048,256]{1,0:T(8,128)(2,1)}, bf16[2048,256]{1,0:T(8,128)(2,1)S(1)}, u32[]{:S(2)}) copy-start(bf16[2048,256]{1,0:T(8,128)(2,1)S(1)} %get-tuple-element.16) | copy-start | bytes 3145732
  26.8 6.4 %collective-permute-start.5 = (bf16[256,256]{1,0:T(8,128)(2,1)S(1)}, bf16[256,256]{1,0:T(8,128)(2,1)S(1)}, u32[]{:S(2)}, u32[]{:S(2)}) collective-permute-start(bf16[256,256]{1,0:T(8,128)(2,1)S(1)} %get-tuple-element.9), channel_id=1, source_target_pairs={{4,0},{8,4},{12,8},{16,12},{20,16},{24,20},{28,24},{5,1},{9,5},{13... | collective-permute-start | bytes 393224 | tf_op jit(solution)/shard_map/ppermute | solution.py:20
  28.5 5.4 %collective-permute-start.4 = (bf16[256,256]{1,0:T(8,128)(2,1)S(1)}, bf16[256,256]{1,0:T(8,128)(2,1)S(1)}, u32[]{:S(2)}, u32[]{:S(2)}) collective-permute-start(bf16[256,256]{1,0:T(8,128)(2,1)S(1)} %get-tuple-element.8), channel_id=1, source_target_pairs={{0,4},{4,8},{8,12},{12,16},{16,20},{20,24},{24,28},{1,5},{5,9},{9,... | collective-permute-start | bytes 393224 | tf_op jit(solution)/shard_map/ppermute | solution.py:17
  34.4 4.9 %copy-start.9 = (f32[2048,256]{1,0:T(8,128)}, f32[2048,256]{1,0:T(8,128)S(1)}, u32[]{:S(2)}) copy-start(f32[2048,256]{1,0:T(8,128)S(1)} %fusion.12) | copy-start | bytes 6291460
  34.5 4.9 %copy-start.12 = (bf16[1,2048,1024]{2,1,0:T(8,128)(2,1)S(1)}, bf16[1,2048,1024]{2,1,0:T(8,128)(2,1)}, u32[]{:S(2)}) copy-start(bf16[1,2048,1024]{2,1,0:T(8,128)(2,1)} %param.5) | copy-start | bytes 12582916
  49.2 12.7 %copy-start.3 = (bf16[2048,256]{1,0:T(8,128)(2,1)S(1)}, bf16[2048,256]{1,0:T(8,128)(2,1)}, u32[]{:S(2)}) copy-start(bf16[2048,256]{1,0:T(8,128)(2,1)} %copy-done.2) | copy-start | bytes 3145732
  63.4 93.3 %reduce-scatter.3.cloned.1.call-start = ((), (), s32[]{:S(2)}) async-start(), calls=%async_computation.2 | async-start | bytes 2949120 | tf_op jit(solution)/shard_map/reduce_scatter | solution.py:87
  63.4 12.7 %collective-permute-start.6 = (f32[256,256]{1,0:T(8,128)}, f32[256,256]{1,0:T(8,128)S(1)}, u32[]{:S(2)}, u32[]{:S(2)}) collective-permute-start(f32[256,256]{1,0:T(8,128)} %get-tuple-element.7), channel_id=1, source_target_pairs={{4,0},{8,4},{12,8},{16,12},{20,16},{24,20},{28,24},{5,1},{9,5},{13... | collective-permute-start | bytes 786440 | tf_op jit(solution)/shard_map/ppermute | solution.py:20
  64.7 13.8 %collective-permute-start.7 = (f32[256,256]{1,0:T(8,128)S(1)}, f32[256,256]{1,0:T(8,128)S(1)}, u32[]{:S(2)}, u32[]{:S(2)}) collective-permute-start(f32[256,256]{1,0:T(8,128)S(1)} %get-tuple-element.6), channel_id=1, source_target_pairs={{0,4},{4,8},{8,12},{12,16},{16,20},{20,24},{24,28},{1,5},{5,9},{9,... | collective-permute-start | bytes 786440 | tf_op jit(solution)/shard_map/ppermute | solution.py:17
  73.2 2.9 %copy-start.8 = (f32[2048,256]{1,0:T(8,128)S(1)}, f32[2048,256]{1,0:T(8,128)}, u32[]{:S(2)}) copy-start(f32[2048,256]{1,0:T(8,128)} %get-tuple-element.19) | copy-start | bytes 6291460
  73.2 2.9 %copy-start.11 = (bf16[3,3,256,256]{3,2,1,0:T(8,128)(2,1)S(1)}, bf16[3,3,256,256]{3,2,1,0:T(8,128)(2,1)}, u32[]{:S(2)}) copy-start(bf16[3,3,256,256]{3,2,1,0:T(8,128)(2,1)} %param.6) | copy-start | bytes 3538948
  77.3 1.6 copy-start.13
  80.6 1.2 copy-start.5
  83.3 9.6 %collective-permute-start.8 = (f32[64,256]{1,0:T(8,128)S(1)}, f32[64,256]{1,0:T(8,128)S(1)}, u32[]{:S(2)}, u32[]{:S(2)}) collective-permute-start(f32[64,256]{1,0:T(8,128)S(1)} %get-tuple-element.5), channel_id=1, source_target_pairs={{4,0},{8,4},{12,8},{16,12},{20,16},{24,20},{28,24},{5,1},{9,5},{13... | collective-permute-start | bytes 196616 | tf_op jit(solution)/shard_map/ppermute | solution.py:20
  84.6 9.5 %collective-permute-start.9 = (f32[64,256]{1,0:T(8,128)S(1)}, f32[64,256]{1,0:T(8,128)S(1)}, u32[]{:S(2)}, u32[]{:S(2)}) collective-permute-start(f32[64,256]{1,0:T(8,128)S(1)} %get-tuple-element.4), channel_id=1, source_target_pairs={{0,4},{4,8},{8,12},{12,16},{16,20},{20,24},{24,28},{1,5},{5,9},{9,... | collective-permute-start | bytes 196616 | tf_op jit(solution)/shard_map/ppermute | solution.py:17
  92.9 1.6 copy-start.14
  94.5 1.7 copy-start.7
  102.3 117.0 %copy-start.1 = (bf16[256,1024]{1,0:T(8,128)(2,1)S(1)}, bf16[256,1024]{1,0:T(8,128)(2,1)}, u32[]{:S(2)}) copy-start(bf16[256,1024]{1,0:T(8,128)(2,1)} %param.7) | copy-start | bytes 1572868
  102.3 113.4 %all-reduce.3.cloned.1.call-start = ((), (), s32[]{:S(2)}) async-start(), calls=%async_computation.4 | async-start | bytes 1703936 | tf_op jit(solution)/shard_map/psum | solution.py:85
Sparse Core Ops, SparseCore 0:
  63.5 35.1 reduce-scatter.4
  102.5 54.1 reduce-scatter.2
  160.3 55.4 all-reduce.2
where the time goes:
time: 230 us; the launch traced here: 226 us
  waiting for transfers between devices  114 us (50%)
  matrix products  59.3 us (26%)
  starting transfers between devices  30.3 us (13%)
  between operations  14.6 us (6%)
  local copies, waits for them, and re-layouts  6.18 us (3%)
    psum x1, waiting for transfers between devices, on_device(): summed = lax.psum((conv_local, head_local), 'tm')  59 us
    reduce_scatter x1, waiting for transfers between devices, on_device(): lax.psum_scatter(summed[0], 'pen', scatter_dimension=2, tiled=True)  54.3 us
    dot_general x10, matrix products, trans_dot(): lax.dot_general(left.astype(jnp.float32), right, (((0,), (0,)), ((), ()))...  25.7 us
    ppermute x5, starting transfers between devices, padded_2(): lax.ppermute(lax.slice_in_dim(block, block.shape[dim] - width, None, axis...  23.8 us
    dot_general x7, matrix products, full_dot(): jnp.dot(left, right.astype(jnp.float32), precision=lax.Precision.HIGHEST,...  19.8 us
    ppermute x5, starting transfers between devices, padded_2(): lax.ppermute(lax.slice_in_dim(block, 0, width, axis=dim), axis, backward)  6.44 us
    dot_general x3, matrix products, three_taps(): jnp.dot(source[0:length], weights[0], preferred_element_type=jnp.float32)  5 us
    dot_general x1, matrix products, on_device(): pred = jnp.dot(hidden, head_weight, preferred_element_type=jnp.float32)  4.92 us
  transfers between devices with their start and end apart: 13, of which 4 were waited for; matrix products, arithmetic and copies ran while one was open for 12% of the time, Pallas kernels for 0%

commit v1 on v0

v1 whole, which is shorter than its diff:
```python
import functools

import jax
import jax.numpy as jnp
from jax import lax
from jax.experimental import pallas as pl
from jax.experimental.pallas import tpu as pltpu
from jax.sharding import PartitionSpec as P

W = 256
FEAT = 1024
DILATIONS = (16, 64, 256)
BACK = DILATIONS[1] + DILATIONS[2]
HALO = BACK + sum(DILATIONS)
SCALE = 2.0 / FEAT
SUM_LANES = 9 * W + FEAT


def dot(left, right):
    return lax.dot_general(
        left, right, (((1,), (0,)), ((), ())), preferred_element_type=jnp.float32
    )


def dot_nt(left, right):
    return lax.dot_general(
        left, right, (((1,), (1,)), ((), ())), preferred_element_type=jnp.float32
    )


def dot_tn(left, right):
    return lax.dot_general(
        left, right, (((0,), (0,)), ((), ())), preferred_element_type=jnp.float32
    )


def split(value):
    high = value.astype(jnp.bfloat16)
    return high, (value - high.astype(jnp.float32)).astype(jnp.bfloat16)


def tile_of(rows, most):
    best = 16
    for size in range(16, most + 1, 16):
        if rows % size == 0:
            best = size
    return best


def project_kernel(target_ref, head_ref, out_ref):
    out_ref[...] = dot_nt(target_ref[...], head_ref[...])


def project(target, head_weight):
    count = target.shape[0]
    tile = tile_of(count, 512)
    return pl.pallas_call(
        project_kernel,
        grid=(count // tile,),
        in_specs=[
            pl.BlockSpec((tile, FEAT), lambda i: (i, 0)),
            pl.BlockSpec((W, FEAT), lambda i: (0, 0)),
        ],
        out_specs=pl.BlockSpec((tile, W), lambda i: (i, 0)),
        out_shape=jax.ShapeDtypeStruct((count, W), jnp.float32),
        cost_estimate=pl.CostEstimate(
            flops=2 * count * W * FEAT, bytes_accessed=count * (2 * FEAT + 4 * W), transcendentals=0
        ),
        name="project_targets",
    )(target, head_weight)


def loop_rows(start, stop, most, body):
    tile = tile_of(stop - start, most)

    def step(index, carry):
        body(index * tile + start, tile)
        return carry

    lax.fori_loop(0, (stop - start) // tile, step, 0)


def main_kernel(
    count,
    place_ref,
    clip_ref,
    clip_a_ref,
    clip_b_ref,
    target_ref,
    proj_ref,
    proj_a_ref,
    proj_b_ref,
    conv_ref,
    head_ref,
    out_ref,
    h0,
    h1,
    h2,
    h3,
    s1,
    s2,
    s3,
    err,
    back,
    conv_t,
    gram,
    head_acc,
):
    first = place_ref[0] == 0
    last = place_ref[0] == place_ref[1] - 1
    even = place_ref[0] % 2 == 0
    hidden = (h0, h1, h2, h3)
    slopes = (None, s1, s2, s3)

    def at(frame, size):
        return pl.ds(pl.multiple_of(frame + HALO, 16), size)

    def inside(frame, size):
        rows = lax.broadcasted_iota(jnp.int32, (size, 1), 0) + frame
        return ((rows >= 0) | jnp.logical_not(first)) & ((rows < count) | jnp.logical_not(last))

    h0[HALO : HALO + count, :] = clip_ref[...]
    err[HALO : HALO + count, :] = proj_ref[...]

    @pl.when(even)
    def _():
        h0[0:HALO, :] = clip_b_ref[...]
        h0[HALO + count :, :] = clip_a_ref[...]
        err[HALO - BACK : HALO, :] = proj_b_ref[...]
        err[HALO + count : HALO + count + BACK, :] = proj_a_ref[...]

    @pl.when(jnp.logical_not(even))
    def _():
        h0[0:HALO, :] = clip_a_ref[...]
        h0[HALO + count :, :] = clip_b_ref[...]
        err[HALO - BACK : HALO, :] = proj_a_ref[...]
        err[HALO + count : HALO + count + BACK, :] = proj_b_ref[...]

    for layer in (1, 2):
        for k in range(3):
            turned = jnp.transpose(conv_ref[layer, k])
            conv_t[layer - 1, 2 * k * W : (2 * k + 1) * W, :] = turned
            conv_t[layer - 1, (2 * k + 1) * W : (2 * k + 2) * W, :] = turned
    high, low = split(dot_nt(head_ref[...], head_ref[...]))
    gram[0:W, :] = high
    gram[W : 2 * W, :] = low

    reach = HALO
    for layer in range(3):
        width = DILATIONS[layer]
        reach -= width
        source, result, slope = hidden[layer], hidden[layer + 1], slopes[layer + 1]
        weights = conv_ref[layer].reshape(3 * W, W)

        def forward(frame, size):
            taps = [source[at(frame + (k - 1) * width, size), :] for k in range(3)]
            pre = dot(jnp.concatenate(taps, axis=1), weights)
            sig = 0.5 * jnp.tanh(0.5 * pre) + 0.5
            new = taps[1].astype(jnp.float32) + pre * sig
            result[at(frame, size), :] = jnp.where(inside(frame, size), new, 0.0).astype(jnp.bfloat16)
            slope[at(frame, size), :] = sig * (1.0 + pre * (1.0 - sig))

        loop_rows(-reach, count + reach, 416, forward)

    def store_back(frame, size, error, slope):
        high, low = split(error * slope[at(frame, size), :])
        back[at(frame, size), 0:W] = high
        back[at(frame, size), W : 2 * W] = low

    def head_error(frame, size):
        top = h3[at(frame, size), :]
        error = SCALE * (dot(jnp.concatenate([top, top], axis=1), gram[...]) - err[at(frame, size), :])
        err[at(frame, size), :] = error
        store_back(frame, size, error, s3)

    loop_rows(-BACK, count + BACK, 416, head_error)

    head_acc[...] = jnp.zeros_like(head_acc)

    def head_sum(frame, size):
        top = h3[at(frame, size), :]
        goal = target_ref[pl.ds(pl.multiple_of(frame, 16), size), :]
        head_acc[...] += dot_tn(top, jnp.concatenate([goal, top], axis=1))

    loop_rows(0, count, 512, head_sum)
    square = head_acc[:, FEAT:]
    high = square.astype(jnp.bfloat16)
    middle, low = split(square - high.astype(jnp.float32))
    weight = head_ref[...]
    product = dot(high, weight) + (dot(middle, weight) + dot(low, weight))
    out_ref[:, 9 * W :] = SCALE * (product - head_acc[:, 0:FEAT])

    reach = BACK
    for layer in (2, 1, 0):
        width = DILATIONS[layer]
        source = hidden[layer]
        first_lane = 3 * layer * W
        out_ref[:, first_lane : first_lane + 3 * W] = jnp.zeros((W, 3 * W), jnp.float32)

        def weight_sum(frame, size):
            right = back[at(frame, size), :]
            for k in range(3):
                both = dot_tn(source[at(frame + (k - 1) * width, size), :], right)
                lanes = pl.ds(first_lane + k * W, W)
                out_ref[:, lanes] += both[:, 0:W] + both[:, W:]

        loop_rows(0, count, 512, weight_sum)
        if layer > 0:
            reach -= width

            def pull_back(frame, size):
                taps = [back[at(frame - (k - 1) * width, size), :] for k in range(3)]
                err[at(frame, size), :] += dot(jnp.concatenate(taps, axis=1), conv_t[layer - 1])

            loop_rows(-reach, count + reach, 416, pull_back)

            def slope_back(frame, size):
                error = jnp.where(inside(frame, size), err[at(frame, size), :], 0.0)
                store_back(frame, size, error, slopes[layer])

            loop_rows(-reach, count + reach, 416, slope_back)


def main(place, clip, clip_a, clip_b, target, proj, proj_a, proj_b, conv_weight, head_weight):
    count = clip.shape[0]
    rows = count + 2 * HALO
    vmem = pl.BlockSpec(memory_space=pltpu.VMEM)
    flops = 2 * W * W * (9 * rows + 14 * rows + 18 * count + 6 * count)
    return pl.pallas_call(
        functools.partial(main_kernel, count),
        in_specs=[pl.BlockSpec(memory_space=pltpu.SMEM)] + [vmem] * 9,
        out_specs=vmem,
        out_shape=jax.ShapeDtypeStruct((W, SUM_LANES), jnp.float32),
        scratch_shapes=[pltpu.VMEM((rows, W), jnp.bfloat16)] * 4
        + [pltpu.VMEM((rows, W), jnp.float32)] * 4
        + [
            pltpu.VMEM((rows, 2 * W), jnp.bfloat16),
            pltpu.VMEM((2, 6 * W, W), jnp.bfloat16),
            pltpu.VMEM((2 * W, W), jnp.bfloat16),
            pltpu.VMEM((W, FEAT + W), jnp.float32),
        ],
        compiler_params=pltpu.CompilerParams(vmem_limit_bytes=56 * 2**20),
        cost_estimate=pl.CostEstimate(flops=flops, bytes_accessed=16 * 2**20, transcendentals=3 * rows * W),
        name="forward_backward",
    )(place, clip, clip_a, clip_b, target, proj, proj_a, proj_b, conv_weight, head_weight)


def edges(block, width):
    count = lax.axis_size("tm")
    even = lax.axis_index("tm") % 2 == 0
    low, high = block[:width], block[block.shape[0] - width :]
    near = [(i, i ^ 1) for i in range(count)]
    far = [(i, i + 1) for i in range(1, count - 1, 2)]
    far = far + [(j, i) for i, j in far]
    from_far = lax.ppermute(jnp.where(even, low, high), "tm", far)
    from_near = lax.ppermute(jnp.where(even, high, low), "tm", near)
    return from_near, from_far


def pick(array, index, axis):
    return lax.dynamic_index_in_dim(array, index, axis, keepdims=False)


def reduce_rows(total):
    n, pens = lax.axis_size("tm"), lax.axis_size("pen")
    place, pen = lax.axis_index("tm"), lax.axis_index("pen")
    core, group, groups = place % 2, place // 2, n // 2
    part = total.reshape(pens, 2, groups, total.shape[0] // (pens * n), total.shape[1])
    other = lax.ppermute(pick(part, 1 - core, 1), "tm", [(i, i ^ 1) for i in range(n)])
    part = pick(part, core, 1) + other
    arrived = [
        lax.ppermute(pick(part, group ^ j, 1), "tm", [(i, i ^ (2 * j)) for i in range(n)])
        for j in range(1, groups)
    ]
    part = pick(part, group, 1)
    for other in arrived:
        part = part + other
    arrived = [
        lax.ppermute(pick(part, pen ^ j, 0), "pen", [(i, i ^ j) for i in range(pens)])
        for j in range(1, pens)
    ]
    part = pick(part, pen, 0)
    for other in arrived:
        part = part + other
    return part


def gather_rows(part):
    n = lax.axis_size("tm")
    place = lax.axis_index("tm")
    core, group, groups = place % 2, place // 2, n // 2
    half = jnp.zeros((groups,) + part.shape, part.dtype)
    half = lax.dynamic_update_index_in_dim(half, part, group, 0)
    for j in range(1, groups):
        other = lax.ppermute(part, "tm", [(i, i ^ (2 * j)) for i in range(n)])
        half = lax.dynamic_update_index_in_dim(half, other, group ^ j, 0)
    half = half.reshape((-1,) + part.shape[1:])
    other = lax.ppermute(half, "tm", [(i, i ^ 1) for i in range(n)])
    return jnp.concatenate([jnp.where(core == 0, half, other), jnp.where(core == 0, other, half)], axis=0)


def on_device(clips, targets, conv_weight, head_weight):
    clip, target = clips[0], targets[0]
    place = jnp.stack([lax.axis_index("tm"), lax.axis_size("tm")]).astype(jnp.int32)
    clip_a, clip_b = edges(clip, HALO)
    proj = project(target, head_weight)
    proj_a, proj_b = edges(proj, BACK)
    total = main(place, clip, clip_a, clip_b, target, proj, proj_a, proj_b, conv_weight, head_weight)
    mine = gather_rows(reduce_rows(total))
    conv = mine[:, : 9 * W].reshape(-1, 3, 3, W).transpose(1, 2, 0, 3)
    return conv, mine[:, 9 * W :]


def solution(mesh):
    in_specs = (P("pen", "tm", None), P("pen", "tm", None), P(), P())
    out_specs = (P(None, None, "pen", None), P("pen", None))
    return jax.shard_map(
        on_device, mesh=mesh, in_specs=in_specs, out_specs=out_specs, check_vma=False
    )
```

time: 230 us -> 118 us (0.51); the launches traced: 226 us -> 118 us
  waiting for transfers between devices: 114 us -> 36 us
  matrix products: 59.3 us -> 0 us
  Pallas kernels: 0 us -> 41.6 us
  between operations: 14.6 us -> 0.82 us
  other arithmetic: 1.73 us -> 6.45 us
  starting transfers between devices: 30.3 us -> 27.9 us
    dot_general x27 -> x0, matrix products: 59.3 us -> none  [the longest x10 25.7 us: trans_dot(): lax.dot_general(left.astype(jnp.float32), right, (((0,), (0,)), ((), ()))...]
    psum x1 -> x0, waiting for transfers between devices: 59 us -> none  [on_device(): summed = lax.psum((conv_local, head_local), 'tm')]
    reduce_scatter x2 -> x0, waiting for transfers between devices: 54.3 us -> none  [the longest x1 54.3 us: on_device(): lax.psum_scatter(summed[0], 'pen', scatter_dimension=2, tiled=True)]
    pallas_call x0 -> x2, Pallas kernels: none -> 41.6 us  [the longest x1 36.4 us: main(): pl.pallas_call(functools.partial(main_kernel, count), in_specs=[pl.BlockS...]
    ppermute x10 -> x15, waiting for transfers between devices: 0.76 us -> 36 us  [the longest x3 19.3 us: reduce_rows(): lax.ppermute(pick(part, group ^ j, 1), 'tm', [(i, i ^ 2 * j) for i in ran...]
    add x0 -> x2, other arithmetic: none -> 2.71 us  [the longest x1 1.63 us: reduce_rows(): part = pick(part, core, 1) + other]
    unnamed x32 -> x9, local copies, waits for them, and re-layouts: 4.54 us -> 1.93 us
    squeeze x0 -> x3, local copies, waits for them, and re-layouts: none -> 2.47 us  [pick(): return lax.dynamic_index_in_dim(array, index, axis, keepdims=False)]
  transfers between devices with their start and end apart: 13 -> 15, of which waited for: 4 -> 10; matrix products, arithmetic and copies ran while one was open for 12% -> 2% of each run, Pallas kernels for 0% -> 4%
where the time goes in v1:
time: 118 us
  Pallas kernels  41.6 us (35%)
  waiting for transfers between devices  36 us (31%)
  starting transfers between devices  27.9 us (24%)
  other arithmetic  6.45 us (5%)
  local copies, waits for them, and re-layouts  4.78 us (4%)
    pallas_call x1, Pallas kernels, main(): pl.pallas_call(functools.partial(main_kernel, count), in_specs=[pl.BlockS...  36.4 us
    ppermute x3, waiting for transfers between devices, reduce_rows(): lax.ppermute(pick(part, group ^ j, 1), 'tm', [(i, i ^ 2 * j) for i in ran...  19.3 us
    ppermute x1, starting transfers between devices, reduce_rows(): lax.ppermute(pick(part, 1 - core, 1), 'tm', [(i, i ^ 1) for i in range(n)])  9.81 us
    ppermute x3, waiting for transfers between devices, reduce_rows(): lax.ppermute(pick(part, pen ^ j, 0), 'pen', [(i, i ^ j) for i in range(pe...  7.65 us
    pallas_call x1, Pallas kernels, project(): pl.pallas_call(project_kernel, grid=(count // tile,), in_specs=[pl.BlockS...  5.24 us
    ppermute x3, starting transfers between devices, reduce_rows(): lax.ppermute(pick(part, pen ^ j, 0), 'pen', [(i, i ^ j) for i in range(pe...  4.45 us
    ppermute x2, starting transfers between devices, edges(): from_near = lax.ppermute(jnp.where(even, high, low), 'tm', near)  4.43 us
    ppermute x3, starting transfers between devices, reduce_rows(): lax.ppermute(pick(part, group ^ j, 1), 'tm', [(i, i ^ 2 * j) for i in ran...  4.2 us
  transfers between devices with their start and end apart: 15, of which 10 were waited for; matrix products, arithmetic and copies ran while one was open for 2% of the time, Pallas kernels for 4%

profile of v1, /device:TPU:0, one launch (start us, length us, event | category | flops | bytes accessed | tf_op | source)
XLA Modules:
  0.0 117.6 jit_solution(7011488623804988925)
XLA Ops:
  0.6 1.1 select_bitcast_fusion
  1.8 0.5 collective-permute-start
  2.3 0.7 collective-permute-start.1
  3.0 5.2 %project_targets.1.proj_ref = f32[2048,256]{1,0:T(8,128)} custom-call(bf16[2048,1024]{1,0:T(8,128)(2,1)} %bitcast.49, bf16[256,1024]{1,0:T(8,128)(2,1)} %head_ref.3), custom_call_target="tpu_custom_call" | custom-call | flops 1073741824 | bytes 6291456 | tf_op jit(solution)/shard_map/project_targets/pallas_call | solution.py:57
  8.2 1.1 slice_select_fusion
  9.3 3.9 %collective-permute-start.2 = (f32[320,256]{1,0:T(8,128)S(1)}, f32[320,256]{1,0:T(8,128)S(1)}, u32[]{:S(2)}, u32[]{:S(2)}) collective-permute-start(f32[320,256]{1,0:T(8,128)S(1)} %get-tuple-element.7), channel_id=1, source_target_pairs={{0,4},{4,0},{8,12},{12,8},{16,20},{20,16},{24,28},{28,24},{1,5},{5... | collective-permute-start | bytes 983048 | tf_op jit(solution)/shard_map/ppermute | solution.py:256
  13.2 0.7 collective-permute-start.3
  13.9 0.7 pad_add_fusion.place_ref
  14.6 0.0 collective-permute-done.2.proj_a_ref
  14.6 0.0 collective-permute-done.3.proj_b_ref
  14.6 0.0 collective-permute-done.clip_a_ref
  14.6 0.0 copy-start
  14.6 0.0 collective-permute-done.1.clip_b_ref
  14.7 0.7 copy-done.2
  15.3 0.1 copy-done.3
  15.4 0.1 copy-done
  15.5 0.1 copy-done.1
  15.7 36.4 %forward_backward.1 = f32[256,3328]{1,0:T(8,128)} custom-call(s32[2]{0:T(128)} %pad_add_fusion.place_ref, bf16[2048,256]{1,0:T(8,128)(2,1)} %bitcast.55, bf16[656,256]{1,0:T(8,128)(2,1)} %copy-done, bf16[656,256]{1,0:T(8,128)(2,1)} %copy-done.1, bf16[2048,1024]{1,0:T(8,128)(2,1)} %bitcast.50, f32[2048,256]{1,0:T(8,128)} %project_targets.1.proj_ref, ...), custom_call_target="tpu_custom_call" | custom-call | flops 16571695104 | bytes 16777216 | tf_op jit(solution)/shard_map/forward_backward/pallas_call | solution.py:229
  52.0 1.6 %dynamic-slice_bitcast_fusion = f32[4,4,8,3328]{3,2,1,0:T(8,128)S(1)} fusion(f32[4,2,4,8,3328]{4,3,2,1,0:T(8,128)} %bitcast.51, s32[]{:T(128)S(6)} %select_n.109), kind=kLoop, calls=%fused_computation.1 | loop fusion | bytes 3407876 | tf_op jit(solution)/shard_map/jit(dynamic_index_in_dim)/squeeze | solution.py:261
  53.6 9.8 %collective-permute-start.4 = (f32[4,4,8,3328]{3,2,1,0:T(8,128)S(1)}, f32[4,4,8,3328]{3,2,1,0:T(8,128)S(1)}, u32[]{:S(2)}, u32[]{:S(2)}) collective-permute-start(f32[4,4,8,3328]{3,2,1,0:T(8,128)S(1)} %dynamic-slice_bitcast_fusion), channel_id=1, source_target_pairs={{0,4},{4,0},{8,12},{12,8},{16,20},{20,16},{24,28},{28,24},{1,5},{5... | collective-permute-start | bytes 5111816 | tf_op jit(solution)/shard_map/ppermute | solution.py:269
  63.5 3.2 %collective-permute-done.4 = f32[4,4,8,3328]{3,2,1,0:T(8,128)S(1)} collective-permute-done((f32[4,4,8,3328]{3,2,1,0:T(8,128)S(1)}, f32[4,4,8,3328]{3,2,1,0:T(8,128)S(1)}, u32[]{:S(2)}, u32[]{:S(2)}) %collective-permute-start.4) | collective-permute-done | bytes 1703968 | tf_op jit(solution)/shard_map/ppermute | solution.py:269
  66.7 1.6 %bitcast_add_fusion = f32[4,4,8,3328]{3,2,1,0:T(8,128)S(1)} fusion(f32[4,4,8,3328]{3,2,1,0:T(8,128)S(1)} %collective-permute-done.4, f32[4,2,4,8,3328]{4,3,2,1,0:T(8,128)} %bitcast.52, s32[]{:T(128)S(6)} %select_n.108), kind=kLoop, calls=%fused_computation | loop fusion | flops 425984 | bytes 5111812 | tf_op jit(solution)/shard_map/add | solution.py:270
  68.3 0.9 dynamic-slice_bitcast_fusion.3
  69.2 2.0 %collective-permute-start.5 = (f32[4,8,3328]{2,1,0:T(8,128)}, f32[4,8,3328]{2,1,0:T(8,128)S(1)}, u32[]{:S(2)}, u32[]{:S(2)}) collective-permute-start(f32[4,8,3328]{2,1,0:T(8,128)} %get-tuple-element.8), channel_id=1, source_target_pairs={{0,8},{4,12},{8,0},{12,4},{16,24},{20,28},{24,16},{28,20},{1,9},{5... | collective-permute-start | bytes 1277960 | tf_op jit(solution)/shard_map/ppermute | solution.py:272
  71.2 0.7 collective-permute-start.6
  71.9 1.5 %collective-permute-start.7 = (f32[4,8,3328]{2,1,0:T(8,128)S(1)}, f32[4,8,3328]{2,1,0:T(8,128)}, u32[]{:S(2)}, u32[]{:S(2)}) collective-permute-start(f32[4,8,3328]{2,1,0:T(8,128)S(1)} %get-tuple-element.9), channel_id=1, source_target_pairs={{0,24},{4,28},{8,16},{12,20},{16,8},{20,12},{24,0},{28,4},{1,25},{... | collective-permute-start | bytes 1277960 | tf_op jit(solution)/shard_map/ppermute | solution.py:272
  73.4 8.6 %collective-permute-done.5 = f32[4,8,3328]{2,1,0:T(8,128)S(1)} collective-permute-done((f32[4,8,3328]{2,1,0:T(8,128)}, f32[4,8,3328]{2,1,0:T(8,128)S(1)}, u32[]{:S(2)}, u32[]{:S(2)}) %collective-permute-start.5) | collective-permute-done | bytes 426016 | tf_op jit(solution)/shard_map/ppermute | solution.py:272
  82.0 8.5 %collective-permute-done.6 = f32[4,8,3328]{2,1,0:T(8,128)S(1)} collective-permute-done((f32[4,8,3328]{2,1,0:T(8,128)S(1)}, f32[4,8,3328]{2,1,0:T(8,128)S(1)}, u32[]{:S(2)}, u32[]{:S(2)}) %collective-permute-start.6) | collective-permute-done | bytes 426016 | tf_op jit(solution)/shard_map/ppermute | solution.py:272
  90.4 2.2 %collective-permute-done.7 = f32[4,8,3328]{2,1,0:T(8,128)} collective-permute-done((f32[4,8,3328]{2,1,0:T(8,128)S(1)}, f32[4,8,3328]{2,1,0:T(8,128)}, u32[]{:S(2)}, u32[]{:S(2)}) %collective-permute-start.7) | collective-permute-done | bytes 426016 | tf_op jit(solution)/shard_map/ppermute | solution.py:272
  92.6 1.1 fusion.2
  93.8 3.7 %collective-permute-start.10 = (f32[8,3328]{1,0:T(8,128)S(1)}, f32[8,3328]{1,0:T(8,128)S(1)}, u32[]{:S(2)}, u32[]{:S(2)}) collective-permute-start(f32[8,3328]{1,0:T(8,128)S(1)} %get-tuple-element.16), channel_id=1, source_target_pairs={{0,3},{1,2},{2,1},{3,0},{4,7},{5,6},{6,5},{7,4},{8,11},{9,10},{10,... | collective-permute-start | bytes 319496 | tf_op jit(solution)/shard_map/ppermute | solution.py:279
  97.4 0.0 collective-permute-start.8
  97.4 0.8 collective-permute-start.9
  98.2 2.9 %collective-permute-done.10 = f32[8,3328]{1,0:T(8,128)S(1)} collective-permute-done((f32[8,3328]{1,0:T(8,128)S(1)}, f32[8,3328]{1,0:T(8,128)S(1)}, u32[]{:S(2)}, u32[]{:S(2)}) %collective-permute-start.10) | collective-permute-done | bytes 106528 | tf_op jit(solution)/shard_map/ppermute | solution.py:279
  101.1 2.3 %collective-permute-done.8 = f32[8,3328]{1,0:T(8,128)S(1)} collective-permute-done((f32[8,3328]{1,0:T(8,128)S(1)}, f32[8,3328]{1,0:T(8,128)S(1)}, u32[]{:S(2)}, u32[]{:S(2)}) %collective-permute-start.8) | collective-permute-done | bytes 106528 | tf_op jit(solution)/shard_map/ppermute | solution.py:279
  103.4 2.5 %collective-permute-done.9 = f32[8,3328]{1,0:T(8,128)S(1)} collective-permute-done((f32[8,3328]{1,0:T(8,128)S(1)}, f32[8,3328]{1,0:T(8,128)S(1)}, u32[]{:S(2)}, u32[]{:S(2)}) %collective-permute-start.9) | collective-permute-done | bytes 106528 | tf_op jit(solution)/shard_map/ppermute | solution.py:279
  105.9 0.7 collective-permute-start.11
  106.6 1.2 %collective-permute-start.12 = (f32[8,3328]{1,0:T(8,128)S(1)}, f32[8,3328]{1,0:T(8,128)S(1)}, u32[]{:S(2)}, u32[]{:S(2)}) collective-permute-start(f32[8,3328]{1,0:T(8,128)S(1)} %get-tuple-element.5), channel_id=1, source_target_pairs={{0,16},{4,20},{8,24},{12,28},{16,0},{20,4},{24,8},{28,12},{1,17},{... | collective-permute-start | bytes 319496 | tf_op jit(solution)/shard_map/ppermute | solution.py:295
  107.8 1.6 %collective-permute-start.13 = (f32[8,3328]{1,0:T(8,128)S(1)}, f32[8,3328]{1,0:T(8,128)S(1)}, u32[]{:S(2)}, u32[]{:S(2)}) collective-permute-start(f32[8,3328]{1,0:T(8,128)S(1)} %get-tuple-element.5), channel_id=1, source_target_pairs={{0,24},{4,28},{8,16},{12,20},{16,8},{20,12},{24,0},{28,4},{1,25},{... | collective-permute-start | bytes 319496 | tf_op jit(solution)/shard_map/ppermute | solution.py:295
  109.5 2.3 %collective-permute-done.11 = f32[8,3328]{1,0:T(8,128)S(1)} collective-permute-done((f32[8,3328]{1,0:T(8,128)S(1)}, f32[8,3328]{1,0:T(8,128)S(1)}, u32[]{:S(2)}, u32[]{:S(2)}) %collective-permute-start.11) | collective-permute-done | bytes 106528 | tf_op jit(solution)/shard_map/ppermute | solution.py:295
  111.8 1.8 %collective-permute-done.12 = f32[8,3328]{1,0:T(8,128)S(1)} collective-permute-done((f32[8,3328]{1,0:T(8,128)S(1)}, f32[8,3328]{1,0:T(8,128)S(1)}, u32[]{:S(2)}, u32[]{:S(2)}) %collective-permute-start.12) | collective-permute-done | bytes 106528 | tf_op jit(solution)/shard_map/ppermute | solution.py:295
  113.7 0.0 collective-permute-done.13
  113.7 0.1 collective-permute-start.14
  113.8 1.8 %collective-permute-done.14 = f32[32,3328]{1,0:T(8,128)S(1)} collective-permute-done((f32[32,3328]{1,0:T(8,128)S(1)}, f32[32,3328]{1,0:T(8,128)S(1)}, u32[]{:S(2)}, u32[]{:S(2)}) %collective-permute-start.14) | collective-permute-done | bytes 426016 | tf_op jit(solution)/shard_map/ppermute | solution.py:298
  115.5 0.1 broadcast_select_fusion
  115.6 0.7 pad_maximum_fusion
  116.3 0.3 reshape.21
  116.7 0.9 copy.7
  (10 shorter events, 0.2 us)
Async XLA Ops:
  1.8 12.8 %collective-permute-start = (bf16[656,256]{1,0:T(8,128)(2,1)S(1)}, bf16[656,256]{1,0:T(8,128)(2,1)S(1)}, u32[]{:S(2)}, u32[]{:S(2)}) collective-permute-start(bf16[656,256]{1,0:T(8,128)(2,1)S(1)} %get-tuple-element.12), channel_id=1, source_target_pairs={{0,4},{4,0},{8,12},{12,8},{16,20},{20,16},{24,28},{28,24},{1,5},{5... | collective-permute-start | bytes 1007624 | tf_op jit(solution)/shard_map/ppermute | solution.py:256
  2.3 12.3 %collective-permute-start.1 = (bf16[656,256]{1,0:T(8,128)(2,1)S(1)}, bf16[656,256]{1,0:T(8,128)(2,1)S(1)}, u32[]{:S(2)}, u32[]{:S(2)}) collective-permute-start(bf16[656,256]{1,0:T(8,128)(2,1)S(1)} %get-tuple-element.11), channel_id=1, source_target_pairs={{4,8},{12,16},{20,24},{8,4},{16,12},{24,20},{5,9},{13,17},{21,25},... | collective-permute-start | bytes 1007624 | tf_op jit(solution)/shard_map/ppermute | solution.py:255
  9.3 5.3 %collective-permute-start.2 = (f32[320,256]{1,0:T(8,128)S(1)}, f32[320,256]{1,0:T(8,128)S(1)}, u32[]{:S(2)}, u32[]{:S(2)}) collective-permute-start(f32[320,256]{1,0:T(8,128)S(1)} %get-tuple-element.7), channel_id=1, source_target_pairs={{0,4},{4,0},{8,12},{12,8},{16,20},{20,16},{24,28},{28,24},{1,5},{5... | collective-permute-start | bytes 983048 | tf_op jit(solution)/shard_map/ppermute | solution.py:256
  13.2 1.3 %collective-permute-start.3 = (f32[320,256]{1,0:T(8,128)S(1)}, f32[320,256]{1,0:T(8,128)S(1)}, u32[]{:S(2)}, u32[]{:S(2)}) collective-permute-start(f32[320,256]{1,0:T(8,128)S(1)} %get-tuple-element.6), channel_id=1, source_target_pairs={{4,8},{12,16},{20,24},{8,4},{16,12},{24,20},{5,9},{13,17},{21,25},... | collective-permute-start | bytes 983048 | tf_op jit(solution)/shard_map/ppermute | solution.py:255
  14.6 0.7 copy-start.2
  14.6 0.8 copy-start.3
  14.6 0.9 copy-start
  14.6 1.0 copy-start.1
  53.6 13.0 %collective-permute-start.4 = (f32[4,4,8,3328]{3,2,1,0:T(8,128)S(1)}, f32[4,4,8,3328]{3,2,1,0:T(8,128)S(1)}, u32[]{:S(2)}, u32[]{:S(2)}) collective-permute-start(f32[4,4,8,3328]{3,2,1,0:T(8,128)S(1)} %dynamic-slice_bitcast_fusion), channel_id=1, source_target_pairs={{0,4},{4,0},{8,12},{12,8},{16,20},{20,16},{24,28},{28,24},{1,5},{5... | collective-permute-start | bytes 5111816 | tf_op jit(solution)/shard_map/ppermute | solution.py:269
  69.2 12.8 %collective-permute-start.5 = (f32[4,8,3328]{2,1,0:T(8,128)}, f32[4,8,3328]{2,1,0:T(8,128)S(1)}, u32[]{:S(2)}, u32[]{:S(2)}) collective-permute-start(f32[4,8,3328]{2,1,0:T(8,128)} %get-tuple-element.8), channel_id=1, source_target_pairs={{0,8},{4,12},{8,0},{12,4},{16,24},{20,28},{24,16},{28,20},{1,9},{5... | collective-permute-start | bytes 1277960 | tf_op jit(solution)/shard_map/ppermute | solution.py:272
  71.2 19.3 %collective-permute-start.6 = (f32[4,8,3328]{2,1,0:T(8,128)S(1)}, f32[4,8,3328]{2,1,0:T(8,128)S(1)}, u32[]{:S(2)}, u32[]{:S(2)}) collective-permute-start(f32[4,8,3328]{2,1,0:T(8,128)S(1)} %get-tuple-element.10), channel_id=1, source_target_pairs={{0,16},{4,20},{8,24},{12,28},{16,0},{20,4},{24,8},{28,12},{1,17},{... | collective-permute-start | bytes 1277960 | tf_op jit(solution)/shard_map/ppermute | solution.py:272
  71.9 20.7 %collective-permute-start.7 = (f32[4,8,3328]{2,1,0:T(8,128)S(1)}, f32[4,8,3328]{2,1,0:T(8,128)}, u32[]{:S(2)}, u32[]{:S(2)}) collective-permute-start(f32[4,8,3328]{2,1,0:T(8,128)S(1)} %get-tuple-element.9), channel_id=1, source_target_pairs={{0,24},{4,28},{8,16},{12,20},{16,8},{20,12},{24,0},{28,4},{1,25},{... | collective-permute-start | bytes 1277960 | tf_op jit(solution)/shard_map/ppermute | solution.py:272
  93.8 7.3 %collective-permute-start.10 = (f32[8,3328]{1,0:T(8,128)S(1)}, f32[8,3328]{1,0:T(8,128)S(1)}, u32[]{:S(2)}, u32[]{:S(2)}) collective-permute-start(f32[8,3328]{1,0:T(8,128)S(1)} %get-tuple-element.16), channel_id=1, source_target_pairs={{0,3},{1,2},{2,1},{3,0},{4,7},{5,6},{6,5},{7,4},{8,11},{9,10},{10,... | collective-permute-start | bytes 319496 | tf_op jit(solution)/shard_map/ppermute | solution.py:279
  97.4 6.0 %collective-permute-start.8 = (f32[8,3328]{1,0:T(8,128)S(1)}, f32[8,3328]{1,0:T(8,128)S(1)}, u32[]{:S(2)}, u32[]{:S(2)}) collective-permute-start(f32[8,3328]{1,0:T(8,128)S(1)} %get-tuple-element.15), channel_id=1, source_target_pairs={{0,1},{1,0},{2,3},{3,2},{4,5},{5,4},{6,7},{7,6},{8,9},{9,8},{10,11... | collective-permute-start | bytes 319496 | tf_op jit(solution)/shard_map/ppermute | solution.py:279
  97.4 8.4 %collective-permute-start.9 = (f32[8,3328]{1,0:T(8,128)S(1)}, f32[8,3328]{1,0:T(8,128)S(1)}, u32[]{:S(2)}, u32[]{:S(2)}) collective-permute-start(f32[8,3328]{1,0:T(8,128)S(1)} %get-tuple-element.17), channel_id=1, source_target_pairs={{0,2},{1,3},{2,0},{3,1},{4,6},{5,7},{6,4},{7,5},{8,10},{9,11},{10,... | collective-permute-start | bytes 319496 | tf_op jit(solution)/shard_map/ppermute | solution.py:279
  105.9 5.9 %collective-permute-start.11 = (f32[8,3328]{1,0:T(8,128)S(1)}, f32[8,3328]{1,0:T(8,128)S(1)}, u32[]{:S(2)}, u32[]{:S(2)}) collective-permute-start(f32[8,3328]{1,0:T(8,128)S(1)} %get-tuple-element.5), channel_id=1, source_target_pairs={{0,8},{4,12},{8,0},{12,4},{16,24},{20,28},{24,16},{28,20},{1,9},{5... | collective-permute-start | bytes 319496 | tf_op jit(solution)/shard_map/ppermute | solution.py:295
  106.6 7.0 %collective-permute-start.12 = (f32[8,3328]{1,0:T(8,128)S(1)}, f32[8,3328]{1,0:T(8,128)S(1)}, u32[]{:S(2)}, u32[]{:S(2)}) collective-permute-start(f32[8,3328]{1,0:T(8,128)S(1)} %get-tuple-element.5), channel_id=1, source_target_pairs={{0,16},{4,20},{8,24},{12,28},{16,0},{20,4},{24,8},{28,12},{1,17},{... | collective-permute-start | bytes 319496 | tf_op jit(solution)/shard_map/ppermute | solution.py:295
  107.8 5.8 %collective-permute-start.13 = (f32[8,3328]{1,0:T(8,128)S(1)}, f32[8,3328]{1,0:T(8,128)S(1)}, u32[]{:S(2)}, u32[]{:S(2)}) collective-permute-start(f32[8,3328]{1,0:T(8,128)S(1)} %get-tuple-element.5), channel_id=1, source_target_pairs={{0,24},{4,28},{8,16},{12,20},{16,8},{20,12},{24,0},{28,4},{1,25},{... | collective-permute-start | bytes 319496 | tf_op jit(solution)/shard_map/ppermute | solution.py:295
  113.7 1.8 %collective-permute-start.14 = (f32[32,3328]{1,0:T(8,128)S(1)}, f32[32,3328]{1,0:T(8,128)S(1)}, u32[]{:S(2)}, u32[]{:S(2)}) collective-permute-start(f32[32,3328]{1,0:T(8,128)S(1)} %bitcast.54), channel_id=1, source_target_pairs={{0,4},{4,0},{8,12},{12,8},{16,20},{20,16},{24,28},{28,24},{1,5},{5... | collective-permute-start | bytes 1277960 | tf_op jit(solution)/shard_map/ppermute | solution.py:298

commit v2 on v1

v2 whole, which is shorter than its diff:
```python
import functools
import math

import jax
import jax.numpy as jnp
from jax import lax
from jax.experimental import pallas as pl
from jax.experimental.pallas import tpu as pltpu
from jax.sharding import PartitionSpec as P

W = 256
FEAT = 1024
DILATIONS = (16, 64, 256)
BACK = DILATIONS[1] + DILATIONS[2]
HALO = BACK + sum(DILATIONS)
SCALE = 2.0 / FEAT
SUM_LANES = 9 * W + FEAT
GROUPS = ((0, 3 * W), (3 * W, 6 * W), (6 * W, 9 * W), (9 * W, SUM_LANES))
CODE_LANES = SUM_LANES + 128
BASE = 125.0 * math.log(2.0)
SPAN = 250.0 * math.log(2.0)


def dot(left, right):
    return lax.dot_general(
        left, right, (((1,), (0,)), ((), ())), preferred_element_type=jnp.float32
    )


def dot_nt(left, right):
    return lax.dot_general(
        left, right, (((1,), (1,)), ((), ())), preferred_element_type=jnp.float32
    )


def dot_tn(left, right):
    return lax.dot_general(
        left, right, (((0,), (0,)), ((), ())), preferred_element_type=jnp.float32
    )


def split(value):
    high = value.astype(jnp.bfloat16)
    return high, (value - high.astype(jnp.float32)).astype(jnp.bfloat16)


def tile_of(rows, most):
    best = 16
    for size in range(16, most + 1, 16):
        if rows % size == 0:
            best = size
    return best


def loop_rows(start, stop, most, body):
    tile = tile_of(stop - start, most)
    for frame in range(start, stop, tile):
        body(frame, tile)


def project_kernel(place_ref, target_ref, head_ref, out_ref, near_ref, far_ref):
    count = target_ref.shape[0]
    low, high = slice(0, BACK), slice(count - BACK, count)
    even = place_ref[0] % 2 == 0
    loop_rows(0, count, 512, functools.partial(project_rows, target_ref, head_ref, out_ref))

    @pl.when(even)
    def _():
        near_ref[...] = out_ref[high, :]
        far_ref[...] = out_ref[low, :]

    @pl.when(jnp.logical_not(even))
    def _():
        near_ref[...] = out_ref[low, :]
        far_ref[...] = out_ref[high, :]


def project_rows(target_ref, head_ref, out_ref, frame, size):
    out_ref[frame : frame + size, :] = dot_nt(target_ref[frame : frame + size, :], head_ref[...])


def project(place, target, head_weight):
    count = target.shape[0]
    return pl.pallas_call(
        project_kernel,
        in_specs=[smem(), whole(), whole()],
        out_specs=[whole()] * 3,
        out_shape=[jax.ShapeDtypeStruct((rows, W), jnp.float32) for rows in (count, BACK, BACK)],
        compiler_params=pltpu.CompilerParams(vmem_limit_bytes=24 * 2**20),
        cost_estimate=pl.CostEstimate(
            flops=2 * count * W * FEAT, bytes_accessed=count * (2 * FEAT + 4 * W), transcendentals=0
        ),
        name="project_targets",
    )(place, target, head_weight)


def main_kernel(
    count,
    place_ref,
    clip_ref,
    clip_a_ref,
    clip_b_ref,
    target_hbm,
    proj_ref,
    proj_a_ref,
    proj_b_ref,
    conv_hbm,
    head_hbm,
    keep_ref,
    send_ref,
    h0,
    h1,
    h2,
    h3,
    s1,
    s2,
    s3,
    err,
    back,
    conv_t,
    gram,
    head_acc,
    sums,
    conv_ref,
    head_ref,
    target_ref,
    in_sem,
    out_sem,
):
    first = place_ref[0] == 0
    last = place_ref[0] == place_ref[1] - 1
    even = place_ref[0] % 2 == 0
    hidden = (h0, h1, h2, h3)
    slopes = (None, s1, s2, s3)

    def at(frame, size):
        return slice(frame + HALO, frame + HALO + size)

    def inside(frame, size):
        rows = lax.broadcasted_iota(jnp.int32, (size, 1), 0) + frame
        return ((rows >= 0) | jnp.logical_not(first)) & ((rows < count) | jnp.logical_not(last))

    def masked(frame, size, value):
        if frame >= 0 and frame + size <= count:
            return value
        return jnp.where(inside(frame, size), value, 0.0)

    above = pl.multiple_of(jnp.where(even, HALO + count, 0), 16)
    below = pl.multiple_of(jnp.where(even, 0, HALO + count), 16)
    err_above = pl.multiple_of(jnp.where(even, HALO + count, HALO - BACK), 16)
    err_below = pl.multiple_of(jnp.where(even, HALO - BACK, HALO + count), 16)
    loads = [
        (conv_hbm.at[0], conv_ref.at[0]),
        (clip_ref, h0.at[HALO : HALO + count]),
        (clip_a_ref, h0.at[pl.ds(above, HALO)]),
        (clip_b_ref, h0.at[pl.ds(below, HALO)]),
        (conv_hbm.at[1:3], conv_ref.at[1:3]),
        (head_hbm, head_ref),
        (proj_ref, err.at[HALO : HALO + count]),
        (proj_a_ref, err.at[pl.ds(err_above, BACK)]),
        (proj_b_ref, err.at[pl.ds(err_below, BACK)]),
        (target_hbm, target_ref),
    ]
    loads = [pltpu.make_async_copy(*load, in_sem.at[i]) for i, load in enumerate(loads)]
    for load in loads:
        load.start()

    half = keep_ref.shape[1]
    stores = []

    def store(first_lane, lanes):
        for pen in range(keep_ref.shape[0]):
            for side, target in enumerate((keep_ref, send_ref)):
                start = pl.multiple_of((2 * pen + (place_ref[0] + side) % 2) * half, 8)
                copy = pltpu.make_async_copy(
                    sums.at[pl.ds(start, half), first_lane : first_lane + lanes],
                    target.at[pen, :, first_lane : first_lane + lanes],
                    out_sem.at[len(stores)],
                )
                copy.start()
                stores.append(copy)

    for load in loads[:4]:
        load.wait()
    reach = HALO
    for layer in range(3):
        width = DILATIONS[layer]
        reach -= width
        source, result, slope = hidden[layer], hidden[layer + 1], slopes[layer + 1]
        weights = conv_ref[layer].reshape(3 * W, W)

        def forward(frame, size):
            taps = [source[at(frame + (k - 1) * width, size), :] for k in range(3)]
            pre = dot(jnp.concatenate(taps, axis=1), weights)
            sig = 0.5 * jnp.tanh(0.5 * pre) + 0.5
            new = taps[1].astype(jnp.float32) + pre * sig
            result[at(frame, size), :] = masked(frame, size, new).astype(jnp.bfloat16)
            slope[at(frame, size), :] = sig * (1.0 + pre * (1.0 - sig))

        loop_rows(-reach, count + reach, 416, forward)
        if layer == 0:
            loads[4].wait()
            for turn in (1, 2):
                for k in range(3):
                    turned = jnp.transpose(conv_ref[turn, k])
                    conv_t[turn - 1, 2 * k * W : (2 * k + 1) * W, :] = turned
                    conv_t[turn - 1, (2 * k + 1) * W : (2 * k + 2) * W, :] = turned

    def store_back(frame, size, error, slope):
        high, low = split(error * slope[at(frame, size), :])
        back[at(frame, size), 0:W] = high
        back[at(frame, size), W : 2 * W] = low

    def head_error(frame, size):
        top = h3[at(frame, size), :]
        error = SCALE * (dot(jnp.concatenate([top, top], axis=1), gram[...]) - err[at(frame, size), :])
        err[at(frame, size), :] = error
        store_back(frame, size, error, s3)

    for load in loads[5:9]:
        load.wait()
    high, low = split(dot_nt(head_ref[...], head_ref[...]))
    gram[0:W, :] = high
    gram[W : 2 * W, :] = low
    loop_rows(-BACK, count + BACK, 416, head_error)

    loads[9].wait()
    top = h3[at(0, count), :]
    head_acc[...] = dot_tn(top, target_ref[...])
    square = dot_tn(top, top)
    high = square.astype(jnp.bfloat16)
    middle, low = split(square - high.astype(jnp.float32))
    weight = head_ref[...]
    product = dot(high, weight) + (dot(middle, weight) + dot(low, weight))
    sums[:, 9 * W :] = SCALE * (product - head_acc[...])
    store(9 * W, FEAT)

    reach = BACK
    for layer in (2, 1, 0):
        width = DILATIONS[layer]
        source = hidden[layer]
        first_lane = 3 * layer * W
        right = back[at(0, count), :]
        for k in range(3):
            both = dot_tn(source[at((k - 1) * width, count), :], right)
            sums[:, first_lane + k * W : first_lane + (k + 1) * W] = both[:, 0:W] + both[:, W:]
        store(first_lane, 3 * W)
        if layer > 0:
            reach -= width

            def pull_back(frame, size):
                taps = [back[at(frame - (k - 1) * width, size), :] for k in range(3)]
                err[at(frame, size), :] += dot(jnp.concatenate(taps, axis=1), conv_t[layer - 1])

            loop_rows(-reach, count + reach, 416, pull_back)

            def slope_back(frame, size):
                error = masked(frame, size, err[at(frame, size), :])
                store_back(frame, size, error, slopes[layer])

            loop_rows(-reach, count + reach, 416, slope_back)
    for copy in stores:
        copy.wait()


def main(pens, place, clip, clip_a, clip_b, target, proj, proj_a, proj_b, conv_weight, head_weight):
    count = clip.shape[0]
    rows = count + 2 * HALO
    flops = 2 * W * W * (9 * rows + 14 * rows + 18 * count + 6 * count)
    return pl.pallas_call(
        functools.partial(main_kernel, count),
        in_specs=[smem()] + [pl.BlockSpec(memory_space=pl.ANY)] * 9,
        out_specs=[pl.BlockSpec(memory_space=pl.ANY)] * 2,
        out_shape=[jax.ShapeDtypeStruct((pens, W // (2 * pens), SUM_LANES), jnp.float32)] * 2,
        scratch_shapes=[pltpu.VMEM((rows, W), jnp.bfloat16)] * 4
        + [pltpu.VMEM((rows, W), jnp.float32)] * 4
        + [
            pltpu.VMEM((rows, 2 * W), jnp.bfloat16),
            pltpu.VMEM((2, 6 * W, W), jnp.bfloat16),
            pltpu.VMEM((2 * W, W), jnp.bfloat16),
            pltpu.VMEM((W, FEAT), jnp.float32),
            pltpu.VMEM((W, SUM_LANES), jnp.float32),
            pltpu.VMEM(conv_weight.shape, jnp.bfloat16),
            pltpu.VMEM(head_weight.shape, jnp.bfloat16),
            pltpu.VMEM(target.shape, jnp.bfloat16),
            pltpu.SemaphoreType.DMA((10,)),
            pltpu.SemaphoreType.DMA((8 * pens,)),
        ],
        compiler_params=pltpu.CompilerParams(vmem_limit_bytes=56 * 2**20),
        cost_estimate=pl.CostEstimate(flops=flops, bytes_accessed=16 * 2**20, transcendentals=3 * rows * W),
        name="forward_backward",
    )(place, clip, clip_a, clip_b, target, proj, proj_a, proj_b, conv_weight, head_weight)


def swap(near, far):
    count = lax.axis_size("tm")
    pairs = [(i, i + 1) for i in range(1, count - 1, 2)]
    from_far = lax.ppermute(far, "tm", pairs + [(j, i) for i, j in pairs])
    return lax.ppermute(near, "tm", [(i, i ^ 1) for i in range(count)]), from_far


def encode(values, code_ref):
    pens = len(values)
    for place, (first, stop) in enumerate(GROUPS):
        lanes = range(first, stop, 128)
        most = functools.reduce(
            jnp.maximum, [jnp.abs(values[pen][:, lane : lane + 128]) for pen in range(pens) for lane in lanes]
        )
        most = (most * 1.0079).astype(jnp.bfloat16)
        code_ref[place, :, SUM_LANES:] = most
        most = most.astype(jnp.float32)
        grow = jnp.where(most > 1e-36, SPAN / jnp.maximum(most, 1e-36), 0.0)
        for pen in range(pens):
            for lane in lanes:
                part = values[pen][:, lane : lane + 128]
                code = jnp.exp(jnp.abs(part) * grow - BASE)
                code = jnp.where(part < 0.0, -code, code)
                code_ref[pen, :, lane : lane + 128] = code.astype(jnp.bfloat16)
    for pen in range(len(GROUPS), pens):
        code_ref[pen, :, SUM_LANES:] = jnp.zeros_like(code_ref[pen, :, SUM_LANES:])


def decode(code_ref, pen, lane, place):
    code = code_ref[pen, :, lane : lane + 128].astype(jnp.float32)
    most = code_ref[place, :, SUM_LANES:].astype(jnp.float32) * (1.0 / SPAN)
    size = (jnp.log(jnp.abs(code)) + BASE) * most
    return jnp.where(code < 0.0, -size, size)


def cores_kernel(place_ref, keep_ref, other_ref, own_ref, *sent):
    groups, pens, rows = len(sent) + 1, own_ref.shape[0], own_ref.shape[1]
    group = place_ref[0] // 2

    def rows_of(index, pen):
        if rows % 8 == 0:
            here = pl.ds(pl.multiple_of(index * rows, 8), rows)
            return keep_ref[pen, here, :] + other_ref[pen, here, :]
        total = keep_ref[pen] + other_ref[pen]
        return functools.reduce(
            lambda a, b: a + b,
            [jnp.where(index == i, total[i * rows : (i + 1) * rows], 0.0) for i in range(groups)],
        )

    for pen in range(pens):
        own_ref[pen] = rows_of(group, pen)
    for j in range(1, groups):
        encode([rows_of(group ^ j, pen) for pen in range(pens)], sent[j - 1])


def chips_kernel(place_ref, own_ref, *refs):
    pens = own_ref.shape[0]
    arrived, mine_ref, sent = refs[:-2], refs[-2], refs[-1]
    for place, (first, stop) in enumerate(GROUPS):
        for lane in range(first, stop, 128):
            for pen in range(pens):
                total = own_ref[pen, :, lane : lane + 128]
                for other in arrived:
                    total = total + decode(other, pen, lane, place)
                sent[pen, :, lane : lane + 128] = total
    mine_ref[...] = sent[place_ref[2]]


def smem():
    return pl.BlockSpec(memory_space=pltpu.SMEM)


def whole():
    return pl.BlockSpec(memory_space=pltpu.VMEM)


def sum_cores(place, keep, other, groups):
    pens, half, lanes = keep.shape
    rows = half // groups
    return pl.pallas_call(
        cores_kernel,
        in_specs=[smem()] + [whole()] * 2,
        out_specs=[whole()] * groups,
        out_shape=[jax.ShapeDtypeStruct((pens, rows, lanes), jnp.float32)]
        + [jax.ShapeDtypeStruct((pens, rows, CODE_LANES), jnp.bfloat16)] * (groups - 1),
        name="sum_cores",
    )(place, keep, other)


def sum_chips(place, own, arrived):
    pens, rows, lanes = own.shape
    def kernel(place_ref, *refs):
        ins, outs, total = refs[: 1 + len(arrived)], refs[1 + len(arrived) : -1], refs[-1]
        chips_kernel(place_ref, *ins, outs[0], total)
        for j in range(1, pens):
            outs[j][...] = total[place_ref[2] ^ j]

    return pl.pallas_call(
        kernel,
        in_specs=[smem()] + [whole()] * (1 + len(arrived)),
        out_specs=[whole()] * pens,
        out_shape=[jax.ShapeDtypeStruct((rows, lanes), jnp.float32)] * pens,
        scratch_shapes=[pltpu.VMEM((pens, rows, lanes), jnp.float32)],
        name="sum_chips",
    )(place, own, *arrived)


def reduce_sums(place, keep, send):
    n, pens = lax.axis_size("tm"), lax.axis_size("pen")
    groups = n // 2
    sibling = [(i, i ^ 1) for i in range(n)]
    chips = [[(i, i ^ (2 * j)) for i in range(n)] for j in range(1, groups)]
    streams = [[(i, i ^ j) for i in range(pens)] for j in range(1, pens)]
    other = lax.ppermute(send, "tm", sibling)
    own, *codes = sum_cores(place, keep, other, groups)
    arrived = [lax.ppermute(code, "tm", pairs) for code, pairs in zip(codes, chips)]
    mine, *parts = sum_chips(place, own, arrived)
    for part, pairs in zip(parts, streams):
        mine = mine + lax.ppermute(part, "pen", pairs)
    core, group = place[0] % 2, place[0] // 2
    half = jnp.zeros((groups,) + mine.shape, mine.dtype)
    half = lax.dynamic_update_index_in_dim(half, mine, group, 0)
    for j, pairs in enumerate(chips, 1):
        half = lax.dynamic_update_index_in_dim(half, lax.ppermute(mine, "tm", pairs), group ^ j, 0)
    half = half.reshape(-1, half.shape[2])
    other = lax.ppermute(half, "tm", sibling)
    rows = jnp.concatenate([jnp.where(core == 0, half, other), jnp.where(core == 0, other, half)], axis=0)
    return rows[:, : 9 * W].reshape(-1, 3, 3, W).transpose(1, 2, 0, 3), rows[:, 9 * W :]


def on_device(clips, targets, conv_weight, head_weight):
    clip, target = clips[0], targets[0]
    count, pens = lax.axis_size("tm"), lax.axis_size("pen")
    place = jnp.stack([lax.axis_index("tm"), count, lax.axis_index("pen"), pens]).astype(jnp.int32)
    even = place[0] % 2 == 0
    low, high = clip[:HALO], clip[clip.shape[0] - HALO :]
    clip_a, clip_b = swap(jnp.where(even, high, low), jnp.where(even, low, high))
    proj, near, far = project(place, target, head_weight)
    proj_a, proj_b = swap(near, far)
    keep, send = main(
        pens, place, clip, clip_a, clip_b, target, proj, proj_a, proj_b, conv_weight, head_weight
    )
    return reduce_sums(place, keep, send)


def solution(mesh):
    in_specs = (P("pen", "tm", None), P("pen", "tm", None), P(), P())
    out_specs = (P(None, None, "pen", None), P("pen", None))
    return jax.shard_map(
        on_device, mesh=mesh, in_specs=in_specs, out_specs=out_specs, check_vma=False
    )
```

time: 118 us -> 97.5 us (0.83)
  Pallas kernels: 41.6 us -> 29.6 us
  waiting for transfers between devices: 36 us -> 28.2 us
  other arithmetic: 6.45 us -> 3.01 us
  local copies, waits for them, and re-layouts: 4.78 us -> 7.77 us
    pallas_call x2 -> x4, Pallas kernels: 41.6 us -> 29.6 us  [the longest x1 22 us: main(): pl.pallas_call(functools.partial(main_kernel, count), in_specs=[smem()] +...]
    ppermute x15, waiting for transfers between devices: 36 us -> 28.2 us  [the longest x3 10.4 us: reduce_sums(): lax.ppermute(code, 'tm', pairs)]
    unnamed x9 -> x25, local copies, waits for them, and re-layouts: 1.93 us -> 7.39 us
    add x2 -> x0, other arithmetic: 2.71 us -> none  [the longest x1 1.63 us: reduce_rows(): part = pick(part, core, 1) + other]
    squeeze x3 -> x0, local copies, waits for them, and re-layouts: 2.47 us -> none  [pick(): return lax.dynamic_index_in_dim(array, index, axis, keepdims=False)]
  transfers between devices with their start and end apart: 15 -> 15, of which waited for: 10 -> 11; matrix products, arithmetic and copies ran while one was open for 2% -> 0% of each run, Pallas kernels for 4% -> 2%
where the time goes in v2:
time: 97.5 us; the launch traced here: 97.2 us
  Pallas kernels  29.6 us (30%)
  waiting for transfers between devices  28.2 us (29%)
  starting transfers between devices  27.8 us (29%)
  local copies, waits for them, and re-layouts  7.77 us (8%)
  other arithmetic  3.01 us (3%)
    pallas_call x1, Pallas kernels, main(): pl.pallas_call(functools.partial(main_kernel, count), in_specs=[smem()] +...  22 us
    ppermute x3, waiting for transfers between devices, reduce_sums(): lax.ppermute(code, 'tm', pairs)  10.4 us
    ppermute x1, starting transfers between devices, reduce_sums(): other = lax.ppermute(send, 'tm', sibling)  9.87 us
    ppermute x3, waiting for transfers between devices, reduce_sums(): mine = mine + lax.ppermute(part, 'pen', pairs)  7.87 us
    unnamed x25, local copies, waits for them, and re-layouts  7.39 us
    ppermute x3, starting transfers between devices, reduce_sums(): mine = mine + lax.ppermute(part, 'pen', pairs)  4.39 us
    ppermute x2, starting transfers between devices, swap(): lax.ppermute(near, 'tm', [(i, i ^ 1) for i in range(count)])  4.37 us
    ppermute x3, starting transfers between devices, reduce_sums(): lax.ppermute(code, 'tm', pairs)  4.22 us
  transfers between devices with their start and end apart: 15, of which 11 were waited for; matrix products, arithmetic and copies ran while one was open for 0% of the time, Pallas kernels for 2%

profile of v2, /device:TPU:0, one launch (start us, length us, event | category | flops | bytes accessed | tf_op | source)
XLA Modules:
  0.0 97.2 jit_solution(15069257839972871240)
XLA Ops:
  0.6 0.0 copy-start.1
  0.7 1.2 %select_bitcast_fusion = (bf16[656,256]{1,0:T(8,128)(2,1)S(1)}, bf16[656,256]{1,0:T(8,128)(2,1)S(1)}) fusion(pred[]{:T(512)S(6)} %eq.8, bf16[1,2048,256]{2,1,0:T(8,128)(2,1)} %param.4), kind=kLoop, calls=%fused_computation.3 | loop fusion | flops 335872 | bytes 1343489 | tf_op jit(solution)/shard_map/jit(_where)/select_n | solution.py:431
  1.8 0.5 collective-permute-start
  2.4 0.7 collective-permute-start.1
  3.0 0.1 pad_add_fusion.place_ref
  3.1 2.2 %copy-done = bf16[1,2048,1024]{2,1,0:T(8,128)(2,1)S(1)} copy-done((bf16[1,2048,1024]{2,1,0:T(8,128)(2,1)S(1)}, bf16[1,2048,1024]{2,1,0:T(8,128)(2,1)}, u32[]{:S(2)}) %copy-start) | copy-done | bytes 4194328
  5.3 1.9 %project_targets.1 = (f32[2048,256]{1,0:T(8,128)S(1)}, f32[320,256]{1,0:T(8,128)S(1)}, f32[320,256]{1,0:T(8,128)S(1)}) custom-call(s32[4]{0:T(128)S(1)} %pad_add_fusion.place_ref, bf16[2048,1024]{1,0:T(8,128)(2,1)S(1)} %bitcast.21, bf16[256,1024]{1,0:T(8,128)(2,1)S(1)} %copy-done.1), custom_call_target="tpu_custom_call" | custom-call | flops 1073741824 | bytes 6291456 | tf_op jit(solution)/shard_map/project_targets/pallas_call | solution.py:84
  7.2 1.3 %copy-done.3 = f32[2048,256]{1,0:T(8,128)} copy-done((f32[2048,256]{1,0:T(8,128)}, f32[2048,256]{1,0:T(8,128)S(1)}, u32[]{:S(2)}) %copy-start.3) | copy-done | bytes 2097176
  8.6 3.9 %collective-permute-start.2 = (f32[320,256]{1,0:T(8,128)S(1)}, f32[320,256]{1,0:T(8,128)S(1)}, u32[]{:S(2)}, u32[]{:S(2)}) collective-permute-start(f32[320,256]{1,0:T(8,128)S(1)} %get-tuple-element.16), channel_id=1, source_target_pairs={{0,4},{4,0},{8,12},{12,8},{16,20},{20,16},{24,28},{28,24},{1,5},{5... | collective-permute-start | bytes 983048 | tf_op jit(solution)/shard_map/ppermute | solution.py:299
  12.4 0.7 collective-permute-start.3
  13.1 0.6 collective-permute-done.2.proj_a_ref
  13.7 0.0 collective-permute-done.3.proj_b_ref
  13.7 0.0 copy-start.8
  13.7 0.7 copy-done.10
  14.4 0.1 copy-done.11
  14.5 0.1 copy-done.8
  14.6 0.1 copy-done.9
  14.7 22.0 %forward_backward.1 = (f32[4,32,3328]{2,1,0:T(8,128)}, f32[4,32,3328]{2,1,0:T(8,128)}) custom-call(s32[4]{0:T(128)} %copy-done.2, bf16[2048,256]{1,0:T(8,128)(2,1)} %bitcast.24, bf16[656,256]{1,0:T(8,128)(2,1)} %copy-done.8, bf16[656,256]{1,0:T(8,128)(2,1)} %copy-done.9, bf16[2048,1024]{1,0:T(8,128)(2,1)} %bitcast.20, f32[2048,256]{1,0:T(8,128)} %copy-done.3, ...), custom_call_target="tpu_custom_call" | custom-call | flops 16571695104 | bytes 16777216 | tf_op jit(solution)/shard_map/forward_backward/pallas_call | solution.py:270
  36.8 9.9 %collective-permute-start.4 = (f32[4,32,3328]{2,1,0:T(8,128)}, f32[4,32,3328]{2,1,0:T(8,128)S(1)}, u32[]{:S(2)}, u32[]{:S(2)}) collective-permute-start(f32[4,32,3328]{2,1,0:T(8,128)} %get-tuple-element.19), channel_id=1, source_target_pairs={{0,4},{4,0},{8,12},{12,8},{16,20},{20,16},{24,28},{28,24},{1,5},{5... | collective-permute-start | bytes 5111816 | tf_op jit(solution)/shard_map/ppermute | solution.py:408
  46.6 3.4 %collective-permute-done.4.other_ref = f32[4,32,3328]{2,1,0:T(8,128)S(1)} collective-permute-done((f32[4,32,3328]{2,1,0:T(8,128)}, f32[4,32,3328]{2,1,0:T(8,128)S(1)}, u32[]{:S(2)}, u32[]{:S(2)}) %collective-permute-start.4) | collective-permute-done | bytes 1703968 | tf_op jit(solution)/shard_map/ppermute | solution.py:408
  50.1 1.2 %copy-done.4 = f32[4,32,3328]{2,1,0:T(8,128)} copy-done((f32[4,32,3328]{2,1,0:T(8,128)}, f32[4,32,3328]{2,1,0:T(8,128)S(1)}, u32[]{:S(2)}) %copy-start.4) | copy-done | bytes 1703960
  51.3 3.3 %sum_cores.1 = (f32[4,8,3328]{2,1,0:T(8,128)}, bf16[4,8,3456]{2,1,0:T(8,128)(2,1)}, bf16[4,8,3456]{2,1,0:T(8,128)(2,1)}, bf16[4,8,3456]{2,1,0:T(8,128)(2,1)}) custom-call(s32[4]{0:T(128)} %copy-done.2, f32[4,32,3328]{2,1,0:T(8,128)} %get-tuple-element.18.keep_ref, f32[4,32,3328]{2,1,0:T(8,128)} %copy-done.4), custom_call_target="tpu_custom_call" | custom-call | tf_op jit(solution)/shard_map/sum_cores/pallas_call | solution.py:374
  54.6 2.0 %collective-permute-start.5 = (bf16[4,8,3456]{2,1,0:T(8,128)(2,1)}, bf16[4,8,3456]{2,1,0:T(8,128)(2,1)S(1)}, u32[]{:S(2)}, u32[]{:S(2)}) collective-permute-start(bf16[4,8,3456]{2,1,0:T(8,128)(2,1)} %get-tuple-element.21), channel_id=1, source_target_pairs={{0,8},{4,12},{8,0},{12,4},{16,24},{20,28},{24,16},{28,20},{1,9},{5... | collective-permute-start | bytes 663560 | tf_op jit(solution)/shard_map/ppermute | solution.py:410
  56.6 0.7 collective-permute-start.6
  57.3 1.5 %collective-permute-start.7 = (bf16[4,8,3456]{2,1,0:T(8,128)(2,1)}, bf16[4,8,3456]{2,1,0:T(8,128)(2,1)S(1)}, u32[]{:S(2)}, u32[]{:S(2)}) collective-permute-start(bf16[4,8,3456]{2,1,0:T(8,128)(2,1)} %get-tuple-element.23), channel_id=1, source_target_pairs={{0,24},{4,28},{8,16},{12,20},{16,8},{20,12},{24,0},{28,4},{1,25},{... | collective-permute-start | bytes 663560 | tf_op jit(solution)/shard_map/ppermute | solution.py:410
  58.8 4.3 %collective-permute-done.5.refs_1_ = bf16[4,8,3456]{2,1,0:T(8,128)(2,1)S(1)} collective-permute-done((bf16[4,8,3456]{2,1,0:T(8,128)(2,1)}, bf16[4,8,3456]{2,1,0:T(8,128)(2,1)S(1)}, u32[]{:S(2)}, u32[]{:S(2)}) %collective-permute-start.5) | collective-permute-done | bytes 221216 | tf_op jit(solution)/shard_map/ppermute | solution.py:410
  63.1 4.3 %collective-permute-done.6.refs_2_ = bf16[4,8,3456]{2,1,0:T(8,128)(2,1)S(1)} collective-permute-done((bf16[4,8,3456]{2,1,0:T(8,128)(2,1)}, bf16[4,8,3456]{2,1,0:T(8,128)(2,1)S(1)}, u32[]{:S(2)}, u32[]{:S(2)}) %collective-permute-start.6) | collective-permute-done | bytes 221216 | tf_op jit(solution)/shard_map/ppermute | solution.py:410
  67.4 1.8 %collective-permute-done.7.refs_3_ = bf16[4,8,3456]{2,1,0:T(8,128)(2,1)S(1)} collective-permute-done((bf16[4,8,3456]{2,1,0:T(8,128)(2,1)}, bf16[4,8,3456]{2,1,0:T(8,128)(2,1)S(1)}, u32[]{:S(2)}, u32[]{:S(2)}) %collective-permute-start.7) | collective-permute-done | bytes 221216 | tf_op jit(solution)/shard_map/ppermute | solution.py:410
  69.2 0.7 copy-done.7
  69.9 2.5 %sum_chips.1 = (f32[8,3328]{1,0:T(8,128)}, f32[8,3328]{1,0:T(8,128)}, f32[8,3328]{1,0:T(8,128)}, f32[8,3328]{1,0:T(8,128)}) custom-call(s32[4]{0:T(128)} %copy-done.2, f32[4,8,3328]{2,1,0:T(8,128)} %get-tuple-element.20.refs_0_, bf16[4,8,3456]{2,1,0:T(8,128)(2,1)} %copy-done.5, bf16[4,8,3456]{2,1,0:T(8,128)(2,1)} %copy-done.6, bf16[4,8,3456]{2,1,0:T(8,128)(2,1)} %copy-done.7), custom_call_target="tpu_custom_call" | custom-call | tf_op jit(solution)/shard_map/sum_chips/pallas_call | solution.py:392
  72.3 3.6 %collective-permute-start.10 = (f32[8,3328]{1,0:T(8,128)}, f32[8,3328]{1,0:T(8,128)S(1)}, u32[]{:S(2)}, u32[]{:S(2)}) collective-permute-start(f32[8,3328]{1,0:T(8,128)} %get-tuple-element.27), channel_id=1, source_target_pairs={{0,3},{1,2},{2,1},{3,0},{4,7},{5,6},{6,5},{7,4},{8,11},{9,10},{10,... | collective-permute-start | bytes 319496 | tf_op jit(solution)/shard_map/ppermute | solution.py:413
  75.9 0.8 collective-permute-start.9
  76.7 3.1 %collective-permute-done.10 = f32[8,3328]{1,0:T(8,128)S(1)} collective-permute-done((f32[8,3328]{1,0:T(8,128)}, f32[8,3328]{1,0:T(8,128)S(1)}, u32[]{:S(2)}, u32[]{:S(2)}) %collective-permute-start.10) | collective-permute-done | bytes 106528 | tf_op jit(solution)/shard_map/ppermute | solution.py:413
  79.8 2.3 %collective-permute-done.8 = f32[8,3328]{1,0:T(8,128)S(1)} collective-permute-done((f32[8,3328]{1,0:T(8,128)}, f32[8,3328]{1,0:T(8,128)S(1)}, u32[]{:S(2)}, u32[]{:S(2)}) %collective-permute-start.8) | collective-permute-done | bytes 106528 | tf_op jit(solution)/shard_map/ppermute | solution.py:413
  82.1 2.5 %collective-permute-done.9 = f32[8,3328]{1,0:T(8,128)S(1)} collective-permute-done((f32[8,3328]{1,0:T(8,128)}, f32[8,3328]{1,0:T(8,128)S(1)}, u32[]{:S(2)}, u32[]{:S(2)}) %collective-permute-start.9) | collective-permute-done | bytes 106528 | tf_op jit(solution)/shard_map/ppermute | solution.py:413
  84.6 0.9 bitcast_dynamic-update-slice_fusion.3
  85.5 0.7 collective-permute-start.11
  86.3 1.2 %collective-permute-start.12 = (f32[8,3328]{1,0:T(8,128)S(1)}, f32[8,3328]{1,0:T(8,128)S(1)}, u32[]{:S(2)}, u32[]{:S(2)}) collective-permute-start(f32[8,3328]{1,0:T(8,128)S(1)} %get-tuple-element.31), channel_id=1, source_target_pairs={{0,16},{4,20},{8,24},{12,28},{16,0},{20,4},{24,8},{28,12},{1,17},{... | collective-permute-start | bytes 319496 | tf_op jit(solution)/shard_map/ppermute | solution.py:418
  87.4 1.7 %collective-permute-start.13 = (f32[8,3328]{1,0:T(8,128)S(1)}, f32[8,3328]{1,0:T(8,128)S(1)}, u32[]{:S(2)}, u32[]{:S(2)}) collective-permute-start(f32[8,3328]{1,0:T(8,128)S(1)} %get-tuple-element.31), channel_id=1, source_target_pairs={{0,24},{4,28},{8,16},{12,20},{16,8},{20,12},{24,0},{28,4},{1,25},{... | collective-permute-start | bytes 319496 | tf_op jit(solution)/shard_map/ppermute | solution.py:418
  89.1 2.2 %collective-permute-done.11 = f32[8,3328]{1,0:T(8,128)S(1)} collective-permute-done((f32[8,3328]{1,0:T(8,128)S(1)}, f32[8,3328]{1,0:T(8,128)S(1)}, u32[]{:S(2)}, u32[]{:S(2)}) %collective-permute-start.11) | collective-permute-done | bytes 106528 | tf_op jit(solution)/shard_map/ppermute | solution.py:418
  91.3 2.0 %collective-permute-done.12 = f32[8,3328]{1,0:T(8,128)S(1)} collective-permute-done((f32[8,3328]{1,0:T(8,128)S(1)}, f32[8,3328]{1,0:T(8,128)S(1)}, u32[]{:S(2)}, u32[]{:S(2)}) %collective-permute-start.12) | collective-permute-done | bytes 106528 | tf_op jit(solution)/shard_map/ppermute | solution.py:418
  93.3 0.0 collective-permute-done.13
  93.3 0.1 collective-permute-start.14
  93.4 1.8 %collective-permute-done.14 = f32[32,3328]{1,0:T(8,128)S(1)} collective-permute-done((f32[32,3328]{1,0:T(8,128)S(1)}, f32[32,3328]{1,0:T(8,128)S(1)}, u32[]{:S(2)}, u32[]{:S(2)}) %collective-permute-start.14) | collective-permute-done | bytes 426016 | tf_op jit(solution)/shard_map/ppermute | solution.py:420
  95.1 0.1 broadcast_select_fusion
  95.2 0.7 pad_maximum_fusion
  96.0 0.3 reshape.17
  96.3 0.9 copy.7
  (22 shorter events, 0.1 us)
Async XLA Ops:
  0.6 2.5 %copy-start.1 = (bf16[256,1024]{1,0:T(8,128)(2,1)S(1)}, bf16[256,1024]{1,0:T(8,128)(2,1)}, u32[]{:S(2)}) copy-start(bf16[256,1024]{1,0:T(8,128)(2,1)} %head_hbm.1) | copy-start | bytes 1572868
  1.8 11.9 %collective-permute-start = (bf16[656,256]{1,0:T(8,128)(2,1)S(1)}, bf16[656,256]{1,0:T(8,128)(2,1)S(1)}, u32[]{:S(2)}, u32[]{:S(2)}) collective-permute-start(bf16[656,256]{1,0:T(8,128)(2,1)S(1)} %get-tuple-element.33), channel_id=1, source_target_pairs={{0,4},{4,0},{8,12},{12,8},{16,20},{20,16},{24,28},{28,24},{1,5},{5... | collective-permute-start | bytes 1007624 | tf_op jit(solution)/shard_map/ppermute | solution.py:299
  2.4 11.4 %collective-permute-start.1 = (bf16[656,256]{1,0:T(8,128)(2,1)S(1)}, bf16[656,256]{1,0:T(8,128)(2,1)S(1)}, u32[]{:S(2)}, u32[]{:S(2)}) collective-permute-start(bf16[656,256]{1,0:T(8,128)(2,1)S(1)} %get-tuple-element.32), channel_id=1, source_target_pairs={{4,8},{12,16},{20,24},{8,4},{16,12},{24,20},{5,9},{13,17},{21,25},... | collective-permute-start | bytes 1007624 | tf_op jit(solution)/shard_map/ppermute | solution.py:298
  3.1 4.1 %copy-start.2 = (s32[4]{0:T(128)}, s32[4]{0:T(128)S(1)}, u32[]{:S(2)}) copy-start(s32[4]{0:T(128)S(1)} %pad_add_fusion.place_ref) | copy-start | bytes 52
  3.1 2.2 %copy-start = (bf16[1,2048,1024]{2,1,0:T(8,128)(2,1)S(1)}, bf16[1,2048,1024]{2,1,0:T(8,128)(2,1)}, u32[]{:S(2)}) copy-start(bf16[1,2048,1024]{2,1,0:T(8,128)(2,1)} %param.5) | copy-start | bytes 12582916
  7.2 1.4 %copy-start.3 = (f32[2048,256]{1,0:T(8,128)}, f32[2048,256]{1,0:T(8,128)S(1)}, u32[]{:S(2)}) copy-start(f32[2048,256]{1,0:T(8,128)S(1)} %get-tuple-element.15.proj_ref) | copy-start | bytes 6291460
  8.6 5.1 %collective-permute-start.2 = (f32[320,256]{1,0:T(8,128)S(1)}, f32[320,256]{1,0:T(8,128)S(1)}, u32[]{:S(2)}, u32[]{:S(2)}) collective-permute-start(f32[320,256]{1,0:T(8,128)S(1)} %get-tuple-element.16), channel_id=1, source_target_pairs={{0,4},{4,0},{8,12},{12,8},{16,20},{20,16},{24,28},{28,24},{1,5},{5... | collective-permute-start | bytes 983048 | tf_op jit(solution)/shard_map/ppermute | solution.py:299
  12.4 1.3 %collective-permute-start.3 = (f32[320,256]{1,0:T(8,128)S(1)}, f32[320,256]{1,0:T(8,128)S(1)}, u32[]{:S(2)}, u32[]{:S(2)}) collective-permute-start(f32[320,256]{1,0:T(8,128)S(1)} %get-tuple-element.17), channel_id=1, source_target_pairs={{4,8},{12,16},{20,24},{8,4},{16,12},{24,20},{5,9},{13,17},{21,25},... | collective-permute-start | bytes 983048 | tf_op jit(solution)/shard_map/ppermute | solution.py:298
  13.7 0.7 copy-start.10
  13.7 0.8 copy-start.11
  13.7 0.9 copy-start.8
  13.7 1.0 %copy-start.9 = (bf16[656,256]{1,0:T(8,128)(2,1)}, bf16[656,256]{1,0:T(8,128)(2,1)S(1)}, u32[]{:S(2)}) copy-start(bf16[656,256]{1,0:T(8,128)(2,1)S(1)} %collective-permute-done.1.clip_b_ref) | copy-start | bytes 1007620
  36.8 13.3 %collective-permute-start.4 = (f32[4,32,3328]{2,1,0:T(8,128)}, f32[4,32,3328]{2,1,0:T(8,128)S(1)}, u32[]{:S(2)}, u32[]{:S(2)}) collective-permute-start(f32[4,32,3328]{2,1,0:T(8,128)} %get-tuple-element.19), channel_id=1, source_target_pairs={{0,4},{4,0},{8,12},{12,8},{16,20},{20,16},{24,28},{28,24},{1,5},{5... | collective-permute-start | bytes 5111816 | tf_op jit(solution)/shard_map/ppermute | solution.py:408
  50.1 1.2 %copy-start.4 = (f32[4,32,3328]{2,1,0:T(8,128)}, f32[4,32,3328]{2,1,0:T(8,128)S(1)}, u32[]{:S(2)}) copy-start(f32[4,32,3328]{2,1,0:T(8,128)S(1)} %collective-permute-done.4.other_ref) | copy-start | bytes 5111812
  54.6 8.5 %collective-permute-start.5 = (bf16[4,8,3456]{2,1,0:T(8,128)(2,1)}, bf16[4,8,3456]{2,1,0:T(8,128)(2,1)S(1)}, u32[]{:S(2)}, u32[]{:S(2)}) collective-permute-start(bf16[4,8,3456]{2,1,0:T(8,128)(2,1)} %get-tuple-element.21), channel_id=1, source_target_pairs={{0,8},{4,12},{8,0},{12,4},{16,24},{20,28},{24,16},{28,20},{1,9},{5... | collective-permute-start | bytes 663560 | tf_op jit(solution)/shard_map/ppermute | solution.py:410
  56.6 10.8 %collective-permute-start.6 = (bf16[4,8,3456]{2,1,0:T(8,128)(2,1)}, bf16[4,8,3456]{2,1,0:T(8,128)(2,1)S(1)}, u32[]{:S(2)}, u32[]{:S(2)}) collective-permute-start(bf16[4,8,3456]{2,1,0:T(8,128)(2,1)} %get-tuple-element.22), channel_id=1, source_target_pairs={{0,16},{4,20},{8,24},{12,28},{16,0},{20,4},{24,8},{28,12},{1,17},{... | collective-permute-start | bytes 663560 | tf_op jit(solution)/shard_map/ppermute | solution.py:410
  57.3 11.9 %collective-permute-start.7 = (bf16[4,8,3456]{2,1,0:T(8,128)(2,1)}, bf16[4,8,3456]{2,1,0:T(8,128)(2,1)S(1)}, u32[]{:S(2)}, u32[]{:S(2)}) collective-permute-start(bf16[4,8,3456]{2,1,0:T(8,128)(2,1)} %get-tuple-element.23), channel_id=1, source_target_pairs={{0,24},{4,28},{8,16},{12,20},{16,8},{20,12},{24,0},{28,4},{1,25},{... | collective-permute-start | bytes 663560 | tf_op jit(solution)/shard_map/ppermute | solution.py:410
  63.1 6.1 %copy-start.5 = (bf16[4,8,3456]{2,1,0:T(8,128)(2,1)}, bf16[4,8,3456]{2,1,0:T(8,128)(2,1)S(1)}, u32[]{:S(2)}) copy-start(bf16[4,8,3456]{2,1,0:T(8,128)(2,1)S(1)} %collective-permute-done.5.refs_1_) | copy-start | bytes 663556
  67.4 1.8 %copy-start.6 = (bf16[4,8,3456]{2,1,0:T(8,128)(2,1)}, bf16[4,8,3456]{2,1,0:T(8,128)(2,1)S(1)}, u32[]{:S(2)}) copy-start(bf16[4,8,3456]{2,1,0:T(8,128)(2,1)S(1)} %collective-permute-done.6.refs_2_) | copy-start | bytes 663556
  69.2 0.7 copy-start.7
  72.3 7.5 %collective-permute-start.10 = (f32[8,3328]{1,0:T(8,128)}, f32[8,3328]{1,0:T(8,128)S(1)}, u32[]{:S(2)}, u32[]{:S(2)}) collective-permute-start(f32[8,3328]{1,0:T(8,128)} %get-tuple-element.27), channel_id=1, source_target_pairs={{0,3},{1,2},{2,1},{3,0},{4,7},{5,6},{6,5},{7,4},{8,11},{9,10},{10,... | collective-permute-start | bytes 319496 | tf_op jit(solution)/shard_map/ppermute | solution.py:413
  75.9 6.2 %collective-permute-start.8 = (f32[8,3328]{1,0:T(8,128)}, f32[8,3328]{1,0:T(8,128)S(1)}, u32[]{:S(2)}, u32[]{:S(2)}) collective-permute-start(f32[8,3328]{1,0:T(8,128)} %get-tuple-element.25), channel_id=1, source_target_pairs={{0,1},{1,0},{2,3},{3,2},{4,5},{5,4},{6,7},{7,6},{8,9},{9,8},{10,11... | collective-permute-start | bytes 319496 | tf_op jit(solution)/shard_map/ppermute | solution.py:413
  75.9 8.7 %collective-permute-start.9 = (f32[8,3328]{1,0:T(8,128)}, f32[8,3328]{1,0:T(8,128)S(1)}, u32[]{:S(2)}, u32[]{:S(2)}) collective-permute-start(f32[8,3328]{1,0:T(8,128)} %get-tuple-element.26), channel_id=1, source_target_pairs={{0,2},{1,3},{2,0},{3,1},{4,6},{5,7},{6,4},{7,5},{8,10},{9,11},{10,... | collective-permute-start | bytes 319496 | tf_op jit(solution)/shard_map/ppermute | solution.py:413
  85.5 5.7 %collective-permute-start.11 = (f32[8,3328]{1,0:T(8,128)S(1)}, f32[8,3328]{1,0:T(8,128)S(1)}, u32[]{:S(2)}, u32[]{:S(2)}) collective-permute-start(f32[8,3328]{1,0:T(8,128)S(1)} %get-tuple-element.31), channel_id=1, source_target_pairs={{0,8},{4,12},{8,0},{12,4},{16,24},{20,28},{24,16},{28,20},{1,9},{5... | collective-permute-start | bytes 319496 | tf_op jit(solution)/shard_map/ppermute | solution.py:418
  86.3 7.0 %collective-permute-start.12 = (f32[8,3328]{1,0:T(8,128)S(1)}, f32[8,3328]{1,0:T(8,128)S(1)}, u32[]{:S(2)}, u32[]{:S(2)}) collective-permute-start(f32[8,3328]{1,0:T(8,128)S(1)} %get-tuple-element.31), channel_id=1, source_target_pairs={{0,16},{4,20},{8,24},{12,28},{16,0},{20,4},{24,8},{28,12},{1,17},{... | collective-permute-start | bytes 319496 | tf_op jit(solution)/shard_map/ppermute | solution.py:418
  87.4 5.8 %collective-permute-start.13 = (f32[8,3328]{1,0:T(8,128)S(1)}, f32[8,3328]{1,0:T(8,128)S(1)}, u32[]{:S(2)}, u32[]{:S(2)}) collective-permute-start(f32[8,3328]{1,0:T(8,128)S(1)} %get-tuple-element.31), channel_id=1, source_target_pairs={{0,24},{4,28},{8,16},{12,20},{16,8},{20,12},{24,0},{28,4},{1,25},{... | collective-permute-start | bytes 319496 | tf_op jit(solution)/shard_map/ppermute | solution.py:418
  93.3 1.8 %collective-permute-start.14 = (f32[32,3328]{1,0:T(8,128)S(1)}, f32[32,3328]{1,0:T(8,128)S(1)}, u32[]{:S(2)}, u32[]{:S(2)}) collective-permute-start(f32[32,3328]{1,0:T(8,128)S(1)} %bitcast.23), channel_id=1, source_target_pairs={{0,4},{4,0},{8,12},{12,8},{16,20},{20,16},{24,28},{28,24},{1,5},{5... | collective-permute-start | bytes 1277960 | tf_op jit(solution)/shard_map/ppermute | solution.py:420

commit v3 on v2

--- a/solution.py
+++ b/solution.py
@@ -16,7 +16,8 @@
 SCALE = 2.0 / FEAT
 SUM_LANES = 9 * W + FEAT
 GROUPS = ((0, 3 * W), (3 * W, 6 * W), (6 * W, 9 * W), (9 * W, SUM_LANES))
-CODE_LANES = SUM_LANES + 128
+CODE_LANES = SUM_LANES + 128 * 4
+VMEM_LIMIT = 52 * 2**20
 BASE = 125.0 * math.log(2.0)
 SPAN = 250.0 * math.log(2.0)
 
@@ -58,52 +59,72 @@
         body(frame, tile)
 
 
-def project_kernel(place_ref, target_ref, head_ref, out_ref, near_ref, far_ref):
-    count = target_ref.shape[0]
-    low, high = slice(0, BACK), slice(count - BACK, count)
+def edges_kernel(place_ref, clip_hbm, target_hbm, head_ref, near_ref, far_ref, goal_ref, sem):
+    count = clip_hbm.shape[0]
     even = place_ref[0] % 2 == 0
-    loop_rows(0, count, 512, functools.partial(project_rows, target_ref, head_ref, out_ref))
-
-    @pl.when(even)
-    def _():
-        near_ref[...] = out_ref[high, :]
-        far_ref[...] = out_ref[low, :]
-
-    @pl.when(jnp.logical_not(even))
-    def _():
-        near_ref[...] = out_ref[low, :]
-        far_ref[...] = out_ref[high, :]
-
-
-def project_rows(target_ref, head_ref, out_ref, frame, size):
-    out_ref[frame : frame + size, :] = dot_nt(target_ref[frame : frame + size, :], head_ref[...])
-
-
-def project(place, target, head_weight):
+    loads = []
+    for side, (edge_ref, flag) in enumerate(((near_ref, even), (far_ref, jnp.logical_not(even)))):
+        for rows, source, target in (
+            (BACK, target_hbm, goal_ref.at[side * BACK : (side + 1) * BACK]),
+            (HALO, clip_hbm, edge_ref.at[0:HALO]),
+        ):
+            start = pl.multiple_of(jnp.where(flag, count - rows, 0), 16)
+            loads.append(pltpu.make_async_copy(source.at[pl.ds(start, rows)], target, sem.at[len(loads)]))
+            loads[-1].start()
+    for side, edge_ref in enumerate((near_ref, far_ref)):
+        loads[2 * side].wait()
+        high, low = split(dot_nt(goal_ref[side * BACK : (side + 1) * BACK], head_ref[...]))
+        edge_ref[HALO : HALO + BACK] = high
+        edge_ref[HALO + BACK :] = low
+    for load in loads[1::2]:
+        load.wait()
+
+
+def edges(place, clip, target, head_weight):
+    anywhere = pl.BlockSpec(memory_space=pl.ANY)
+    return pl.pallas_call(
+        edges_kernel,
+        in_specs=[smem(), anywhere, anywhere, whole()],
+        out_specs=[whole()] * 2,
+        out_shape=[jax.ShapeDtypeStruct((HALO + 2 * BACK, W), jnp.bfloat16)] * 2,
+        scratch_shapes=[pltpu.VMEM((2 * BACK, FEAT), jnp.bfloat16), pltpu.SemaphoreType.DMA((4,))],
+        compiler_params=pltpu.CompilerParams(vmem_limit_bytes=VMEM_LIMIT),
+        name="edges",
+    )(place, clip, target, head_weight)
+
+
+def project_kernel(target_ref, head_ref, out_ref):
+    out_ref[...] = dot_nt(target_ref[...], head_ref[...])
+
+
+def project(target, head_weight):
     count = target.shape[0]
+    tile = tile_of(count, 512)
     return pl.pallas_call(
         project_kernel,
-        in_specs=[smem(), whole(), whole()],
-        out_specs=[whole()] * 3,
-        out_shape=[jax.ShapeDtypeStruct((rows, W), jnp.float32) for rows in (count, BACK, BACK)],
-        compiler_params=pltpu.CompilerParams(vmem_limit_bytes=24 * 2**20),
+        grid=(count // tile,),
+        in_specs=[
+            pl.BlockSpec((tile, FEAT), lambda i: (i, 0)),
+            pl.BlockSpec((W, FEAT), lambda i: (0, 0)),
+        ],
+        out_specs=pl.BlockSpec((tile, W), lambda i: (i, 0)),
+        out_shape=jax.ShapeDtypeStruct((count, W), jnp.float32),
+        compiler_params=pltpu.CompilerParams(vmem_limit_bytes=VMEM_LIMIT),
         cost_estimate=pl.CostEstimate(
             flops=2 * count * W * FEAT, bytes_accessed=count * (2 * FEAT + 4 * W), transcendentals=0
         ),
         name="project_targets",
-    )(place, target, head_weight)
+    )(target, head_weight)
 
 
 def main_kernel(
     count,
     place_ref,
     clip_ref,
-    clip_a_ref,
-    clip_b_ref,
+    near_ref,
+    far_ref,
     target_hbm,
     proj_ref,
-    proj_a_ref,
-    proj_b_ref,
     conv_hbm,
     head_hbm,
     keep_ref,
@@ -124,6 +145,7 @@
     conv_ref,
     head_ref,
     target_ref,
+    goals,
     in_sem,
     out_sem,
 ):
@@ -152,13 +174,13 @@
     loads = [
         (conv_hbm.at[0], conv_ref.at[0]),
         (clip_ref, h0.at[HALO : HALO + count]),
-        (clip_a_ref, h0.at[pl.ds(above, HALO)]),
-        (clip_b_ref, h0.at[pl.ds(below, HALO)]),
+        (near_ref.at[0:HALO], h0.at[pl.ds(above, HALO)]),
+        (far_ref.at[0:HALO], h0.at[pl.ds(below, HALO)]),
         (conv_hbm.at[1:3], conv_ref.at[1:3]),
         (head_hbm, head_ref),
         (proj_ref, err.at[HALO : HALO + count]),
-        (proj_a_ref, err.at[pl.ds(err_above, BACK)]),
-        (proj_b_ref, err.at[pl.ds(err_below, BACK)]),
+        (near_ref.at[HALO:], goals.at[0]),
+        (far_ref.at[HALO:], goals.at[1]),
         (target_hbm, target_ref),
     ]
     loads = [pltpu.make_async_copy(*load, in_sem.at[i]) for i, load in enumerate(loads)]
@@ -219,6 +241,9 @@
 
     for load in loads[5:9]:
         load.wait()
+    for side, start in enumerate((err_above, err_below)):
+        high, low = goals[side, 0:BACK, :], goals[side, BACK:, :]
+        err[pl.ds(start, BACK), :] = high.astype(jnp.float32) + low.astype(jnp.float32)
     high, low = split(dot_nt(head_ref[...], head_ref[...]))
     gram[0:W, :] = high
     gram[W : 2 * W, :] = low
@@ -263,13 +288,13 @@
         copy.wait()
 
 
-def main(pens, place, clip, clip_a, clip_b, target, proj, proj_a, proj_b, conv_weight, head_weight):
+def main(pens, place, clip, near, far, target, proj, conv_weight, head_weight):
     count = clip.shape[0]
     rows = count + 2 * HALO
     flops = 2 * W * W * (9 * rows + 14 * rows + 18 * count + 6 * count)
     return pl.pallas_call(
         functools.partial(main_kernel, count),
-        in_specs=[smem()] + [pl.BlockSpec(memory_space=pl.ANY)] * 9,
+        in_specs=[smem()] + [pl.BlockSpec(memory_space=pl.ANY)] * 7,
         out_specs=[pl.BlockSpec(memory_space=pl.ANY)] * 2,
         out_shape=[jax.ShapeDtypeStruct((pens, W // (2 * pens), SUM_LANES), jnp.float32)] * 2,
         scratch_shapes=[pltpu.VMEM((rows, W), jnp.bfloat16)] * 4
@@ -283,13 +308,14 @@
             pltpu.VMEM(conv_weight.shape, jnp.bfloat16),
             pltpu.VMEM(head_weight.shape, jnp.bfloat16),
             pltpu.VMEM(target.shape, jnp.bfloat16),
+            pltpu.VMEM((2, 2 * BACK, W), jnp.bfloat16),
             pltpu.SemaphoreType.DMA((10,)),
             pltpu.SemaphoreType.DMA((8 * pens,)),
         ],
-        compiler_params=pltpu.CompilerParams(vmem_limit_bytes=56 * 2**20),
+        compiler_params=pltpu.CompilerParams(vmem_limit_bytes=VMEM_LIMIT),
         cost_estimate=pl.CostEstimate(flops=flops, bytes_accessed=16 * 2**20, transcendentals=3 * rows * W),
         name="forward_backward",
-    )(place, clip, clip_a, clip_b, target, proj, proj_a, proj_b, conv_weight, head_weight)
+    )(place, clip, near, far, target, proj, conv_weight, head_weight)
 
 
 def swap(near, far):
@@ -299,65 +325,123 @@
     return lax.ppermute(near, "tm", [(i, i ^ 1) for i in range(count)]), from_far
 
 
-def encode(values, code_ref):
-    pens = len(values)
-    for place, (first, stop) in enumerate(GROUPS):
-        lanes = range(first, stop, 128)
-        most = functools.reduce(
-            jnp.maximum, [jnp.abs(values[pen][:, lane : lane + 128]) for pen in range(pens) for lane in lanes]
-        )
-        most = (most * 1.0079).astype(jnp.bfloat16)
-        code_ref[place, :, SUM_LANES:] = most
-        most = most.astype(jnp.float32)
-        grow = jnp.where(most > 1e-36, SPAN / jnp.maximum(most, 1e-36), 0.0)
-        for pen in range(pens):
-            for lane in lanes:
-                part = values[pen][:, lane : lane + 128]
-                code = jnp.exp(jnp.abs(part) * grow - BASE)
-                code = jnp.where(part < 0.0, -code, code)
-                code_ref[pen, :, lane : lane + 128] = code.astype(jnp.bfloat16)
-    for pen in range(len(GROUPS), pens):
-        code_ref[pen, :, SUM_LANES:] = jnp.zeros_like(code_ref[pen, :, SUM_LANES:])
-
-
-def decode(code_ref, pen, lane, place):
-    code = code_ref[pen, :, lane : lane + 128].astype(jnp.float32)
-    most = code_ref[place, :, SUM_LANES:].astype(jnp.float32) * (1.0 / SPAN)
-    size = (jnp.log(jnp.abs(code)) + BASE) * most
+def encode(parts):
+    most = functools.reduce(jnp.maximum, [jnp.abs(part) for part in parts])
+    most = (most * 1.0079).astype(jnp.bfloat16)
+    wide = most.astype(jnp.float32)
+    grow = jnp.where(wide > 1e-36, SPAN / jnp.maximum(wide, 1e-36), 0.0)
+    codes = []
+    for part in parts:
+        code = jnp.exp(jnp.abs(part) * grow - BASE)
+        codes.append(jnp.where(part < 0.0, -code, code).astype(jnp.bfloat16))
+    return codes, most
+
+
+def decode(code, most):
+    code = code.astype(jnp.float32)
+    size = (jnp.log(jnp.abs(code)) + BASE) * (most.astype(jnp.float32) * (1.0 / SPAN))
     return jnp.where(code < 0.0, -size, size)
+
+
+def tiles_of(group):
+    return [slice(lane, lane + 128) for lane in range(*GROUPS[group], 128)]
+
+
+def tail_of(group):
+    return slice(SUM_LANES + 128 * group, SUM_LANES + 128 * (group + 1))
+
+
+def encode_rows(ref, code_ref):
+    for group in range(len(GROUPS)):
+        tiles = tiles_of(group)
+        codes, most = encode([ref[:, tile] for tile in tiles])
+        for tile, code in zip(tiles, codes):
+            code_ref[:, tile] = code
+        code_ref[:, tail_of(group)] = most
 
 
 def cores_kernel(place_ref, keep_ref, other_ref, own_ref, *sent):
     groups, pens, rows = len(sent) + 1, own_ref.shape[0], own_ref.shape[1]
-    group = place_ref[0] // 2
-
-    def rows_of(index, pen):
+    mine = place_ref[0] // 2
+
+    def rows_of(index, pen, tile):
         if rows % 8 == 0:
             here = pl.ds(pl.multiple_of(index * rows, 8), rows)
-            return keep_ref[pen, here, :] + other_ref[pen, here, :]
-        total = keep_ref[pen] + other_ref[pen]
+            return keep_ref[pen, here, tile] + other_ref[pen, here, tile]
+        total = keep_ref[pen, :, tile] + other_ref[pen, :, tile]
         return functools.reduce(
             lambda a, b: a + b,
             [jnp.where(index == i, total[i * rows : (i + 1) * rows], 0.0) for i in range(groups)],
         )
 
-    for pen in range(pens):
-        own_ref[pen] = rows_of(group, pen)
-    for j in range(1, groups):
-        encode([rows_of(group ^ j, pen) for pen in range(pens)], sent[j - 1])
+    for group in range(len(GROUPS)):
+        places = [(pen, tile) for pen in range(pens) for tile in tiles_of(group)]
+        for pen, tile in places:
+            own_ref[pen, :, tile] = rows_of(mine, pen, tile)
+        for j in range(1, groups):
+            codes, most = encode([rows_of(mine ^ j, pen, tile) for pen, tile in places])
+            for (pen, tile), code in zip(places, codes):
+                sent[j - 1][pen, :, tile] = code
+            sent[j - 1][group, :, SUM_LANES:] = most
+    for pen in range(len(GROUPS), pens):
+        for code_ref in sent:
+            code_ref[pen, :, SUM_LANES:] = jnp.zeros_like(code_ref[pen, :, SUM_LANES:])
 
 
 def chips_kernel(place_ref, own_ref, *refs):
     pens = own_ref.shape[0]
-    arrived, mine_ref, sent = refs[:-2], refs[-2], refs[-1]
-    for place, (first, stop) in enumerate(GROUPS):
-        for lane in range(first, stop, 128):
+    arrived, mine_ref, sent, total_ref = refs[: -pens - 1], refs[-pens - 1], refs[-pens:-1], refs[-1]
+    for group in range(len(GROUPS)):
+        for tile in tiles_of(group):
             for pen in range(pens):
-                total = own_ref[pen, :, lane : lane + 128]
+                total = own_ref[pen, :, tile]
                 for other in arrived:
-                    total = total + decode(other, pen, lane, place)
-                sent[pen, :, lane : lane + 128] = total
-    mine_ref[...] = sent[place_ref[2]]
+                    total = total + decode(other[pen, :, tile], other[group, :, SUM_LANES:])
+                total_ref[pen, :, tile] = total
+    mine_ref[...] = total_ref[place_ref[2]]
+    for j, code_ref in enumerate(sent, 1):
+        encode_rows(total_ref.at[place_ref[2] ^ j], code_ref)
+
+
+def streams_kernel(mine_ref, *refs):
+    arrived, code_ref, total_ref = refs[:-2], refs[-2], refs[-1]
+    for group in range(len(GROUPS)):
+        for tile in tiles_of(group):
+            total = mine_ref[:, tile]
+            for other in arrived:
+                total = total + decode(other[:, tile], other[:, tail_of(group)])
+            total_ref[:, tile] = total
+    encode_rows(total_ref, code_ref)
+
+
+def unpack_kernel(place_ref, *refs):
+    codes, (conv_ref, head_ref) = refs[:-2], refs[-2:]
+    groups, rows = len(codes) // 2, codes[0].shape[0]
+    core, mine = place_ref[0] % 2, place_ref[0] // 2
+
+    def write(code_ref, here):
+        for group in range(len(GROUPS)):
+            for tile in tiles_of(group):
+                value = decode(code_ref[:, tile], code_ref[:, tail_of(group)])
+                if group < 3:
+                    tap, lane = (tile.start - GROUPS[group][0]) // W, tile.start % W
+                    conv_ref[group, tap, here, lane : lane + 128] = value
+                else:
+                    lane = tile.start - GROUPS[3][0]
+                    head_ref[here, lane : lane + 128] = value
+
+    for side in range(2):
+        for j in range(groups):
+            code_ref = codes[side * groups + j]
+            index = (core ^ side) * groups + (mine ^ j)
+            if rows % 8 == 0:
+                write(code_ref, pl.ds(pl.multiple_of(index * rows, 8), rows))
+            else:
+                for known in range(2 * groups):
+
+                    @pl.when(index == known)
+                    def _():
+                        write(code_ref, slice(known * rows, (known + 1) * rows))
 
 
 def smem():
@@ -366,6 +450,14 @@
 
 def whole():
     return pl.BlockSpec(memory_space=pltpu.VMEM)
+
+
+def near(arrays):
+    return [pltpu.with_memory_space_constraint(array, pltpu.VMEM) for array in arrays]
+
+
+def on_vmem():
+    return pltpu.CompilerParams(vmem_limit_bytes=16 * 2**20)
 
 
 def sum_cores(place, keep, other, groups):
@@ -373,30 +465,54 @@
     rows = half // groups
     return pl.pallas_call(
         cores_kernel,
-        in_specs=[smem()] + [whole()] * 2,
+        in_specs=[smem(), whole(), whole()],
         out_specs=[whole()] * groups,
         out_shape=[jax.ShapeDtypeStruct((pens, rows, lanes), jnp.float32)]
-        + [jax.ShapeDtypeStruct((pens, rows, CODE_LANES), jnp.bfloat16)] * (groups - 1),
+        + [jax.ShapeDtypeStruct((pens, rows, lanes + 128), jnp.bfloat16)] * (groups - 1),
+        compiler_params=on_vmem(),
         name="sum_cores",
-    )(place, keep, other)
+    )(place, *near([keep, other]))
 
 
 def sum_chips(place, own, arrived):
     pens, rows, lanes = own.shape
-    def kernel(place_ref, *refs):
-        ins, outs, total = refs[: 1 + len(arrived)], refs[1 + len(arrived) : -1], refs[-1]
-        chips_kernel(place_ref, *ins, outs[0], total)
-        for j in range(1, pens):
-            outs[j][...] = total[place_ref[2] ^ j]
-
-    return pl.pallas_call(
-        kernel,
+    return pl.pallas_call(
+        chips_kernel,
         in_specs=[smem()] + [whole()] * (1 + len(arrived)),
         out_specs=[whole()] * pens,
-        out_shape=[jax.ShapeDtypeStruct((rows, lanes), jnp.float32)] * pens,
-        scratch_shapes=[pltpu.VMEM((pens, rows, lanes), jnp.float32)],
+        out_shape=[jax.ShapeDtypeStruct((rows, lanes), jnp.float32)]
+        + [jax.ShapeDtypeStruct((rows, CODE_LANES), jnp.bfloat16)] * (pens - 1),
+        scratch_shapes=[pltpu.VMEM(own.shape, jnp.float32)],
+        compiler_params=on_vmem(),
         name="sum_chips",
-    )(place, own, *arrived)
+    )(place, *near([own] + arrived))
+
+
+def sum_streams(mine, arrived):
+    return pl.pallas_call(
+        streams_kernel,
+        in_specs=[whole()] * (1 + len(arrived)),
+        out_specs=whole(),
+        out_shape=jax.ShapeDtypeStruct((mine.shape[0], CODE_LANES), jnp.bfloat16),
+        scratch_shapes=[pltpu.VMEM(mine.shape, jnp.float32)],
+        compiler_params=on_vmem(),
+        name="sum_streams",
+    )(*near([mine] + arrived))
+
+
+def unpack(place, codes):
+    rows = len(codes) * codes[0].shape[0]
+    return pl.pallas_call(
+        unpack_kernel,
+        in_specs=[smem()] + [whole()] * len(codes),
+        out_specs=[whole()] * 2,
+        out_shape=[
+            jax.ShapeDtypeStruct((3, 3, rows, W), jnp.float32),
+            jax.ShapeDtypeStruct((rows, FEAT), jnp.float32),
+        ],
+        compiler_params=on_vmem(),
+        name="unpack",
+    )(place, *near(codes))
 
 
 def reduce_sums(place, keep, send):
@@ -408,32 +524,20 @@
     other = lax.ppermute(send, "tm", sibling)
     own, *codes = sum_cores(place, keep, other, groups)
     arrived = [lax.ppermute(code, "tm", pairs) for code, pairs in zip(codes, chips)]
-    mine, *parts = sum_chips(place, own, arrived)
-    for part, pairs in zip(parts, streams):
-        mine = mine + lax.ppermute(part, "pen", pairs)
-    core, group = place[0] % 2, place[0] // 2
-    half = jnp.zeros((groups,) + mine.shape, mine.dtype)
-    half = lax.dynamic_update_index_in_dim(half, mine, group, 0)
-    for j, pairs in enumerate(chips, 1):
-        half = lax.dynamic_update_index_in_dim(half, lax.ppermute(mine, "tm", pairs), group ^ j, 0)
-    half = half.reshape(-1, half.shape[2])
-    other = lax.ppermute(half, "tm", sibling)
-    rows = jnp.concatenate([jnp.where(core == 0, half, other), jnp.where(core == 0, other, half)], axis=0)
-    return rows[:, : 9 * W].reshape(-1, 3, 3, W).transpose(1, 2, 0, 3), rows[:, 9 * W :]
+    mine, *codes = sum_chips(place, own, arrived)
+    arrived = [lax.ppermute(code, "pen", pairs) for code, pairs in zip(codes, streams)]
+    code = sum_streams(mine, arrived)
+    half = [code] + [lax.ppermute(code, "tm", pairs) for pairs in chips]
+    return unpack(place, half + [lax.ppermute(code, "tm", sibling) for code in half])
 
 
 def on_device(clips, targets, conv_weight, head_weight):
     clip, target = clips[0], targets[0]
     count, pens = lax.axis_size("tm"), lax.axis_size("pen")
     place = jnp.stack([lax.axis_index("tm"), count, lax.axis_index("pen"), pens]).astype(jnp.int32)
-    even = place[0] % 2 == 0
-    low, high = clip[:HALO], clip[clip.shape[0] - HALO :]
-    clip_a, clip_b = swap(jnp.where(even, high, low), jnp.where(even, low, high))
-    proj, near, far = project(place, target, head_weight)
-    proj_a, proj_b = swap(near, far)
-    keep, send = main(
-        pens, place, clip, clip_a, clip_b, target, proj, proj_a, proj_b, conv_weight, head_weight
-    )
+    near, far = swap(*edges(place, clip, target, head_weight))
+    proj = project(target, head_weight)
+    keep, send = main(pens, place, clip, near, far, target, proj, conv_weight, head_weight)
     return reduce_sums(place, keep, send)
 
 

time: 97.5 us -> 88.4 us (0.907)
  local copies, waits for them, and re-layouts: 7.77 us -> 2.5 us
  waiting for transfers between devices: 28.2 us -> 23.4 us
  Pallas kernels: 29.6 us -> 33.7 us
  other arithmetic: 3.01 us -> 0.08 us
    unnamed x25 -> x4, local copies, waits for them, and re-layouts: 7.39 us -> 2.5 us
    ppermute x7 -> x10, waiting for transfers between devices: 13.8 us -> 9.33 us  [the longest x3 5.79 us: reduce_sums(): lax.ppermute(code, 'pen', pairs)]
    pallas_call x3 -> x6, Pallas kernels: 7.63 us -> 12 us  [the longest x1 5.11 us: project(): pl.pallas_call(project_kernel, grid=(count // tile,), in_specs=[pl.BlockS...]
    ppermute x2 -> x1, starting transfers between devices: 4.37 us -> 0.52 us  [swap(): lax.ppermute(near, 'tm', [(i, i ^ 1) for i in range(count)])]
    ppermute x1, starting transfers between devices: 9.87 us -> 13.3 us  [reduce_sums(): other = lax.ppermute(send, 'tm', sibling)]
    select_n x2 -> x0, other arithmetic: 1.24 us -> none  [the longest x1 1.18 us: on_device(): jnp.where(even, low, high)]
    ppermute x7 -> x10, starting transfers between devices: 8.01 us -> 8.26 us  [the longest x3 4.45 us: reduce_sums(): lax.ppermute(code, 'pen', pairs)]
  transfers between devices with their start and end apart: 15 -> 16, of which waited for: 11 -> 12; matrix products, arithmetic and copies ran while one was open for 0% -> 0% of each run, Pallas kernels for 2% -> 6%
where the time goes in v3:
time: 88.4 us; the launch traced here: 88.1 us
  Pallas kernels  33.7 us (38%)
  starting transfers between devices  27.7 us (31%)
  waiting for transfers between devices  23.4 us (26%)
  local copies, waits for them, and re-layouts  2.5 us (3%)
    pallas_call x1, Pallas kernels, main(): pl.pallas_call(functools.partial(main_kernel, count), in_specs=[smem()] +...  21.7 us
    ppermute x1, starting transfers between devices, reduce_sums(): other = lax.ppermute(send, 'tm', sibling)  13.3 us
    ppermute x3, waiting for transfers between devices, reduce_sums(): lax.ppermute(code, 'tm', pairs)  10.6 us
    ppermute x3, waiting for transfers between devices, reduce_sums(): lax.ppermute(code, 'pen', pairs)  5.79 us
    pallas_call x1, Pallas kernels, project(): pl.pallas_call(project_kernel, grid=(count // tile,), in_specs=[pl.BlockS...  5.11 us
    ppermute x3, starting transfers between devices, reduce_sums(): lax.ppermute(code, 'tm', pairs)  4.91 us
    ppermute x3, starting transfers between devices, reduce_sums(): lax.ppermute(code, 'pen', pairs)  4.45 us
    ppermute x3, starting transfers between devices, reduce_sums(): half = [code] + [lax.ppermute(code, 'tm', pairs) for pairs in chips]  3.55 us
  transfers between devices with their start and end apart: 16, of which 12 were waited for; matrix products, arithmetic and copies ran while one was open for 0% of the time, Pallas kernels for 6%

profile of v3, /device:TPU:0, one launch (start us, length us, event | category | flops | bytes accessed | tf_op | source)
XLA Modules:
  0.0 88.1 jit_solution(8823259872228877471)
XLA Ops:
  0.6 0.1 pad_add_fusion.place_ref
  0.7 0.0 copy-start
  0.7 1.0 %copy-done = bf16[256,1024]{1,0:T(8,128)(2,1)S(1)} copy-done((bf16[256,1024]{1,0:T(8,128)(2,1)S(1)}, bf16[256,1024]{1,0:T(8,128)(2,1)}, u32[]{:S(2)}) %copy-start) | copy-done | bytes 524312
  1.8 2.7 %edges.1 = (bf16[1296,256]{1,0:T(8,128)(2,1)S(1)}, bf16[1296,256]{1,0:T(8,128)(2,1)S(1)}) custom-call(s32[4]{0:T(128)S(1)} %pad_add_fusion.place_ref, bf16[2048,256]{1,0:T(8,128)(2,1)} %bitcast.7, bf16[2048,1024]{1,0:T(8,128)(2,1)} %bitcast.4, bf16[256,1024]{1,0:T(8,128)(2,1)S(1)} %copy-done), custom_call_target="tpu_custom_call" | custom-call | tf_op jit(solution)/shard_map/edges/pallas_call | solution.py:85
  4.5 0.5 collective-permute-start
  5.0 0.7 collective-permute-start.1
  5.7 5.1 %project_targets.1.proj_ref = f32[2048,256]{1,0:T(8,128)} custom-call(bf16[2048,1024]{1,0:T(8,128)(2,1)} %bitcast.5, bf16[256,1024]{1,0:T(8,128)(2,1)S(1)} %copy-done), custom_call_target="tpu_custom_call" | custom-call | flops 1073741824 | bytes 6291456 | tf_op jit(solution)/shard_map/project_targets/pallas_call | solution.py:103
  10.8 0.0 collective-permute-done.near_ref
  10.8 0.0 collective-permute-done.1.far_ref
  10.8 21.7 %forward_backward.1 = (f32[4,32,3328]{2,1,0:T(8,128)}, f32[4,32,3328]{2,1,0:T(8,128)}) custom-call(s32[4]{0:T(128)S(1)} %pad_add_fusion.place_ref, bf16[2048,256]{1,0:T(8,128)(2,1)} %bitcast.8, bf16[1296,256]{1,0:T(8,128)(2,1)S(1)} %collective-permute-done.near_ref, bf16[1296,256]{1,0:T(8,128)(2,1)S(1)} %collective-permute-done.1.far_ref, ...), custom_call_target="tpu_custom_call" | custom-call | flops 16571695104 | bytes 16777216 | tf_op jit(solution)/shard_map/forward_backward/pallas_call | solution.py:295
  32.5 13.3 %collective-permute-start.2 = (f32[4,32,3328]{2,1,0:T(8,128)}, f32[4,32,3328]{2,1,0:T(8,128)S(1)}, u32[]{:S(2)}, u32[]{:S(2)}) collective-permute-start(f32[4,32,3328]{2,1,0:T(8,128)} %get-tuple-element.17), channel_id=1, source_target_pairs={{0,4},{4,0},{8,12},{12,8},{16,20},{20,16},{24,28},{28,24},{1,5},{5... | collective-permute-start | bytes 5111816 | tf_op jit(solution)/shard_map/ppermute | solution.py:524
  45.9 3.4 %collective-permute-done.2.other_ref = f32[4,32,3328]{2,1,0:T(8,128)S(1)} collective-permute-done((f32[4,32,3328]{2,1,0:T(8,128)}, f32[4,32,3328]{2,1,0:T(8,128)S(1)}, u32[]{:S(2)}, u32[]{:S(2)}) %collective-permute-start.2) | collective-permute-done | bytes 1703968 | tf_op jit(solution)/shard_map/ppermute | solution.py:524
  49.3 0.0 copy-start.1
  49.3 1.5 %copy-done.1 = f32[4,32,3328]{2,1,0:T(8,128)S(1)} copy-done((f32[4,32,3328]{2,1,0:T(8,128)S(1)}, f32[4,32,3328]{2,1,0:T(8,128)}, u32[]{:S(2)}) %copy-start.1) | copy-done | bytes 1703960
  50.8 1.2 %sum_cores.1 = (f32[4,8,3328]{2,1,0:T(8,128)S(1)}, bf16[4,8,3456]{2,1,0:T(8,128)(2,1)S(1)}, bf16[4,8,3456]{2,1,0:T(8,128)(2,1)S(1)}, bf16[4,8,3456]{2,1,0:T(8,128)(2,1)S(1)}) custom-call(s32[4]{0:T(128)S(1)} %pad_add_fusion.place_ref, f32[4,32,3328]{2,1,0:T(8,128)S(1)} %copy-done.1, f32[4,32,3328]{2,1,0:T(8,128)S(1)} %collective-permute-done.2.other_ref), custom_call_target="tpu_custom_call" | custom-call | tf_op jit(solution)/shard_map/sum_cores/pallas_call | solution.py:466
  51.9 3.4 %collective-permute-start.3 = (bf16[4,8,3456]{2,1,0:T(8,128)(2,1)S(1)}, bf16[4,8,3456]{2,1,0:T(8,128)(2,1)S(1)}, u32[]{:S(2)}, u32[]{:S(2)}) collective-permute-start(bf16[4,8,3456]{2,1,0:T(8,128)(2,1)S(1)} %get-tuple-element.19), channel_id=1, source_target_pairs={{0,8},{4,12},{8,0},{12,4},{16,24},{20,28},{24,16},{28,20},{1,9},{5... | collective-permute-start | bytes 663560 | tf_op jit(solution)/shard_map/ppermute | solution.py:526
  55.3 0.6 collective-permute-start.4
  55.9 1.0 %collective-permute-start.5 = (bf16[4,8,3456]{2,1,0:T(8,128)(2,1)S(1)}, bf16[4,8,3456]{2,1,0:T(8,128)(2,1)S(1)}, u32[]{:S(2)}, u32[]{:S(2)}) collective-permute-start(bf16[4,8,3456]{2,1,0:T(8,128)(2,1)S(1)} %get-tuple-element.21), channel_id=1, source_target_pairs={{0,24},{4,28},{8,16},{12,20},{16,8},{20,12},{24,0},{28,4},{1,25},{... | collective-permute-start | bytes 663560 | tf_op jit(solution)/shard_map/ppermute | solution.py:526
  56.9 4.7 %collective-permute-done.3.refs_0_ = bf16[4,8,3456]{2,1,0:T(8,128)(2,1)S(1)} collective-permute-done((bf16[4,8,3456]{2,1,0:T(8,128)(2,1)S(1)}, bf16[4,8,3456]{2,1,0:T(8,128)(2,1)S(1)}, u32[]{:S(2)}, u32[]{:S(2)}) %collective-permute-start.3) | collective-permute-done | bytes 221216 | tf_op jit(solution)/shard_map/ppermute | solution.py:526
  61.6 5.9 %collective-permute-done.4.refs_1_ = bf16[4,8,3456]{2,1,0:T(8,128)(2,1)S(1)} collective-permute-done((bf16[4,8,3456]{2,1,0:T(8,128)(2,1)S(1)}, bf16[4,8,3456]{2,1,0:T(8,128)(2,1)S(1)}, u32[]{:S(2)}, u32[]{:S(2)}) %collective-permute-start.4) | collective-permute-done | bytes 221216 | tf_op jit(solution)/shard_map/ppermute | solution.py:526
  67.5 0.0 collective-permute-done.5.refs_2_
  67.5 1.1 %sum_chips.1 = (f32[8,3328]{1,0:T(8,128)S(1)}, bf16[8,3840]{1,0:T(8,128)(2,1)S(1)}, bf16[8,3840]{1,0:T(8,128)(2,1)S(1)}, bf16[8,3840]{1,0:T(8,128)(2,1)S(1)}) custom-call(s32[4]{0:T(128)S(1)} %pad_add_fusion.place_ref, f32[4,8,3328]{2,1,0:T(8,128)S(1)} %get-tuple-element.18.own_ref, bf16[4,8,3456]{2,1,0:T(8,128)(2,1)S(1)} %collective-permute-done.3.refs_0_, ...), custom_call_target="tpu_custom_call" | custom-call | tf_op jit(solution)/shard_map/sum_chips/pallas_call | solution.py:479
  68.6 1.6 %collective-permute-start.6 = (bf16[8,3840]{1,0:T(8,128)(2,1)S(1)}, bf16[8,3840]{1,0:T(8,128)(2,1)S(1)}, u32[]{:S(2)}, u32[]{:S(2)}) collective-permute-start(bf16[8,3840]{1,0:T(8,128)(2,1)S(1)} %get-tuple-element.23), channel_id=1, source_target_pairs={{0,1},{1,0},{2,3},{3,2},{4,5},{5,4},{6,7},{7,6},{8,9},{9,8},{10,11... | collective-permute-start | bytes 184328 | tf_op jit(solution)/shard_map/ppermute | solution.py:528
  70.2 2.6 %collective-permute-start.7 = (bf16[8,3840]{1,0:T(8,128)(2,1)S(1)}, bf16[8,3840]{1,0:T(8,128)(2,1)S(1)}, u32[]{:S(2)}, u32[]{:S(2)}) collective-permute-start(bf16[8,3840]{1,0:T(8,128)(2,1)S(1)} %get-tuple-element.24), channel_id=1, source_target_pairs={{0,2},{1,3},{2,0},{3,1},{4,6},{5,7},{6,4},{7,5},{8,10},{9,11},{10,... | collective-permute-start | bytes 184328 | tf_op jit(solution)/shard_map/ppermute | solution.py:528
  72.8 0.2 collective-permute-start.8
  73.0 0.4 collective-permute-done.6.refs_0_
  73.5 3.2 %collective-permute-done.7.refs_1_ = bf16[8,3840]{1,0:T(8,128)(2,1)S(1)} collective-permute-done((bf16[8,3840]{1,0:T(8,128)(2,1)S(1)}, bf16[8,3840]{1,0:T(8,128)(2,1)S(1)}, u32[]{:S(2)}, u32[]{:S(2)}) %collective-permute-start.7) | collective-permute-done | bytes 61472 | tf_op jit(solution)/shard_map/ppermute | solution.py:528
  76.7 2.2 %collective-permute-done.8.refs_2_ = bf16[8,3840]{1,0:T(8,128)(2,1)S(1)} collective-permute-done((bf16[8,3840]{1,0:T(8,128)(2,1)S(1)}, bf16[8,3840]{1,0:T(8,128)(2,1)S(1)}, u32[]{:S(2)}, u32[]{:S(2)}) %collective-permute-start.8) | collective-permute-done | bytes 61472 | tf_op jit(solution)/shard_map/ppermute | solution.py:528
  78.8 0.2 sum_streams.1.refs_0_
  79.0 1.5 %collective-permute-start.11 = (bf16[8,3840]{1,0:T(8,128)(2,1)S(1)}, bf16[8,3840]{1,0:T(8,128)(2,1)S(1)}, u32[]{:S(2)}, u32[]{:S(2)}) collective-permute-start(bf16[8,3840]{1,0:T(8,128)(2,1)S(1)} %sum_streams.1.refs_0_), channel_id=1, source_target_pairs={{0,24},{4,28},{8,16},{12,20},{16,8},{20,12},{24,0},{28,4},{1,25},{... | collective-permute-start | bytes 184328 | tf_op jit(solution)/shard_map/ppermute | solution.py:530
  80.5 0.4 collective-permute-start.10
  80.9 1.7 %collective-permute-start.9 = (bf16[8,3840]{1,0:T(8,128)(2,1)S(1)}, bf16[8,3840]{1,0:T(8,128)(2,1)S(1)}, u32[]{:S(2)}, u32[]{:S(2)}) collective-permute-start(bf16[8,3840]{1,0:T(8,128)(2,1)S(1)} %sum_streams.1.refs_0_), channel_id=1, source_target_pairs={{0,8},{4,12},{8,0},{12,4},{16,24},{20,28},{24,16},{28,20},{1,9},{5... | collective-permute-start | bytes 184328 | tf_op jit(solution)/shard_map/ppermute | solution.py:530
  82.6 0.0 collective-permute-start.12
  82.6 1.6 %collective-permute-done.11.refs_3_ = bf16[8,3840]{1,0:T(8,128)(2,1)S(1)} collective-permute-done((bf16[8,3840]{1,0:T(8,128)(2,1)S(1)}, bf16[8,3840]{1,0:T(8,128)(2,1)S(1)}, u32[]{:S(2)}, u32[]{:S(2)}) %collective-permute-start.11) | collective-permute-done | bytes 61472 | tf_op jit(solution)/shard_map/ppermute | solution.py:530
  84.2 0.0 collective-permute-start.15
  84.2 0.6 collective-permute-done.10.refs_2_
  84.9 0.0 collective-permute-start.14
  84.9 0.3 collective-permute-done.9.refs_1_
  85.1 0.2 collective-permute-start.13
  85.4 0.0 collective-permute-done.12.refs_4_
  85.4 0.1 collective-permute-done.15.refs_7_
  85.4 0.7 collective-permute-done.14.refs_6_
  86.1 0.3 collective-permute-done.13.refs_5_
  86.4 1.7 %unpack.1 = (f32[3,3,64,256]{3,2,1,0:T(8,128)}, f32[64,1024]{1,0:T(8,128)}) custom-call(s32[4]{0:T(128)S(1)} %pad_add_fusion.place_ref, bf16[8,3840]{1,0:T(8,128)(2,1)S(1)} %sum_streams.1.refs_0_, bf16[8,3840]{1,0:T(8,128)(2,1)S(1)} %collective-permute-done.9.refs_1_, bf16[8,3840]{1,0:T(8,128)(2,1)S(1)} %collective-permute-done.10.refs_2_, ...), custom_call_target="tpu_custom_call" | custom-call | tf_op jit(solution)/shard_map/unpack/pallas_call | solution.py:505
Async XLA Ops:
  0.7 1.0 %copy-start = (bf16[256,1024]{1,0:T(8,128)(2,1)S(1)}, bf16[256,1024]{1,0:T(8,128)(2,1)}, u32[]{:S(2)}) copy-start(bf16[256,1024]{1,0:T(8,128)(2,1)} %head_hbm.1) | copy-start | bytes 1572868
  4.5 6.3 %collective-permute-start = (bf16[1296,256]{1,0:T(8,128)(2,1)S(1)}, bf16[1296,256]{1,0:T(8,128)(2,1)S(1)}, u32[]{:S(2)}, u32[]{:S(2)}) collective-permute-start(bf16[1296,256]{1,0:T(8,128)(2,1)S(1)} %get-tuple-element.14), channel_id=1, source_target_pairs={{0,4},{4,0},{8,12},{12,8},{16,20},{20,16},{24,28},{28,24},{1,5},{5... | collective-permute-start | bytes 1990664 | tf_op jit(solution)/shard_map/ppermute | solution.py:325
  5.0 5.8 %collective-permute-start.1 = (bf16[1296,256]{1,0:T(8,128)(2,1)S(1)}, bf16[1296,256]{1,0:T(8,128)(2,1)S(1)}, u32[]{:S(2)}, u32[]{:S(2)}) collective-permute-start(bf16[1296,256]{1,0:T(8,128)(2,1)S(1)} %get-tuple-element.15), channel_id=1, source_target_pairs={{4,8},{12,16},{20,24},{8,4},{16,12},{24,20},{5,9},{13,17},{21,25},... | collective-permute-start | bytes 1990664 | tf_op jit(solution)/shard_map/ppermute | solution.py:324
  32.5 16.8 %collective-permute-start.2 = (f32[4,32,3328]{2,1,0:T(8,128)}, f32[4,32,3328]{2,1,0:T(8,128)S(1)}, u32[]{:S(2)}, u32[]{:S(2)}) collective-permute-start(f32[4,32,3328]{2,1,0:T(8,128)} %get-tuple-element.17), channel_id=1, source_target_pairs={{0,4},{4,0},{8,12},{12,8},{16,20},{20,16},{24,28},{28,24},{1,5},{5... | collective-permute-start | bytes 5111816 | tf_op jit(solution)/shard_map/ppermute | solution.py:524
  49.3 1.5 %copy-start.1 = (f32[4,32,3328]{2,1,0:T(8,128)S(1)}, f32[4,32,3328]{2,1,0:T(8,128)}, u32[]{:S(2)}) copy-start(f32[4,32,3328]{2,1,0:T(8,128)} %get-tuple-element.16.keep_ref) | copy-start | bytes 5111812
  51.9 9.6 %collective-permute-start.3 = (bf16[4,8,3456]{2,1,0:T(8,128)(2,1)S(1)}, bf16[4,8,3456]{2,1,0:T(8,128)(2,1)S(1)}, u32[]{:S(2)}, u32[]{:S(2)}) collective-permute-start(bf16[4,8,3456]{2,1,0:T(8,128)(2,1)S(1)} %get-tuple-element.19), channel_id=1, source_target_pairs={{0,8},{4,12},{8,0},{12,4},{16,24},{20,28},{24,16},{28,20},{1,9},{5... | collective-permute-start | bytes 663560 | tf_op jit(solution)/shard_map/ppermute | solution.py:526
  55.3 12.2 %collective-permute-start.4 = (bf16[4,8,3456]{2,1,0:T(8,128)(2,1)S(1)}, bf16[4,8,3456]{2,1,0:T(8,128)(2,1)S(1)}, u32[]{:S(2)}, u32[]{:S(2)}) collective-permute-start(bf16[4,8,3456]{2,1,0:T(8,128)(2,1)S(1)} %get-tuple-element.20), channel_id=1, source_target_pairs={{0,16},{4,20},{8,24},{12,28},{16,0},{20,4},{24,8},{28,12},{1,17},{... | collective-permute-start | bytes 663560 | tf_op jit(solution)/shard_map/ppermute | solution.py:526
  55.9 11.6 %collective-permute-start.5 = (bf16[4,8,3456]{2,1,0:T(8,128)(2,1)S(1)}, bf16[4,8,3456]{2,1,0:T(8,128)(2,1)S(1)}, u32[]{:S(2)}, u32[]{:S(2)}) collective-permute-start(bf16[4,8,3456]{2,1,0:T(8,128)(2,1)S(1)} %get-tuple-element.21), channel_id=1, source_target_pairs={{0,24},{4,28},{8,16},{12,20},{16,8},{20,12},{24,0},{28,4},{1,25},{... | collective-permute-start | bytes 663560 | tf_op jit(solution)/shard_map/ppermute | solution.py:526
  68.6 4.9 %collective-permute-start.6 = (bf16[8,3840]{1,0:T(8,128)(2,1)S(1)}, bf16[8,3840]{1,0:T(8,128)(2,1)S(1)}, u32[]{:S(2)}, u32[]{:S(2)}) collective-permute-start(bf16[8,3840]{1,0:T(8,128)(2,1)S(1)} %get-tuple-element.23), channel_id=1, source_target_pairs={{0,1},{1,0},{2,3},{3,2},{4,5},{5,4},{6,7},{7,6},{8,9},{9,8},{10,11... | collective-permute-start | bytes 184328 | tf_op jit(solution)/shard_map/ppermute | solution.py:528
  70.2 6.4 %collective-permute-start.7 = (bf16[8,3840]{1,0:T(8,128)(2,1)S(1)}, bf16[8,3840]{1,0:T(8,128)(2,1)S(1)}, u32[]{:S(2)}, u32[]{:S(2)}) collective-permute-start(bf16[8,3840]{1,0:T(8,128)(2,1)S(1)} %get-tuple-element.24), channel_id=1, source_target_pairs={{0,2},{1,3},{2,0},{3,1},{4,6},{5,7},{6,4},{7,5},{8,10},{9,11},{10,... | collective-permute-start | bytes 184328 | tf_op jit(solution)/shard_map/ppermute | solution.py:528
  72.8 6.0 %collective-permute-start.8 = (bf16[8,3840]{1,0:T(8,128)(2,1)S(1)}, bf16[8,3840]{1,0:T(8,128)(2,1)S(1)}, u32[]{:S(2)}, u32[]{:S(2)}) collective-permute-start(bf16[8,3840]{1,0:T(8,128)(2,1)S(1)} %get-tuple-element.25), channel_id=1, source_target_pairs={{0,3},{1,2},{2,1},{3,0},{4,7},{5,6},{6,5},{7,4},{8,11},{9,10},{10,... | collective-permute-start | bytes 184328 | tf_op jit(solution)/shard_map/ppermute | solution.py:528
  79.0 5.2 %collective-permute-start.11 = (bf16[8,3840]{1,0:T(8,128)(2,1)S(1)}, bf16[8,3840]{1,0:T(8,128)(2,1)S(1)}, u32[]{:S(2)}, u32[]{:S(2)}) collective-permute-start(bf16[8,3840]{1,0:T(8,128)(2,1)S(1)} %sum_streams.1.refs_0_), channel_id=1, source_target_pairs={{0,24},{4,28},{8,16},{12,20},{16,8},{20,12},{24,0},{28,4},{1,25},{... | collective-permute-start | bytes 184328 | tf_op jit(solution)/shard_map/ppermute | solution.py:530
  80.5 4.3 %collective-permute-start.10 = (bf16[8,3840]{1,0:T(8,128)(2,1)S(1)}, bf16[8,3840]{1,0:T(8,128)(2,1)S(1)}, u32[]{:S(2)}, u32[]{:S(2)}) collective-permute-start(bf16[8,3840]{1,0:T(8,128)(2,1)S(1)} %sum_streams.1.refs_0_), channel_id=1, source_target_pairs={{0,16},{4,20},{8,24},{12,28},{16,0},{20,4},{24,8},{28,12},{1,17},{... | collective-permute-start | bytes 184328 | tf_op jit(solution)/shard_map/ppermute | solution.py:530
  80.9 4.2 %collective-permute-start.9 = (bf16[8,3840]{1,0:T(8,128)(2,1)S(1)}, bf16[8,3840]{1,0:T(8,128)(2,1)S(1)}, u32[]{:S(2)}, u32[]{:S(2)}) collective-permute-start(bf16[8,3840]{1,0:T(8,128)(2,1)S(1)} %sum_streams.1.refs_0_), channel_id=1, source_target_pairs={{0,8},{4,12},{8,0},{12,4},{16,24},{20,28},{24,16},{28,20},{1,9},{5... | collective-permute-start | bytes 184328 | tf_op jit(solution)/shard_map/ppermute | solution.py:530
  82.6 2.8 %collective-permute-start.12 = (bf16[8,3840]{1,0:T(8,128)(2,1)S(1)}, bf16[8,3840]{1,0:T(8,128)(2,1)S(1)}, u32[]{:S(2)}, u32[]{:S(2)}) collective-permute-start(bf16[8,3840]{1,0:T(8,128)(2,1)S(1)} %sum_streams.1.refs_0_), channel_id=1, source_target_pairs={{0,4},{4,0},{8,12},{12,8},{16,20},{20,16},{24,28},{28,24},{1,5},{5... | collective-permute-start | bytes 184328 | tf_op jit(solution)/shard_map/ppermute | solution.py:531
  84.2 1.2 %collective-permute-start.15 = (bf16[8,3840]{1,0:T(8,128)(2,1)S(1)}, bf16[8,3840]{1,0:T(8,128)(2,1)S(1)}, u32[]{:S(2)}, u32[]{:S(2)}) collective-permute-start(bf16[8,3840]{1,0:T(8,128)(2,1)S(1)} %collective-permute-done.11.refs_3_), channel_id=1, source_target_pairs={{0,4},{4,0},{8,12},{12,8},{16,20},{20,16},{24,28},{28,24},{1,5},{5... | collective-permute-start | bytes 184328 | tf_op jit(solution)/shard_map/ppermute | solution.py:531
  84.9 1.2 %collective-permute-start.14 = (bf16[8,3840]{1,0:T(8,128)(2,1)S(1)}, bf16[8,3840]{1,0:T(8,128)(2,1)S(1)}, u32[]{:S(2)}, u32[]{:S(2)}) collective-permute-start(bf16[8,3840]{1,0:T(8,128)(2,1)S(1)} %collective-permute-done.10.refs_2_), channel_id=1, source_target_pairs={{0,4},{4,0},{8,12},{12,8},{16,20},{20,16},{24,28},{28,24},{1,5},{5... | collective-permute-start | bytes 184328 | tf_op jit(solution)/shard_map/ppermute | solution.py:531
  85.1 1.2 %collective-permute-start.13 = (bf16[8,3840]{1,0:T(8,128)(2,1)S(1)}, bf16[8,3840]{1,0:T(8,128)(2,1)S(1)}, u32[]{:S(2)}, u32[]{:S(2)}) collective-permute-start(bf16[8,3840]{1,0:T(8,128)(2,1)S(1)} %collective-permute-done.9.refs_1_), channel_id=1, source_target_pairs={{0,4},{4,0},{8,12},{12,8},{16,20},{20,16},{24,28},{28,24},{1,5},{5... | collective-permute-start | bytes 184328 | tf_op jit(solution)/shard_map/ppermute | solution.py:531

commit v4 on v3

--- a/solution.py
+++ b/solution.py
@@ -18,6 +18,7 @@
 GROUPS = ((0, 3 * W), (3 * W, 6 * W), (6 * W, 9 * W), (9 * W, SUM_LANES))
 CODE_LANES = SUM_LANES + 128 * 4
 VMEM_LIMIT = 52 * 2**20
+KERNEL_LIMIT = 10 * 2**20
 BASE = 125.0 * math.log(2.0)
 SPAN = 250.0 * math.log(2.0)
 
@@ -59,9 +60,11 @@
         body(frame, tile)
 
 
-def edges_kernel(place_ref, clip_hbm, target_hbm, head_ref, near_ref, far_ref, goal_ref, sem):
+def edges_kernel(place_ref, clip_hbm, target_hbm, head_hbm, near_ref, far_ref, goal_ref, head_ref, sem):
     count = clip_hbm.shape[0]
     even = place_ref[0] % 2 == 0
+    head_load = pltpu.make_async_copy(head_hbm, head_ref, sem.at[4])
+    head_load.start()
     loads = []
     for side, (edge_ref, flag) in enumerate(((near_ref, even), (far_ref, jnp.logical_not(even)))):
         for rows, source, target in (
@@ -71,11 +74,13 @@
             start = pl.multiple_of(jnp.where(flag, count - rows, 0), 16)
             loads.append(pltpu.make_async_copy(source.at[pl.ds(start, rows)], target, sem.at[len(loads)]))
             loads[-1].start()
+    head_load.wait()
     for side, edge_ref in enumerate((near_ref, far_ref)):
         loads[2 * side].wait()
-        high, low = split(dot_nt(goal_ref[side * BACK : (side + 1) * BACK], head_ref[...]))
-        edge_ref[HALO : HALO + BACK] = high
-        edge_ref[HALO + BACK :] = low
+        goal = dot_nt(goal_ref[side * BACK : (side + 1) * BACK], head_ref[...])
+        codes, most = encode([goal[row : row + 16] for row in range(0, BACK, 16)])
+        edge_ref[HALO : HALO + BACK] = jnp.concatenate(codes, axis=0)
+        edge_ref[HALO + BACK :] = most
     for load in loads[1::2]:
         load.wait()
 
@@ -84,238 +89,291 @@
     anywhere = pl.BlockSpec(memory_space=pl.ANY)
     return pl.pallas_call(
         edges_kernel,
-        in_specs=[smem(), anywhere, anywhere, whole()],
+        in_specs=[smem()] + [anywhere] * 3,
         out_specs=[whole()] * 2,
-        out_shape=[jax.ShapeDtypeStruct((HALO + 2 * BACK, W), jnp.bfloat16)] * 2,
-        scratch_shapes=[pltpu.VMEM((2 * BACK, FEAT), jnp.bfloat16), pltpu.SemaphoreType.DMA((4,))],
+        out_shape=[jax.ShapeDtypeStruct((HALO + BACK + 16, W), jnp.bfloat16)] * 2,
+        scratch_shapes=[
+            pltpu.VMEM((2 * BACK, FEAT), jnp.bfloat16),
+            pltpu.VMEM(head_weight.shape, jnp.bfloat16),
+            pltpu.SemaphoreType.DMA((5,)),
+        ],
         compiler_params=pltpu.CompilerParams(vmem_limit_bytes=VMEM_LIMIT),
         name="edges",
-    )(place, clip, target, head_weight)
-
-
-def project_kernel(target_ref, head_ref, out_ref):
-    out_ref[...] = dot_nt(target_ref[...], head_ref[...])
-
-
-def project(target, head_weight):
-    count = target.shape[0]
-    tile = tile_of(count, 512)
-    return pl.pallas_call(
-        project_kernel,
-        grid=(count // tile,),
-        in_specs=[
-            pl.BlockSpec((tile, FEAT), lambda i: (i, 0)),
-            pl.BlockSpec((W, FEAT), lambda i: (0, 0)),
-        ],
-        out_specs=pl.BlockSpec((tile, W), lambda i: (i, 0)),
-        out_shape=jax.ShapeDtypeStruct((count, W), jnp.float32),
-        compiler_params=pltpu.CompilerParams(vmem_limit_bytes=VMEM_LIMIT),
-        cost_estimate=pl.CostEstimate(
-            flops=2 * count * W * FEAT, bytes_accessed=count * (2 * FEAT + 4 * W), transcendentals=0
-        ),
-        name="project_targets",
-    )(target, head_weight)
-
-
-def main_kernel(
-    count,
-    place_ref,
-    clip_ref,
-    near_ref,
-    far_ref,
-    target_hbm,
-    proj_ref,
-    conv_hbm,
-    head_hbm,
-    keep_ref,
-    send_ref,
-    h0,
-    h1,
-    h2,
-    h3,
-    s1,
-    s2,
-    s3,
-    err,
-    back,
-    conv_t,
-    gram,
-    head_acc,
-    sums,
-    conv_ref,
-    head_ref,
-    target_ref,
-    goals,
-    in_sem,
-    out_sem,
-):
-    first = place_ref[0] == 0
-    last = place_ref[0] == place_ref[1] - 1
-    even = place_ref[0] % 2 == 0
-    hidden = (h0, h1, h2, h3)
-    slopes = (None, s1, s2, s3)
-
-    def at(frame, size):
-        return slice(frame + HALO, frame + HALO + size)
-
-    def inside(frame, size):
+    )(place, clip, target, pltpu.with_memory_space_constraint(head_weight, pltpu.HBM))
+
+
+FORWARD_EDGES = (64, 128, 384)
+BACK_EDGES = {2: 384, 1: 640, 0: 704}
+STATE = ("h0", "h1", "h2", "h3", "s1", "s2", "s3", "err", "back3", "back2", "sums", "goal_acc", "square")
+FIXED = ("conv", "conv_t", "head", "gram")
+
+
+def state_shapes(count):
+    rows = count + 2 * HALO
+    shapes = {name: ((rows, W), jnp.bfloat16) for name in ("h0", "h1", "h2", "h3")}
+    shapes |= {name: ((rows, W), jnp.float32) for name in ("s1", "s2", "s3", "err")}
+    shapes |= {name: ((rows, 2 * W), jnp.bfloat16) for name in ("back3", "back2")}
+    shapes |= {
+        "sums": ((W, SUM_LANES), jnp.float32),
+        "goal_acc": ((W, FEAT), jnp.float32),
+        "square": ((W, W), jnp.float32),
+        "conv": ((3, 3, W, W), jnp.bfloat16),
+        "conv_t": ((2, 6 * W, W), jnp.bfloat16),
+        "head": ((W, FEAT), jnp.bfloat16),
+        "gram": ((2 * W, W), jnp.bfloat16),
+    }
+    return {name: jax.ShapeDtypeStruct(*shape) for name, shape in shapes.items()}
+
+
+def at(frame, size):
+    return slice(frame + HALO, frame + HALO + size)
+
+
+class Block:
+    def __init__(self, count, place_ref, refs, back1, inner):
+        self.count, self.refs, self.inner = count, refs, inner
+        self.first = place_ref[0] == 0
+        self.last = place_ref[0] == place_ref[1] - 1
+        self.backs = {2: refs["back3"], 1: refs["back2"], 0: back1}
+
+    def spans(self, reach, edge):
+        if self.inner:
+            return [(edge, self.count - edge)]
+        return [(-reach, edge), (self.count - edge, self.count + reach)]
+
+    def loop(self, reach, edge, body):
+        for start, stop in self.spans(reach, edge):
+            loop_rows(start, stop, 448, body)
+
+    def masked(self, frame, size, value):
+        if frame >= 0 and frame + size <= self.count:
+            return value
         rows = lax.broadcasted_iota(jnp.int32, (size, 1), 0) + frame
-        return ((rows >= 0) | jnp.logical_not(first)) & ((rows < count) | jnp.logical_not(last))
-
-    def masked(frame, size, value):
-        if frame >= 0 and frame + size <= count:
-            return value
-        return jnp.where(inside(frame, size), value, 0.0)
-
-    above = pl.multiple_of(jnp.where(even, HALO + count, 0), 16)
-    below = pl.multiple_of(jnp.where(even, 0, HALO + count), 16)
-    err_above = pl.multiple_of(jnp.where(even, HALO + count, HALO - BACK), 16)
-    err_below = pl.multiple_of(jnp.where(even, HALO - BACK, HALO + count), 16)
-    loads = [
-        (conv_hbm.at[0], conv_ref.at[0]),
-        (clip_ref, h0.at[HALO : HALO + count]),
-        (near_ref.at[0:HALO], h0.at[pl.ds(above, HALO)]),
-        (far_ref.at[0:HALO], h0.at[pl.ds(below, HALO)]),
-        (conv_hbm.at[1:3], conv_ref.at[1:3]),
-        (head_hbm, head_ref),
-        (proj_ref, err.at[HALO : HALO + count]),
-        (near_ref.at[HALO:], goals.at[0]),
-        (far_ref.at[HALO:], goals.at[1]),
-        (target_hbm, target_ref),
-    ]
-    loads = [pltpu.make_async_copy(*load, in_sem.at[i]) for i, load in enumerate(loads)]
-    for load in loads:
-        load.start()
-
-    half = keep_ref.shape[1]
-    stores = []
-
-    def store(first_lane, lanes):
-        for pen in range(keep_ref.shape[0]):
-            for side, target in enumerate((keep_ref, send_ref)):
-                start = pl.multiple_of((2 * pen + (place_ref[0] + side) % 2) * half, 8)
-                copy = pltpu.make_async_copy(
-                    sums.at[pl.ds(start, half), first_lane : first_lane + lanes],
-                    target.at[pen, :, first_lane : first_lane + lanes],
-                    out_sem.at[len(stores)],
-                )
-                copy.start()
-                stores.append(copy)
-
-    for load in loads[:4]:
-        load.wait()
-    reach = HALO
-    for layer in range(3):
+        inside = (rows >= 0) | jnp.logical_not(self.first)
+        inside = inside & ((rows < self.count) | jnp.logical_not(self.last))
+        return jnp.where(inside, value, 0.0)
+
+    def forward(self, layer):
         width = DILATIONS[layer]
-        reach -= width
-        source, result, slope = hidden[layer], hidden[layer + 1], slopes[layer + 1]
-        weights = conv_ref[layer].reshape(3 * W, W)
-
-        def forward(frame, size):
+        source, result = self.refs[f"h{layer}"], self.refs[f"h{layer + 1}"]
+        slope = self.refs[f"s{layer + 1}"]
+        weights = self.refs["conv"][layer].reshape(3 * W, W)
+
+        def body(frame, size):
             taps = [source[at(frame + (k - 1) * width, size), :] for k in range(3)]
             pre = dot(jnp.concatenate(taps, axis=1), weights)
             sig = 0.5 * jnp.tanh(0.5 * pre) + 0.5
             new = taps[1].astype(jnp.float32) + pre * sig
-            result[at(frame, size), :] = masked(frame, size, new).astype(jnp.bfloat16)
+            result[at(frame, size), :] = self.masked(frame, size, new).astype(jnp.bfloat16)
             slope[at(frame, size), :] = sig * (1.0 + pre * (1.0 - sig))
 
-        loop_rows(-reach, count + reach, 416, forward)
-        if layer == 0:
-            loads[4].wait()
-            for turn in (1, 2):
-                for k in range(3):
-                    turned = jnp.transpose(conv_ref[turn, k])
-                    conv_t[turn - 1, 2 * k * W : (2 * k + 1) * W, :] = turned
-                    conv_t[turn - 1, (2 * k + 1) * W : (2 * k + 2) * W, :] = turned
-
-    def store_back(frame, size, error, slope):
-        high, low = split(error * slope[at(frame, size), :])
-        back[at(frame, size), 0:W] = high
-        back[at(frame, size), W : 2 * W] = low
-
-    def head_error(frame, size):
-        top = h3[at(frame, size), :]
-        error = SCALE * (dot(jnp.concatenate([top, top], axis=1), gram[...]) - err[at(frame, size), :])
-        err[at(frame, size), :] = error
-        store_back(frame, size, error, s3)
-
-    for load in loads[5:9]:
+        self.loop(HALO - sum(DILATIONS[: layer + 1]), FORWARD_EDGES[layer], body)
+
+    def store_back(self, layer, frame, size, error):
+        high, low = split(error * self.refs[f"s{layer + 1}"][at(frame, size), :])
+        where = at(frame, size) if layer > 0 else slice(frame, frame + size)
+        self.backs[layer][where, 0:W] = high
+        self.backs[layer][where, W : 2 * W] = low
+
+    def head_error(self):
+        err = self.refs["err"]
+
+        def body(frame, size):
+            top = self.refs["h3"][at(frame, size), :]
+            product = dot(jnp.concatenate([top, top], axis=1), self.refs["gram"][...])
+            error = SCALE * (product - err[at(frame, size), :])
+            err[at(frame, size), :] = error
+            self.store_back(2, frame, size, error)
+
+        self.loop(BACK, BACK_EDGES[2], body)
+
+    def add(self, ref, lanes, value, fresh):
+        if fresh:
+            ref[:, lanes] = value
+        else:
+            ref[:, lanes] += value
+
+    def head_sums(self):
+        goal_at = 0
+        for start, stop in self.spans(0, BACK_EDGES[2]):
+            goal_at = start if self.inner else goal_at
+            goal = self.refs["target"][goal_at : goal_at + stop - start, :]
+            goal_at += stop - start
+            top = self.refs["h3"][at(start, stop - start), :]
+            every = slice(None)
+            self.add(self.refs["goal_acc"], every, dot_tn(top, goal), self.inner)
+            self.add(self.refs["square"], every, dot_tn(top, top), self.inner)
+
+    def weight_sums(self, layer):
+        width = DILATIONS[layer]
+        for start, stop in self.spans(0, BACK_EDGES[layer]):
+            size = stop - start
+            where = at(start, size) if layer > 0 else slice(start, stop)
+            right = self.backs[layer][where, :]
+            for k in range(3):
+                both = dot_tn(self.refs[f"h{layer}"][at(start + (k - 1) * width, size), :], right)
+                first = (3 * layer + k) * W
+                self.add(self.refs["sums"], slice(first, first + W), both[:, 0:W] + both[:, W:], self.inner)
+
+    def pull_back(self, layer):
+        width = DILATIONS[layer]
+        err = self.refs["err"]
+
+        def pull(frame, size):
+            taps = [self.backs[layer][at(frame - (k - 1) * width, size), :] for k in range(3)]
+            error = err[at(frame, size), :] + dot(jnp.concatenate(taps, axis=1), self.refs["conv_t"][layer - 1])
+            err[at(frame, size), :] = error
+            self.store_back(layer - 1, frame, size, self.masked(frame, size, error))
+
+        self.loop(BACK - sum(DILATIONS[layer:]), BACK_EDGES[layer - 1], pull)
+
+
+def inner_kernel(count, place_ref, clip_hbm, target_hbm, conv_hbm, head_hbm, *rest):
+    names = STATE + FIXED
+    refs = dict(zip(names, rest[: len(names)]))
+    back1, refs["target"], sem = rest[len(names) :]
+    loads = [
+        (conv_hbm.at[0], refs["conv"].at[0]),
+        (clip_hbm, refs["h0"].at[HALO : HALO + count]),
+        (conv_hbm.at[1:3], refs["conv"].at[1:3]),
+        (head_hbm, refs["head"]),
+        (target_hbm, refs["target"]),
+    ]
+    loads = [pltpu.make_async_copy(*load, sem.at[i]) for i, load in enumerate(loads)]
+    for load in loads:
+        load.start()
+    block = Block(count, place_ref, refs, back1, True)
+    loads[0].wait()
+    loads[1].wait()
+    block.forward(0)
+    loads[2].wait()
+    block.forward(1)
+    block.forward(2)
+    for layer in (1, 2):
+        for k in range(3):
+            turned = jnp.transpose(refs["conv"][layer, k])
+            refs["conv_t"][layer - 1, 2 * k * W : (2 * k + 1) * W, :] = turned
+            refs["conv_t"][layer - 1, (2 * k + 1) * W : (2 * k + 2) * W, :] = turned
+    loads[3].wait()
+    high, low = split(dot_nt(refs["head"][...], refs["head"][...]))
+    refs["gram"][0:W, :] = high
+    refs["gram"][W : 2 * W, :] = low
+    loads[4].wait()
+
+    def project(frame, size):
+        refs["err"][at(frame, size), :] = dot_nt(refs["target"][frame : frame + size, :], refs["head"][...])
+
+    loop_rows(0, count, 512, project)
+    block.head_error()
+    block.head_sums()
+    block.weight_sums(2)
+    block.pull_back(2)
+    block.weight_sums(1)
+    block.pull_back(1)
+    block.weight_sums(0)
+
+
+def inner(place, clip, target, conv_weight, head_weight):
+    count = clip.shape[0]
+    shapes = state_shapes(count)
+    names = STATE + FIXED
+    anywhere = pl.BlockSpec(memory_space=pl.ANY)
+    results = pl.pallas_call(
+        functools.partial(inner_kernel, count),
+        in_specs=[smem()] + [anywhere] * 4,
+        out_specs=[whole()] * len(names),
+        out_shape=[shapes[name] for name in names],
+        scratch_shapes=[
+            pltpu.VMEM((count, 2 * W), jnp.bfloat16),
+            pltpu.VMEM((count, FEAT), jnp.bfloat16),
+            pltpu.SemaphoreType.DMA((5,)),
+        ],
+        compiler_params=pltpu.CompilerParams(vmem_limit_bytes=KERNEL_LIMIT),
+        cost_estimate=pl.CostEstimate(flops=2 * W * W * 60 * count, bytes_accessed=8 * 2**20, transcendentals=0),
+        name="inner_frames",
+    )(place, *[pltpu.with_memory_space_constraint(x, pltpu.HBM) for x in (clip, target, conv_weight, head_weight)])
+    return dict(zip(names, results))
+
+
+def ends_kernel(count, place_ref, target_hbm, near_ref, far_ref, *rest):
+    fixed = dict(zip(FIXED, rest[: len(FIXED)]))
+    rest = rest[len(FIXED) + len(STATE) :]
+    keep_ref, send_ref = rest[:2]
+    refs = fixed | dict(zip(STATE, rest[2 : 2 + len(STATE)]))
+    back1, refs["target"], in_sem = rest[2 + len(STATE) :]
+    even = place_ref[0] % 2 == 0
+    sums = refs["sums"]
+    edge = BACK_EDGES[2]
+    loads = [
+        pltpu.make_async_copy(
+            target_hbm.at[start : start + edge], refs["target"].at[i * edge : (i + 1) * edge], in_sem.at[i]
+        )
+        for i, start in enumerate((0, count - edge))
+    ]
+    for load in loads:
+        load.start()
+    for edge_ref, above in ((near_ref, even), (far_ref, jnp.logical_not(even))):
+        start = pl.multiple_of(jnp.where(above, HALO + count, 0), 16)
+        refs["h0"][pl.ds(start, HALO), :] = edge_ref[0:HALO, :]
+        start = pl.multiple_of(jnp.where(above, HALO + count, HALO - BACK), 16)
+        most = edge_ref[HALO + BACK :, :]
+        for row in range(0, BACK, 16):
+            code = edge_ref[HALO + row : HALO + row + 16, :]
+            goal = jnp.where(code == 0.0, 0.0, decode(code, most))
+            refs["err"][pl.ds(pl.multiple_of(start + row, 16), 16), :] = goal
+
+    half = keep_ref.shape[1]
+
+    def store(first_lane, lanes):
+        part = slice(first_lane, first_lane + lanes)
+        for pen in range(keep_ref.shape[0]):
+            for side, target in enumerate((keep_ref, send_ref)):
+                start = pl.multiple_of((2 * pen + (place_ref[0] + side) % 2) * half, 8)
+                target[pen, :, part] = sums[pl.ds(start, half), part]
+
+    block = Block(count, place_ref, refs, back1, False)
+    for layer in range(3):
+        block.forward(layer)
+    block.head_error()
+    for load in loads:
         load.wait()
-    for side, start in enumerate((err_above, err_below)):
-        high, low = goals[side, 0:BACK, :], goals[side, BACK:, :]
-        err[pl.ds(start, BACK), :] = high.astype(jnp.float32) + low.astype(jnp.float32)
-    high, low = split(dot_nt(head_ref[...], head_ref[...]))
-    gram[0:W, :] = high
-    gram[W : 2 * W, :] = low
-    loop_rows(-BACK, count + BACK, 416, head_error)
-
-    loads[9].wait()
-    top = h3[at(0, count), :]
-    head_acc[...] = dot_tn(top, target_ref[...])
-    square = dot_tn(top, top)
+    block.head_sums()
+    square = refs["square"][...]
     high = square.astype(jnp.bfloat16)
     middle, low = split(square - high.astype(jnp.float32))
-    weight = head_ref[...]
+    weight = refs["head"][...]
     product = dot(high, weight) + (dot(middle, weight) + dot(low, weight))
-    sums[:, 9 * W :] = SCALE * (product - head_acc[...])
+    sums[:, 9 * W :] = SCALE * (product - refs["goal_acc"][...])
     store(9 * W, FEAT)
-
-    reach = BACK
     for layer in (2, 1, 0):
-        width = DILATIONS[layer]
-        source = hidden[layer]
-        first_lane = 3 * layer * W
-        right = back[at(0, count), :]
-        for k in range(3):
-            both = dot_tn(source[at((k - 1) * width, count), :], right)
-            sums[:, first_lane + k * W : first_lane + (k + 1) * W] = both[:, 0:W] + both[:, W:]
-        store(first_lane, 3 * W)
+        block.weight_sums(layer)
+        store(3 * layer * W, 3 * W)
         if layer > 0:
-            reach -= width
-
-            def pull_back(frame, size):
-                taps = [back[at(frame - (k - 1) * width, size), :] for k in range(3)]
-                err[at(frame, size), :] += dot(jnp.concatenate(taps, axis=1), conv_t[layer - 1])
-
-            loop_rows(-reach, count + reach, 416, pull_back)
-
-            def slope_back(frame, size):
-                error = masked(frame, size, err[at(frame, size), :])
-                store_back(frame, size, error, slopes[layer])
-
-            loop_rows(-reach, count + reach, 416, slope_back)
-    for copy in stores:
-        copy.wait()
-
-
-def main(pens, place, clip, near, far, target, proj, conv_weight, head_weight):
-    count = clip.shape[0]
-    rows = count + 2 * HALO
-    flops = 2 * W * W * (9 * rows + 14 * rows + 18 * count + 6 * count)
-    return pl.pallas_call(
-        functools.partial(main_kernel, count),
-        in_specs=[smem()] + [pl.BlockSpec(memory_space=pl.ANY)] * 7,
-        out_specs=[pl.BlockSpec(memory_space=pl.ANY)] * 2,
-        out_shape=[jax.ShapeDtypeStruct((pens, W // (2 * pens), SUM_LANES), jnp.float32)] * 2,
-        scratch_shapes=[pltpu.VMEM((rows, W), jnp.bfloat16)] * 4
-        + [pltpu.VMEM((rows, W), jnp.float32)] * 4
-        + [
-            pltpu.VMEM((rows, 2 * W), jnp.bfloat16),
-            pltpu.VMEM((2, 6 * W, W), jnp.bfloat16),
-            pltpu.VMEM((2 * W, W), jnp.bfloat16),
-            pltpu.VMEM((W, FEAT), jnp.float32),
-            pltpu.VMEM((W, SUM_LANES), jnp.float32),
-            pltpu.VMEM(conv_weight.shape, jnp.bfloat16),
-            pltpu.VMEM(head_weight.shape, jnp.bfloat16),
-            pltpu.VMEM(target.shape, jnp.bfloat16),
-            pltpu.VMEM((2, 2 * BACK, W), jnp.bfloat16),
-            pltpu.SemaphoreType.DMA((10,)),
-            pltpu.SemaphoreType.DMA((8 * pens,)),
+            block.pull_back(layer)
+
+
+def ends(pens, place, target, near_edge, far_edge, state):
+    count = target.shape[0]
+    shapes = state_shapes(count)
+    sent = jax.ShapeDtypeStruct((pens, W // (2 * pens), SUM_LANES), jnp.float32)
+    inputs = [near_edge, far_edge] + [state[name] for name in FIXED + STATE]
+    first = 4 + len(FIXED)
+    results = pl.pallas_call(
+        functools.partial(ends_kernel, count),
+        in_specs=[smem(), pl.BlockSpec(memory_space=pl.ANY)] + [whole()] * len(inputs),
+        out_specs=[whole()] * (2 + len(STATE)),
+        out_shape=[sent, sent] + [shapes[name] for name in STATE],
+        input_output_aliases={first + i: 2 + i for i in range(len(STATE))},
+        scratch_shapes=[
+            pltpu.VMEM((count, 2 * W), jnp.bfloat16),
+            pltpu.VMEM((2 * BACK_EDGES[2], FEAT), jnp.bfloat16),
+            pltpu.SemaphoreType.DMA((2,)),
         ],
-        compiler_params=pltpu.CompilerParams(vmem_limit_bytes=VMEM_LIMIT),
-        cost_estimate=pl.CostEstimate(flops=flops, bytes_accessed=16 * 2**20, transcendentals=3 * rows * W),
-        name="forward_backward",
-    )(place, clip, near, far, target, proj, conv_weight, head_weight)
+        compiler_params=pltpu.CompilerParams(vmem_limit_bytes=KERNEL_LIMIT),
+        cost_estimate=pl.CostEstimate(flops=2 * W * W * 60 * count, bytes_accessed=2**20, transcendentals=0),
+        name="end_frames",
+    )(place, pltpu.with_memory_space_constraint(target, pltpu.HBM), *near(inputs))
+    return results[:2]
 
 
 def swap(near, far):
@@ -535,9 +593,9 @@
     clip, target = clips[0], targets[0]
     count, pens = lax.axis_size("tm"), lax.axis_size("pen")
     place = jnp.stack([lax.axis_index("tm"), count, lax.axis_index("pen"), pens]).astype(jnp.int32)
-    near, far = swap(*edges(place, clip, target, head_weight))
-    proj = project(target, head_weight)
-    keep, send = main(pens, place, clip, near, far, target, proj, conv_weight, head_weight)
+    near_edge, far_edge = swap(*edges(place, clip, target, head_weight))
+    state = inner(place, clip, target, conv_weight, head_weight)
+    keep, send = ends(pens, place, target, near_edge, far_edge, state)
     return reduce_sums(place, keep, send)
 
 

time: 88.4 us -> 73.8 us (0.83)
  starting transfers between devices: 27.7 us -> 17.1 us
  local copies, waits for them, and re-layouts: 2.5 us -> 0 us
  Pallas kernels: 33.7 us -> 32.5 us
    ppermute x1, starting transfers between devices: 13.3 us -> 3.89 us  [reduce_sums(): other = lax.ppermute(send, 'tm', sibling)]
    unnamed x4 -> x0, local copies, waits for them, and re-layouts: 2.5 us -> none
    pallas_call x3, Pallas kernels: 29.5 us -> 28.4 us  [the longest x1 13 us: ends(): pl.pallas_call(functools.partial(ends_kernel, count), in_specs=[smem(), p...]
    ppermute x3, starting transfers between devices: 4.91 us -> 3.78 us  [reduce_sums(): lax.ppermute(code, 'tm', pairs)]
  transfers between devices with their start and end apart: 16 -> 16, of which waited for: 12 -> 12; matrix products, arithmetic and copies ran while one was open for 0% -> 0% of each run, Pallas kernels for 6% -> 17%
where the time goes in v4:
time: 73.8 us; the launch traced here: 73.6 us
  Pallas kernels  32.5 us (44%)
  waiting for transfers between devices  23.2 us (31%)
  starting transfers between devices  17.1 us (23%)
    pallas_call x1, Pallas kernels, ends(): pl.pallas_call(functools.partial(ends_kernel, count), in_specs=[smem(), p...  13 us
    pallas_call x1, Pallas kernels, inner(): pl.pallas_call(functools.partial(inner_kernel, count), in_specs=[smem()]...  12.3 us
    ppermute x3, waiting for transfers between devices, reduce_sums(): lax.ppermute(code, 'tm', pairs)  10.6 us
    ppermute x3, waiting for transfers between devices, reduce_sums(): lax.ppermute(code, 'pen', pairs)  5.8 us
    ppermute x3, starting transfers between devices, reduce_sums(): lax.ppermute(code, 'pen', pairs)  4.45 us
    ppermute x1, starting transfers between devices, reduce_sums(): other = lax.ppermute(send, 'tm', sibling)  3.89 us
    ppermute x3, starting transfers between devices, reduce_sums(): lax.ppermute(code, 'tm', pairs)  3.78 us
    ppermute x3, starting transfers between devices, reduce_sums(): half = [code] + [lax.ppermute(code, 'tm', pairs) for pairs in chips]  3.55 us
  transfers between devices with their start and end apart: 16, of which 12 were waited for; matrix products, arithmetic and copies ran while one was open for 0% of the time, Pallas kernels for 17%

profile of v4, /device:TPU:0, one launch (start us, length us, event | category | flops | bytes accessed | tf_op | source)
XLA Modules:
  0.0 73.6 jit_solution(4751040488341539567)
XLA Ops:
  0.6 0.1 pad_add_fusion.place_ref
  0.7 3.1 %edges.1 = (bf16[992,256]{1,0:T(8,128)(2,1)S(1)}, bf16[992,256]{1,0:T(8,128)(2,1)S(1)}) custom-call(s32[4]{0:T(128)S(1)} %pad_add_fusion.place_ref, bf16[2048,256]{1,0:T(8,128)(2,1)} %bitcast.7, bf16[2048,1024]{1,0:T(8,128)(2,1)} %bitcast.4, bf16[256,1024]{1,0:T(8,128)(2,1)} %head_hbm.3), custom_call_target="tpu_custom_call" | custom-call | tf_op jit(solution)/shard_map/edges/pallas_call | solution.py:90
  3.8 0.5 collective-permute-start
  4.3 0.7 collective-permute-start.1
  5.0 12.3 %inner_frames.1 = (bf16[3360,256]{1,0:T(8,128)(2,1)S(1)}, bf16[3360,256]{1,0:T(8,128)(2,1)S(1)}, bf16[3360,256]{1,0:T(8,128)(2,1)S(1)}, bf16[3360,256]{1,0:T(8,1...) custom-call(s32[4]{0:T(128)S(1)} %pad_add_fusion.place_ref, ...), custom_call_target="tpu_custom_call" | custom-call | flops 16106127360 | bytes 8388608 | tf_op jit(solution)/shard_map/inner_frames/pallas_call | solution.py:281
  17.3 0.0 collective-permute-done.near_ref
  17.3 0.0 collective-permute-done.1.far_ref
  17.3 13.0 %end_frames.1 = (f32[4,32,3328]{2,1,0:T(8,128)S(1)}, f32[4,32,3328]{2,1,0:T(8,128)S(1)}, bf16[3360,256]{1,0:T(8,128)(2,1)S(1)}, bf16[3360,256]{1,0:T(8,128)(2,1)...) custom-call(s32[4]{0:T(128)S(1)} %pad_add_fusion.place_ref, ...), custom_call_target="tpu_custom_call", output_to_operand_aliasing={{2}: (8, {}), {3}: (9, {}), {4}: (10, {}), {5}: (11, {}), {... | custom-call | flops 16106127360 | bytes 1048576 | tf_op jit(solution)/shard_map/end_frames/pallas_call | solution.py:361
  30.4 3.9 %collective-permute-start.2 = (f32[4,32,3328]{2,1,0:T(8,128)S(1)}, f32[4,32,3328]{2,1,0:T(8,128)S(1)}, u32[]{:S(2)}, u32[]{:S(2)}) collective-permute-start(f32[4,32,3328]{2,1,0:T(8,128)S(1)} %get-tuple-element.51), channel_id=1, source_target_pairs={{0,4},{4,0},{8,12},{12,8},{16,20},{20,16},{24,28},{28,24},{1,5},{5... | collective-permute-start | bytes 5111816 | tf_op jit(solution)/shard_map/ppermute | solution.py:582
  34.2 3.2 %collective-permute-done.2.other_ref = f32[4,32,3328]{2,1,0:T(8,128)S(1)} collective-permute-done((f32[4,32,3328]{2,1,0:T(8,128)S(1)}, f32[4,32,3328]{2,1,0:T(8,128)S(1)}, u32[]{:S(2)}, u32[]{:S(2)}) %collective-permute-start.2) | collective-permute-done | bytes 1703968 | tf_op jit(solution)/shard_map/ppermute | solution.py:582
  37.5 1.2 %sum_cores.1 = (f32[4,8,3328]{2,1,0:T(8,128)S(1)}, bf16[4,8,3456]{2,1,0:T(8,128)(2,1)S(1)}, bf16[4,8,3456]{2,1,0:T(8,128)(2,1)S(1)}, bf16[4,8,3456]{2,1,0:T(8,128)(2,1)S(1)}) custom-call(s32[4]{0:T(128)S(1)} %pad_add_fusion.place_ref, f32[4,32,3328]{2,1,0:T(8,128)S(1)} %get-tuple-element.50.keep_ref, f32[4,32,3328]{2,1,0:T(8,128)S(1)} %collective-permute-done.2.other_ref), custom_call_target="tpu_custom_call" | custom-call | tf_op jit(solution)/shard_map/sum_cores/pallas_call | solution.py:524
  38.6 2.2 %collective-permute-start.3 = (bf16[4,8,3456]{2,1,0:T(8,128)(2,1)S(1)}, bf16[4,8,3456]{2,1,0:T(8,128)(2,1)S(1)}, u32[]{:S(2)}, u32[]{:S(2)}) collective-permute-start(bf16[4,8,3456]{2,1,0:T(8,128)(2,1)S(1)} %get-tuple-element.53), channel_id=1, source_target_pairs={{0,8},{4,12},{8,0},{12,4},{16,24},{20,28},{24,16},{28,20},{1,9},{5... | collective-permute-start | bytes 663560 | tf_op jit(solution)/shard_map/ppermute | solution.py:584
  40.9 0.5 collective-permute-start.4
  41.4 1.0 %collective-permute-start.5 = (bf16[4,8,3456]{2,1,0:T(8,128)(2,1)S(1)}, bf16[4,8,3456]{2,1,0:T(8,128)(2,1)S(1)}, u32[]{:S(2)}, u32[]{:S(2)}) collective-permute-start(bf16[4,8,3456]{2,1,0:T(8,128)(2,1)S(1)} %get-tuple-element.55), channel_id=1, source_target_pairs={{0,24},{4,28},{8,16},{12,20},{16,8},{20,12},{24,0},{28,4},{1,25},{... | collective-permute-start | bytes 663560 | tf_op jit(solution)/shard_map/ppermute | solution.py:584
  42.4 4.7 %collective-permute-done.3.refs_0_ = bf16[4,8,3456]{2,1,0:T(8,128)(2,1)S(1)} collective-permute-done((bf16[4,8,3456]{2,1,0:T(8,128)(2,1)S(1)}, bf16[4,8,3456]{2,1,0:T(8,128)(2,1)S(1)}, u32[]{:S(2)}, u32[]{:S(2)}) %collective-permute-start.3) | collective-permute-done | bytes 221216 | tf_op jit(solution)/shard_map/ppermute | solution.py:584
  47.1 5.9 %collective-permute-done.4.refs_1_ = bf16[4,8,3456]{2,1,0:T(8,128)(2,1)S(1)} collective-permute-done((bf16[4,8,3456]{2,1,0:T(8,128)(2,1)S(1)}, bf16[4,8,3456]{2,1,0:T(8,128)(2,1)S(1)}, u32[]{:S(2)}, u32[]{:S(2)}) %collective-permute-start.4) | collective-permute-done | bytes 221216 | tf_op jit(solution)/shard_map/ppermute | solution.py:584
  53.0 0.0 collective-permute-done.5.refs_2_
  53.0 1.1 %sum_chips.1 = (f32[8,3328]{1,0:T(8,128)S(1)}, bf16[8,3840]{1,0:T(8,128)(2,1)S(1)}, bf16[8,3840]{1,0:T(8,128)(2,1)S(1)}, bf16[8,3840]{1,0:T(8,128)(2,1)S(1)}) custom-call(s32[4]{0:T(128)S(1)} %pad_add_fusion.place_ref, f32[4,8,3328]{2,1,0:T(8,128)S(1)} %get-tuple-element.52.own_ref, bf16[4,8,3456]{2,1,0:T(8,128)(2,1)S(1)} %collective-permute-done.3.refs_0_, ...), custom_call_target="tpu_custom_call" | custom-call | tf_op jit(solution)/shard_map/sum_chips/pallas_call | solution.py:537
  54.1 1.6 %collective-permute-start.6 = (bf16[8,3840]{1,0:T(8,128)(2,1)S(1)}, bf16[8,3840]{1,0:T(8,128)(2,1)S(1)}, u32[]{:S(2)}, u32[]{:S(2)}) collective-permute-start(bf16[8,3840]{1,0:T(8,128)(2,1)S(1)} %get-tuple-element.57), channel_id=1, source_target_pairs={{0,1},{1,0},{2,3},{3,2},{4,5},{5,4},{6,7},{7,6},{8,9},{9,8},{10,11... | collective-permute-start | bytes 184328 | tf_op jit(solution)/shard_map/ppermute | solution.py:586
  55.8 2.6 %collective-permute-start.7 = (bf16[8,3840]{1,0:T(8,128)(2,1)S(1)}, bf16[8,3840]{1,0:T(8,128)(2,1)S(1)}, u32[]{:S(2)}, u32[]{:S(2)}) collective-permute-start(bf16[8,3840]{1,0:T(8,128)(2,1)S(1)} %get-tuple-element.58), channel_id=1, source_target_pairs={{0,2},{1,3},{2,0},{3,1},{4,6},{5,7},{6,4},{7,5},{8,10},{9,11},{10,... | collective-permute-start | bytes 184328 | tf_op jit(solution)/shard_map/ppermute | solution.py:586
  58.4 0.2 collective-permute-start.8
  58.6 0.4 collective-permute-done.6.refs_0_
  59.0 3.2 %collective-permute-done.7.refs_1_ = bf16[8,3840]{1,0:T(8,128)(2,1)S(1)} collective-permute-done((bf16[8,3840]{1,0:T(8,128)(2,1)S(1)}, bf16[8,3840]{1,0:T(8,128)(2,1)S(1)}, u32[]{:S(2)}, u32[]{:S(2)}) %collective-permute-start.7) | collective-permute-done | bytes 61472 | tf_op jit(solution)/shard_map/ppermute | solution.py:586
  62.2 2.2 %collective-permute-done.8.refs_2_ = bf16[8,3840]{1,0:T(8,128)(2,1)S(1)} collective-permute-done((bf16[8,3840]{1,0:T(8,128)(2,1)S(1)}, bf16[8,3840]{1,0:T(8,128)(2,1)S(1)}, u32[]{:S(2)}, u32[]{:S(2)}) %collective-permute-start.8) | collective-permute-done | bytes 61472 | tf_op jit(solution)/shard_map/ppermute | solution.py:586
  64.4 0.2 sum_streams.1.refs_0_
  64.6 1.5 %collective-permute-start.11 = (bf16[8,3840]{1,0:T(8,128)(2,1)S(1)}, bf16[8,3840]{1,0:T(8,128)(2,1)S(1)}, u32[]{:S(2)}, u32[]{:S(2)}) collective-permute-start(bf16[8,3840]{1,0:T(8,128)(2,1)S(1)} %sum_streams.1.refs_0_), channel_id=1, source_target_pairs={{0,24},{4,28},{8,16},{12,20},{16,8},{20,12},{24,0},{28,4},{1,25},{... | collective-permute-start | bytes 184328 | tf_op jit(solution)/shard_map/ppermute | solution.py:588
  66.1 0.4 collective-permute-start.10
  66.5 1.7 %collective-permute-start.9 = (bf16[8,3840]{1,0:T(8,128)(2,1)S(1)}, bf16[8,3840]{1,0:T(8,128)(2,1)S(1)}, u32[]{:S(2)}, u32[]{:S(2)}) collective-permute-start(bf16[8,3840]{1,0:T(8,128)(2,1)S(1)} %sum_streams.1.refs_0_), channel_id=1, source_target_pairs={{0,8},{4,12},{8,0},{12,4},{16,24},{20,28},{24,16},{28,20},{1,9},{5... | collective-permute-start | bytes 184328 | tf_op jit(solution)/shard_map/ppermute | solution.py:588
  68.1 0.0 collective-permute-start.12
  68.1 1.6 %collective-permute-done.11.refs_3_ = bf16[8,3840]{1,0:T(8,128)(2,1)S(1)} collective-permute-done((bf16[8,3840]{1,0:T(8,128)(2,1)S(1)}, bf16[8,3840]{1,0:T(8,128)(2,1)S(1)}, u32[]{:S(2)}, u32[]{:S(2)}) %collective-permute-start.11) | collective-permute-done | bytes 61472 | tf_op jit(solution)/shard_map/ppermute | solution.py:588
  69.8 0.0 collective-permute-start.15
  69.8 0.6 collective-permute-done.10.refs_2_
  70.4 0.0 collective-permute-start.14
  70.4 0.3 collective-permute-done.9.refs_1_
  70.7 0.2 collective-permute-start.13
  70.9 0.0 collective-permute-done.12.refs_4_
  70.9 0.1 collective-permute-done.15.refs_7_
  71.0 0.7 collective-permute-done.14.refs_6_
  71.7 0.3 collective-permute-done.13.refs_5_
  71.9 1.7 %unpack.1 = (f32[3,3,64,256]{3,2,1,0:T(8,128)}, f32[64,1024]{1,0:T(8,128)}) custom-call(s32[4]{0:T(128)S(1)} %pad_add_fusion.place_ref, bf16[8,3840]{1,0:T(8,128)(2,1)S(1)} %sum_streams.1.refs_0_, bf16[8,3840]{1,0:T(8,128)(2,1)S(1)} %collective-permute-done.9.refs_1_, bf16[8,3840]{1,0:T(8,128)(2,1)S(1)} %collective-permute-done.10.refs_2_, ...), custom_call_target="tpu_custom_call" | custom-call | tf_op jit(solution)/shard_map/unpack/pallas_call | solution.py:563
Async XLA Ops:
  3.8 13.5 %collective-permute-start = (bf16[992,256]{1,0:T(8,128)(2,1)S(1)}, bf16[992,256]{1,0:T(8,128)(2,1)S(1)}, u32[]{:S(2)}, u32[]{:S(2)}) collective-permute-start(bf16[992,256]{1,0:T(8,128)(2,1)S(1)} %get-tuple-element.31), channel_id=1, source_target_pairs={{0,4},{4,0},{8,12},{12,8},{16,20},{20,16},{24,28},{28,24},{1,5},{5... | collective-permute-start | bytes 1523720 | tf_op jit(solution)/shard_map/ppermute | solution.py:383
  4.3 13.0 %collective-permute-start.1 = (bf16[992,256]{1,0:T(8,128)(2,1)S(1)}, bf16[992,256]{1,0:T(8,128)(2,1)S(1)}, u32[]{:S(2)}, u32[]{:S(2)}) collective-permute-start(bf16[992,256]{1,0:T(8,128)(2,1)S(1)} %get-tuple-element.32), channel_id=1, source_target_pairs={{4,8},{12,16},{20,24},{8,4},{16,12},{24,20},{5,9},{13,17},{21,25},... | collective-permute-start | bytes 1523720 | tf_op jit(solution)/shard_map/ppermute | solution.py:382
  30.4 7.1 %collective-permute-start.2 = (f32[4,32,3328]{2,1,0:T(8,128)S(1)}, f32[4,32,3328]{2,1,0:T(8,128)S(1)}, u32[]{:S(2)}, u32[]{:S(2)}) collective-permute-start(f32[4,32,3328]{2,1,0:T(8,128)S(1)} %get-tuple-element.51), channel_id=1, source_target_pairs={{0,4},{4,0},{8,12},{12,8},{16,20},{20,16},{24,28},{28,24},{1,5},{5... | collective-permute-start | bytes 5111816 | tf_op jit(solution)/shard_map/ppermute | solution.py:582
  38.6 8.5 %collective-permute-start.3 = (bf16[4,8,3456]{2,1,0:T(8,128)(2,1)S(1)}, bf16[4,8,3456]{2,1,0:T(8,128)(2,1)S(1)}, u32[]{:S(2)}, u32[]{:S(2)}) collective-permute-start(bf16[4,8,3456]{2,1,0:T(8,128)(2,1)S(1)} %get-tuple-element.53), channel_id=1, source_target_pairs={{0,8},{4,12},{8,0},{12,4},{16,24},{20,28},{24,16},{28,20},{1,9},{5... | collective-permute-start | bytes 663560 | tf_op jit(solution)/shard_map/ppermute | solution.py:584
  40.9 12.2 %collective-permute-start.4 = (bf16[4,8,3456]{2,1,0:T(8,128)(2,1)S(1)}, bf16[4,8,3456]{2,1,0:T(8,128)(2,1)S(1)}, u32[]{:S(2)}, u32[]{:S(2)}) collective-permute-start(bf16[4,8,3456]{2,1,0:T(8,128)(2,1)S(1)} %get-tuple-element.54), channel_id=1, source_target_pairs={{0,16},{4,20},{8,24},{12,28},{16,0},{20,4},{24,8},{28,12},{1,17},{... | collective-permute-start | bytes 663560 | tf_op jit(solution)/shard_map/ppermute | solution.py:584
  41.4 11.6 %collective-permute-start.5 = (bf16[4,8,3456]{2,1,0:T(8,128)(2,1)S(1)}, bf16[4,8,3456]{2,1,0:T(8,128)(2,1)S(1)}, u32[]{:S(2)}, u32[]{:S(2)}) collective-permute-start(bf16[4,8,3456]{2,1,0:T(8,128)(2,1)S(1)} %get-tuple-element.55), channel_id=1, source_target_pairs={{0,24},{4,28},{8,16},{12,20},{16,8},{20,12},{24,0},{28,4},{1,25},{... | collective-permute-start | bytes 663560 | tf_op jit(solution)/shard_map/ppermute | solution.py:584
  54.1 4.9 %collective-permute-start.6 = (bf16[8,3840]{1,0:T(8,128)(2,1)S(1)}, bf16[8,3840]{1,0:T(8,128)(2,1)S(1)}, u32[]{:S(2)}, u32[]{:S(2)}) collective-permute-start(bf16[8,3840]{1,0:T(8,128)(2,1)S(1)} %get-tuple-element.57), channel_id=1, source_target_pairs={{0,1},{1,0},{2,3},{3,2},{4,5},{5,4},{6,7},{7,6},{8,9},{9,8},{10,11... | collective-permute-start | bytes 184328 | tf_op jit(solution)/shard_map/ppermute | solution.py:586
  55.8 6.4 %collective-permute-start.7 = (bf16[8,3840]{1,0:T(8,128)(2,1)S(1)}, bf16[8,3840]{1,0:T(8,128)(2,1)S(1)}, u32[]{:S(2)}, u32[]{:S(2)}) collective-permute-start(bf16[8,3840]{1,0:T(8,128)(2,1)S(1)} %get-tuple-element.58), channel_id=1, source_target_pairs={{0,2},{1,3},{2,0},{3,1},{4,6},{5,7},{6,4},{7,5},{8,10},{9,11},{10,... | collective-permute-start | bytes 184328 | tf_op jit(solution)/shard_map/ppermute | solution.py:586
  58.4 6.0 %collective-permute-start.8 = (bf16[8,3840]{1,0:T(8,128)(2,1)S(1)}, bf16[8,3840]{1,0:T(8,128)(2,1)S(1)}, u32[]{:S(2)}, u32[]{:S(2)}) collective-permute-start(bf16[8,3840]{1,0:T(8,128)(2,1)S(1)} %get-tuple-element.59), channel_id=1, source_target_pairs={{0,3},{1,2},{2,1},{3,0},{4,7},{5,6},{6,5},{7,4},{8,11},{9,10},{10,... | collective-permute-start | bytes 184328 | tf_op jit(solution)/shard_map/ppermute | solution.py:586
  64.6 5.2 %collective-permute-start.11 = (bf16[8,3840]{1,0:T(8,128)(2,1)S(1)}, bf16[8,3840]{1,0:T(8,128)(2,1)S(1)}, u32[]{:S(2)}, u32[]{:S(2)}) collective-permute-start(bf16[8,3840]{1,0:T(8,128)(2,1)S(1)} %sum_streams.1.refs_0_), channel_id=1, source_target_pairs={{0,24},{4,28},{8,16},{12,20},{16,8},{20,12},{24,0},{28,4},{1,25},{... | collective-permute-start | bytes 184328 | tf_op jit(solution)/shard_map/ppermute | solution.py:588
  66.1 4.3 %collective-permute-start.10 = (bf16[8,3840]{1,0:T(8,128)(2,1)S(1)}, bf16[8,3840]{1,0:T(8,128)(2,1)S(1)}, u32[]{:S(2)}, u32[]{:S(2)}) collective-permute-start(bf16[8,3840]{1,0:T(8,128)(2,1)S(1)} %sum_streams.1.refs_0_), channel_id=1, source_target_pairs={{0,16},{4,20},{8,24},{12,28},{16,0},{20,4},{24,8},{28,12},{1,17},{... | collective-permute-start | bytes 184328 | tf_op jit(solution)/shard_map/ppermute | solution.py:588
  66.5 4.2 %collective-permute-start.9 = (bf16[8,3840]{1,0:T(8,128)(2,1)S(1)}, bf16[8,3840]{1,0:T(8,128)(2,1)S(1)}, u32[]{:S(2)}, u32[]{:S(2)}) collective-permute-start(bf16[8,3840]{1,0:T(8,128)(2,1)S(1)} %sum_streams.1.refs_0_), channel_id=1, source_target_pairs={{0,8},{4,12},{8,0},{12,4},{16,24},{20,28},{24,16},{28,20},{1,9},{5... | collective-permute-start | bytes 184328 | tf_op jit(solution)/shard_map/ppermute | solution.py:588
  68.1 2.8 %collective-permute-start.12 = (bf16[8,3840]{1,0:T(8,128)(2,1)S(1)}, bf16[8,3840]{1,0:T(8,128)(2,1)S(1)}, u32[]{:S(2)}, u32[]{:S(2)}) collective-permute-start(bf16[8,3840]{1,0:T(8,128)(2,1)S(1)} %sum_streams.1.refs_0_), channel_id=1, source_target_pairs={{0,4},{4,0},{8,12},{12,8},{16,20},{20,16},{24,28},{28,24},{1,5},{5... | collective-permute-start | bytes 184328 | tf_op jit(solution)/shard_map/ppermute | solution.py:589
  69.8 1.2 %collective-permute-start.15 = (bf16[8,3840]{1,0:T(8,128)(2,1)S(1)}, bf16[8,3840]{1,0:T(8,128)(2,1)S(1)}, u32[]{:S(2)}, u32[]{:S(2)}) collective-permute-start(bf16[8,3840]{1,0:T(8,128)(2,1)S(1)} %collective-permute-done.11.refs_3_), channel_id=1, source_target_pairs={{0,4},{4,0},{8,12},{12,8},{16,20},{20,16},{24,28},{28,24},{1,5},{5... | collective-permute-start | bytes 184328 | tf_op jit(solution)/shard_map/ppermute | solution.py:589
  70.4 1.2 %collective-permute-start.14 = (bf16[8,3840]{1,0:T(8,128)(2,1)S(1)}, bf16[8,3840]{1,0:T(8,128)(2,1)S(1)}, u32[]{:S(2)}, u32[]{:S(2)}) collective-permute-start(bf16[8,3840]{1,0:T(8,128)(2,1)S(1)} %collective-permute-done.10.refs_2_), channel_id=1, source_target_pairs={{0,4},{4,0},{8,12},{12,8},{16,20},{20,16},{24,28},{28,24},{1,5},{5... | collective-permute-start | bytes 184328 | tf_op jit(solution)/shard_map/ppermute | solution.py:589
  70.7 1.2 %collective-permute-start.13 = (bf16[8,3840]{1,0:T(8,128)(2,1)S(1)}, bf16[8,3840]{1,0:T(8,128)(2,1)S(1)}, u32[]{:S(2)}, u32[]{:S(2)}) collective-permute-start(bf16[8,3840]{1,0:T(8,128)(2,1)S(1)} %collective-permute-done.9.refs_1_), channel_id=1, source_target_pairs={{0,4},{4,0},{8,12},{12,8},{16,20},{20,16},{24,28},{28,24},{1,5},{5... | collective-permute-start | bytes 184328 | tf_op jit(solution)/shard_map/ppermute | solution.py:589
